TPU v7x, 256 devices: a whole 4x4x8 slice. The times are simulated.
256 devices in a mesh: grp: 8 (over z), seq: 32 (over y, x, core).
Axes of the slice: x: 4, y: 4, z: 8, core: 2. Of those that a mesh axis runs over, the one named last changes fastest.
Arguments:
- queries: bfloat16 [32768, 1024], P(('grp', 'seq')), may hold values from -6 to 6
- key_rows: bfloat16 [32768, 1024], P(('grp', 'seq')), may hold values from -6 to 6
- value_rows: bfloat16 [32768, 1024], P(('grp', 'seq')), may hold values from -6 to 6
- channel_gain: float32 [1024], replicated, may hold values from 0.5 to 1.5
- out_cotangent: bfloat16 [32768, 1024], P(('grp', 'seq')), may hold values from -6 to 6
Outputs:
- attended: bfloat16 [32768, 1024], P(('grp', 'seq'))
- grad_queries: bfloat16 [32768, 1024], P(('grp', 'seq'))
- grad_keys: bfloat16 [32768, 1024], P(('grp', 'seq'))
- grad_values: bfloat16 [32768, 1024], P(('grp', 'seq'))
All inputs are finite; a program needn't handle non-finite values.
Results may differ from a plain program's by a relative error of at most 0.0075.
Values sent between devices are 32-bit elements; how exact they have to be, the bound alone decides.
No kernel may reach another device: no remote copies, remote signals or barrier semaphores. Data moves between devices by JAX's collectives and lax.ppermute only.
A program may use at most 256 MiB of HBM per device.

v0:
```python
import jax
import jax.numpy as jnp
from jax import lax
from jax.sharding import PartitionSpec as P

HEADS = 8
HEAD_DIM = 128


epsilon = 1e-06


def entering(x, axis, combine, identity, reverse):
    length, place = (lax.axis_size(axis), lax.axis_index(axis))
    everything = lax.all_gather(x, axis)
    start = jnp.broadcast_to(jnp.asarray(identity, x.dtype), x.shape)

    def step(k, before):
        at = length - 1 - k if reverse else k
        reached = at > place if reverse else at < place
        new = combine(before, everything[at])
        return jnp.where(reached, new, before)

    return lax.fori_loop(0, length, step, start)


def add_states(first_part, second_part):
    return first_part + second_part


def state_before(local_state):
    zero_state = jnp.zeros_like(local_state)
    within = entering(local_state, "seq", add_states, zero_state, False)
    total = lax.psum(local_state, "seq")
    groups = entering(total, "grp", add_states, zero_state, False)
    return within + groups


def state_after(local_state):
    zero_state = jnp.zeros_like(local_state)
    within = entering(local_state, "seq", add_states, zero_state, True)
    total = lax.psum(local_state, "seq")
    groups = entering(total, "grp", add_states, zero_state, True)
    return within + groups


def per_device(queries, key_rows, value_rows, channel_gain, out_cotangent):
    length = queries.shape[0]
    head_shape = (length, HEADS, HEAD_DIM)
    query_heads = queries.reshape(head_shape)
    key_heads = key_rows.reshape(head_shape)
    value_heads = value_rows.reshape(head_shape)
    gain_heads = channel_gain.reshape(HEADS, HEAD_DIM)
    local_state = jnp.einsum(
        "she,shf->hef", key_heads, value_heads, preferred_element_type=jnp.float32
    )
    earlier = state_before(local_state)
    earlier_b = earlier.astype(jnp.bfloat16)
    causal = lax.broadcasted_iota(jnp.int32, (length, length), 0) >= lax.broadcasted_iota(
        jnp.int32, (length, length), 1
    )
    scores = jnp.einsum("the,she->hts", query_heads, key_heads, preferred_element_type=jnp.float32)
    weights = jnp.where(causal[None], scores, 0.0).astype(jnp.bfloat16)
    output = jnp.einsum("hts,shf->thf", weights, value_heads, preferred_element_type=jnp.float32)
    output = output + jnp.einsum(
        "the,hef->thf", query_heads, earlier_b, preferred_element_type=jnp.float32
    )
    inverse = lax.rsqrt(jnp.mean(output * output, axis=-1, keepdims=True) + epsilon)
    normed = output * inverse
    attended = (normed * gain_heads).astype(jnp.bfloat16).reshape(length, -1)
    scaled = out_cotangent.reshape(head_shape).astype(jnp.float32) * gain_heads
    out_delta = (
        inverse * (scaled - normed * jnp.mean(scaled * normed, axis=-1, keepdims=True))
    ).astype(jnp.bfloat16)
    grad_state = jnp.einsum(
        "the,thf->hef", query_heads, out_delta, preferred_element_type=jnp.float32
    )
    suffix_b = state_after(grad_state).astype(jnp.bfloat16)
    delta_raw = jnp.einsum(
        "thf,shf->hts", out_delta, value_heads, preferred_element_type=jnp.float32
    )
    delta_scores = jnp.where(causal[None], delta_raw, 0.0).astype(jnp.bfloat16)
    grad_query = jnp.einsum(
        "hts,she->the", delta_scores, key_heads, preferred_element_type=jnp.float32
    )
    grad_query = grad_query + jnp.einsum(
        "thf,hef->the", out_delta, earlier_b, preferred_element_type=jnp.float32
    )
    grad_key = jnp.einsum(
        "hts,the->she", delta_scores, query_heads, preferred_element_type=jnp.float32
    )
    grad_key = grad_key + jnp.einsum(
        "shf,hef->she", value_heads, suffix_b, preferred_element_type=jnp.float32
    )
    grad_value = jnp.einsum("hts,thf->shf", weights, out_delta, preferred_element_type=jnp.float32)
    grad_value = grad_value + jnp.einsum(
        "she,hef->shf", key_heads, suffix_b, preferred_element_type=jnp.float32
    )
    flat_shape = (length, -1)
    return (
        attended,
        grad_query.astype(jnp.bfloat16).reshape(flat_shape),
        grad_key.astype(jnp.bfloat16).reshape(flat_shape),
        grad_value.astype(jnp.bfloat16).reshape(flat_shape),
    )


def solution(mesh):
    placed = (
        P(("grp", "seq"), None),
        P(("grp", "seq"), None),
        P(("grp", "seq"), None),
        P(),
        P(("grp", "seq"), None),
    )
    return jax.shard_map(
        per_device,
        mesh=mesh,
        in_specs=placed,
        out_specs=(
            P(("grp", "seq"), None),
            P(("grp", "seq"), None),
            P(("grp", "seq"), None),
            P(("grp", "seq"), None),
        ),
        check_vma=False,
    )
```

profile of v0, /device:TPU:1, one launch (start us, length us, event | category | flops | bytes accessed | tf_op | source)
XLA Modules:
  0.0 579.1 jit_solution(2293627145458937658)
XLA Ops:
  9.6 82.8 %all-gather.11.cloned.1.call-done = f32[256,128,128]{2,1,0:T(8,128)} async-done(((f32[8,128,128]{2,1,0:T(8,128)}), f32[256,128,128]{2,1,0:T(8,128)}) %all-gather.11.cloned.1.call-update) | async-done | bytes 16777232 | tf_op jit(solution)/shard_map/all_gather | solution.py:15
  94.3 1.3 fusion.3
  95.6 113.5 %all-reduce.3.cloned.1.call-done = f32[1,8,128,128]{3,2,1,0:T(8,128)} async-done(((f32[1,8,128,128]{3,2,1,0:T(8,128)}), f32[1,8,128,128]{3,2,1,0:T(8,128)}) %all-reduce.3.cloned.1.call-update) | async-done | bytes 524304 | tf_op jit(solution)/shard_map/psum | solution.py:34
  209.1 40.2 %while.60 = (s32[]{:T(128)}, f32[8,128,128]{2,1,0:T(8,128)S(1)}, s32[]{:T(128)}, f32[32,8,128,128]{3,2,1,0:T(8,128)}, s32[]{:T(128)}, /*index=5*/s32[]{:T(128)}) while((s32[]{:T(128)}, f32[8,128,128]{2,1,0:T(8,128)S(1)}, s32[]{:T(128)}, f32[32,8,128,128]{3,2,1,0:T(8,128)}, s32[]{:T(128)}, /*index=5*/s32[]{:T(128)}) %tuple.164), condition=%wide.region_1.2_spmd.clone, body=%wide.region_0.1_spmd.clone.sunk | while | flops 393220 | bytes 1572965 | solution.py:24
  209.1 1.2 add_select_fusion.8
  210.4 1.2 add_select_fusion.8
  211.6 1.2 add_select_fusion.8
  212.9 1.2 add_select_fusion.8
  214.1 1.2 add_select_fusion.8
  215.4 1.2 add_select_fusion.8
  216.6 1.2 add_select_fusion.8
  217.9 1.2 add_select_fusion.8
  219.1 1.2 add_select_fusion.8
  220.4 1.2 add_select_fusion.8
  221.6 1.3 add_select_fusion.8
  222.9 1.2 add_select_fusion.8
  224.2 1.2 add_select_fusion.8
  225.4 1.2 add_select_fusion.8
  226.7 1.2 add_select_fusion.8
  227.9 1.2 add_select_fusion.8
  229.2 1.2 add_select_fusion.8
  230.5 1.2 add_select_fusion.8
  231.7 1.2 add_select_fusion.8
  233.0 1.2 add_select_fusion.8
  234.2 1.2 add_select_fusion.8
  235.5 1.2 add_select_fusion.8
  236.8 1.2 add_select_fusion.8
  238.0 1.2 add_select_fusion.8
  239.3 1.2 add_select_fusion.8
  240.5 1.2 add_select_fusion.8
  241.8 1.2 add_select_fusion.8
  243.0 1.2 add_select_fusion.8
  244.3 1.2 add_select_fusion.8
  245.6 1.2 add_select_fusion.8
  246.8 1.2 add_select_fusion.8
  248.1 1.2 add_select_fusion.8
  249.3 16.2 %all-gather.7.cloned.1.call-done = f32[8,8,128,128]{3,2,1,0:T(8,128)} async-done(((f32[1,8,128,128]{3,2,1,0:T(8,128)}), f32[8,8,128,128]{3,2,1,0:T(8,128)}) %all-gather.7.cloned.1.call-update) | async-done | bytes 4194320 | tf_op jit(solution)/shard_map/all_gather | solution.py:15
  265.5 10.0 %while.61 = (s32[]{:T(128)}, f32[8,128,128]{2,1,0:T(8,128)S(1)}, s32[]{:T(128)}, f32[8,8,128,128]{3,2,1,0:T(8,128)}, s32[]{:T(128)}, /*index=5*/s32[]{:T(128)}) while((s32[]{:T(128)}, f32[8,128,128]{2,1,0:T(8,128)S(1)}, s32[]{:T(128)}, f32[8,8,128,128]{3,2,1,0:T(8,128)}, s32[]{:T(128)}, /*index=5*/s32[]{:T(128)}) %tuple.142), condition=%wide.region_4.5_spmd.clone, body=%wide.region_3.4_spmd.clone.sunk | while | flops 393220 | bytes 1572965 | solution.py:24
  266.7 1.2 add_select_fusion.9
  268.0 1.2 add_select_fusion.9
  269.2 1.2 add_select_fusion.9
  270.5 1.2 add_select_fusion.9
  271.7 1.2 add_select_fusion.9
  273.0 1.2 add_select_fusion.9
  274.2 1.2 add_select_fusion.9
  278.5 115.5 %all-reduce.5.cloned.1.call-done = f32[1,8,128,128]{2,3,1,0:T(8,128)} async-done(((f32[1,8,128,128]{2,3,1,0:T(8,128)}), f32[1,8,128,128]{2,3,1,0:T(8,128)}) %all-reduce.5.cloned.1.call-update) | async-done | bytes 524304 | tf_op jit(solution)/shard_map/psum | solution.py:42
  394.1 2.0 copy.47
  400.8 50.0 %all-gather.9.cloned.1.call-done = f32[8,8,128,128]{3,2,1,0:T(8,128)} async-done(((f32[1,8,128,128]{3,2,1,0:T(8,128)}), f32[8,8,128,128]{3,2,1,0:T(8,128)}) %all-gather.9.cloned.1.call-update) | async-done | bytes 4194320 | tf_op jit(solution)/shard_map/all_gather | solution.py:15
  450.7 10.0 %while.63 = (s32[]{:T(128)}, f32[8,128,128]{2,1,0:T(8,128)S(1)}, s32[]{:T(128)}, f32[8,8,128,128]{3,2,1,0:T(8,128)}, s32[]{:T(128)}, /*index=5*/s32[]{:T(128)}, s32[]{:T(128)}, s32[]{:T(128)}) while((s32[]{:T(128)}, f32[8,128,128]{2,1,0:T(8,128)S(1)}, s32[]{:T(128)}, f32[8,8,128,128]{3,2,1,0:T(8,128)}, s32[]{:T(128)}, ...), condition=%wide.region_11.12_spmd.clone, body=%wide.region_10.11_spmd.clone.sunk | while | flops 393224 | bytes 1573027 | solution.py:24
  452.0 1.2 add_select_fusion.11
  453.2 1.2 add_select_fusion.11
  454.5 1.2 add_select_fusion.11
  455.7 1.2 add_select_fusion.11
  457.0 1.2 add_select_fusion.11
  458.3 1.2 add_select_fusion.11
  459.5 1.2 add_select_fusion.11
  460.8 68.9 %all-gather.13.cloned.1.call-done = f32[256,128,128]{2,1,0:T(8,128)} async-done(((f32[8,128,128]{2,1,0:T(8,128)}), f32[256,128,128]{2,1,0:T(8,128)}) %all-gather.13.cloned.1.call-update) | async-done | bytes 16777232 | tf_op jit(solution)/shard_map/all_gather | solution.py:15
  529.7 40.2 %while.62 = (s32[]{:T(128)}, f32[8,128,128]{2,1,0:T(8,128)S(1)}, s32[]{:T(128)}, f32[32,8,128,128]{3,2,1,0:T(8,128)}, s32[]{:T(128)}, /*index=5*/s32[]{:T(128)}, s32[]{:T(128)}, s32[]{:T(128)}) while((s32[]{:T(128)}, f32[8,128,128]{2,1,0:T(8,128)S(1)}, s32[]{:T(128)}, f32[32,8,128,128]{3,2,1,0:T(8,128)}, s32[]{:T(128)}, ...), condition=%wide.region_8.9_spmd.clone, body=%wide.region_7.8_spmd.clone.sunk | while | flops 393224 | bytes 1573027 | solution.py:24
  530.9 1.2 add_select_fusion.10
  532.2 1.2 add_select_fusion.10
  533.5 1.2 add_select_fusion.10
  542.3 1.2 add_select_fusion.10
  553.6 1.2 add_select_fusion.10
  566.1 1.2 add_select_fusion.10
  (82 shorter events, 48.6 us)
Async XLA Ops:
  7.2 1.4 copy-start
  7.2 268.3 %copy-start.2 = (bf16[128,1024]{1,0:T(8,128)(2,1)S(1)}, bf16[128,1024]{1,0:T(8,128)(2,1)}, u32[]{:S(2)}) copy-start(bf16[128,1024]{1,0:T(8,128)(2,1)} %param.13) | copy-start | bytes 786436
  7.2 269.0 %copy-start.5 = (f32[1024]{0:T(1024)S(1)}, f32[1024]{0:T(1024)}, u32[]{:S(2)}) copy-start(f32[1024]{0:T(1024)} %param.16) | copy-start | bytes 12292
  7.2 85.1 %all-gather.11.cloned.1.call-start = ((), (), s32[]{:S(2)}) async-start(), calls=%async_computation.4 | async-start | bytes 17301504 | tf_op jit(solution)/shard_map/all_gather | solution.py:15
  92.3 116.7 %all-reduce.3.cloned.1.call-start = ((), (), s32[]{:S(2)}) async-start(), calls=%async_computation | async-start | bytes 1048576 | tf_op jit(solution)/shard_map/psum | solution.py:34
  93.1 172.4 %all-gather.7.cloned.1.call-start = ((), (), s32[]{:S(2)}) async-start(), calls=%async_computation.1 | async-start | bytes 4718592 | tf_op jit(solution)/shard_map/all_gather | solution.py:15
  95.6 180.3 %copy-start.4 = (bf16[8,128,128]{2,1,0:T(8,128)(2,1)}, bf16[8,128,128]{2,1,0:T(8,128)(2,1)S(1)}, u32[]{:S(2)}) copy-start(bf16[8,128,128]{2,1,0:T(8,128)(2,1)S(1)} %fusion.3) | copy-start | bytes 786436
  276.2 294.9 %copy-start.3 = (bf16[128,1024]{1,0:T(8,128)(2,1)S(1)}, bf16[128,1024]{1,0:T(8,128)(2,1)}, u32[]{:S(2)}) copy-start(bf16[128,1024]{1,0:T(8,128)(2,1)} %param.14) | copy-start | bytes 786436
  276.9 1.0 copy-start.1
  277.9 116.1 %all-reduce.5.cloned.1.call-start = ((), (), s32[]{:S(2)}) async-start(), calls=%async_computation.2 | async-start | bytes 1048576 | tf_op jit(solution)/shard_map/psum | solution.py:42
  278.5 172.2 %all-gather.9.cloned.1.call-start = ((), (), s32[]{:S(2)}) async-start(), calls=%async_computation.3 | async-start | bytes 4718592 | tf_op jit(solution)/shard_map/all_gather | solution.py:15
  396.1 133.5 %all-gather.13.cloned.1.call-start = ((), (), s32[]{:S(2)}) async-start(), calls=%async_computation.5 | async-start | bytes 17301504 | tf_op jit(solution)/shard_map/all_gather | solution.py:15
Sparse Core Ops, SparseCore 0:
  10.6 81.7 all-gather.10
  96.4 112.6 all-reduce.2
  211.0 54.4 all-gather.6
  282.0 112.0 all-reduce.4
  396.3 54.4 all-gather.8
  453.1 76.5 all-gather.12
where the time goes:
time: 583 us; the launch traced here: 579 us
  waiting for transfers between devices  449 us (77%)
  other arithmetic  98.9 us (17%)
  between operations  14.3 us (2%)
  local copies, waits for them, and re-layouts  8.84 us (2%)
  matrix products  6.16 us (1%)
    all_gather x4, waiting for transfers between devices, entering(): everything = lax.all_gather(x, axis)  218 us
    psum x1, waiting for transfers between devices, state_after(): total = lax.psum(local_state, 'seq')  116 us
    psum x1, waiting for transfers between devices, state_before(): total = lax.psum(local_state, 'seq')  113 us
    select_n x80, other arithmetic, step(): return jnp.where(reached, new, before)  98.3 us
  transfers between devices with their start and end apart: 6, of which 6 were waited for; matrix products, arithmetic and copies ran while one was open for 10% of the time, Pallas kernels for 0%

commit v1 on v0

v1 whole, which is shorter than its diff:
```python
import functools

import jax
import jax.numpy as jnp
from jax import lax
from jax.experimental import pallas as pl
from jax.experimental.pallas import tpu as pltpu
from jax.sharding import Mesh, PartitionSpec as P

HEADS = 8
HEAD_DIM = 128
TOK = 128
HALF = HEADS // 2
WIDE = HALF * HEAD_DIM
PAIR = 2 * TOK
ROWS = WIDE
EPSILON = 1e-06
F32, BF16 = jnp.float32, jnp.bfloat16

NT = (((1,), (1,)), ((), ()))
TN = (((0,), (0,)), ((), ()))
NN = (((1,), (0,)), ((), ()))


def dot(a, b, dims):
    return lax.dot_general(a, b, dims, preferred_element_type=F32)


def call(body, outs, cost=None):
    return pl.pallas_call(
        body,
        out_shape=[jax.ShapeDtypeStruct(shape, dtype) for shape, dtype in outs],
        compiler_params=pltpu.CompilerParams(vmem_limit_bytes=32 * 2**20),
    )


def halves():
    core = lax.axis_index("core")
    mine = pl.ds(pl.multiple_of(core * WIDE, WIDE), WIDE)
    other = pl.ds(pl.multiple_of((1 - core) * WIDE, WIDE), WIDE)
    return mine, other


def rows():
    core = lax.axis_index("core")
    mine = pl.ds(pl.multiple_of(core * TOK, TOK), TOK)
    other = pl.ds(pl.multiple_of((1 - core) * TOK, TOK), TOK)
    return mine, other


def head(h):
    return pl.ds(h * HEAD_DIM, HEAD_DIM)


def pack_body(a_ref, b_ref, send_ref):
    _, other = halves()
    send_ref[:, :WIDE] = a_ref[:, other].astype(F32)
    send_ref[:, WIDE:] = b_ref[:, other].astype(F32)


def unpack(a_ref, b_ref, got_ref, a2_ref, b2_ref):
    mine, _ = halves()
    own, far = rows()
    a2_ref[own, :] = a_ref[:, mine]
    b2_ref[own, :] = b_ref[:, mine]
    a2_ref[far, :] = got_ref[:, :WIDE].astype(BF16)
    b2_ref[far, :] = got_ref[:, WIDE:].astype(BF16)


def state_body(k_ref, v_ref, got_ref, k2_ref, v2_ref, state_ref, first_ref):
    unpack(k_ref, v_ref, got_ref, k2_ref, v2_ref)
    for h in range(HALF):
        first = dot(k2_ref[:TOK, head(h)], v2_ref[:TOK, head(h)], TN)
        first_ref[head(h), :] = first
        state_ref[head(h), :] = first + dot(k2_ref[TOK:, head(h)], v2_ref[TOK:, head(h)], TN)


def causal():
    return lax.broadcasted_iota(jnp.int32, (TOK, TOK), 0) >= lax.broadcasted_iota(
        jnp.int32, (TOK, TOK), 1
    )


BLOCKS = [(b, pl.ds(b * TOK, TOK)) for b in range(2)]


def intra_body(q_ref, dy_ref, got_ref, k2_ref, v2_ref, q2_ref, dy2_ref, weights_ref, intra_ref):
    unpack(q_ref, dy_ref, got_ref, q2_ref, dy2_ref)
    mask = causal()
    for h in range(HALF):
        for b, at in BLOCKS:
            scores = dot(q2_ref[at, head(h)], k2_ref[at, head(h)], NT)
            weights = jnp.where(mask, scores, 0.0).astype(BF16)
            weights_ref[h, b] = weights
            intra_ref[at, head(h)] = dot(weights, v2_ref[at, head(h)], NN)


def total_body(parts_ref, out_ref):
    total = jnp.sum(parts_ref[...], axis=0)
    for g in range(out_ref.shape[0]):
        out_ref[g] = total


def scan_body(reverse, parts_ref, totals_ref, out_ref):
    place = lax.axis_index("z")
    groups = totals_ref.shape[0]
    running = jnp.zeros(parts_ref.shape[1:], F32)
    for g in range(groups):
        reached = g > place if reverse else g < place
        running = running + jnp.where(reached, totals_ref[g], 0.0)
    steps = parts_ref.shape[0]
    for i in range(steps):
        at = steps - 1 - i if reverse else i
        out_ref[at] = running
        running = running + parts_ref[at]


def entering(before_ref, first_ref, h, b):
    before = before_ref[head(h), :]
    return (before + first_ref[head(h), :] if b else before).astype(BF16)


def mid_body(
    q2_ref, dy2_ref, intra_ref, before_ref, first_ref, gain_ref,
    attended_ref, delta_ref, state_ref, second_ref,
):
    mine, _ = halves()
    gain = gain_ref[:, mine]
    for h in range(HALF):
        gain_h = gain[:, h * HEAD_DIM : (h + 1) * HEAD_DIM]
        states = []
        for b, at in BLOCKS:
            q = q2_ref[at, head(h)]
            out = intra_ref[at, head(h)] + dot(q, entering(before_ref, first_ref, h, b), NN)
            inverse = lax.rsqrt(jnp.mean(out * out, axis=-1, keepdims=True) + EPSILON)
            normed = out * inverse
            attended_ref[at, head(h)] = (normed * gain_h).astype(BF16)
            scaled = dy2_ref[at, head(h)].astype(F32) * gain_h
            mean = jnp.mean(scaled * normed, axis=-1, keepdims=True)
            delta = (inverse * (scaled - normed * mean)).astype(BF16)
            delta_ref[at, head(h)] = delta
            states.append(dot(q, delta, TN))
        second_ref[head(h), :] = states[1]
        state_ref[head(h), :] = states[0] + states[1]


def back_body(
    q2_ref, k2_ref, v2_ref, weights_ref, delta_ref, before_ref, first_ref, attended_ref,
    send_ref, grad_query_ref, grad_key_ref, grad_value_ref, all_ref,
):
    own, far = rows()
    mask = causal()
    for h in range(HALF):
        for b, at in BLOCKS:
            delta = delta_ref[at, head(h)]
            raw = dot(delta, v2_ref[at, head(h)], NT)
            scores = jnp.where(mask, raw, 0.0).astype(BF16)
            all_ref[at, head(h)] = dot(scores, k2_ref[at, head(h)], NN) + dot(
                delta, entering(before_ref, first_ref, h, b), NT
            )
            grad_key_ref[at, head(h)] = dot(scores, q2_ref[at, head(h)], TN)
            grad_value_ref[at, head(h)] = dot(weights_ref[h, b], delta, TN)
    grad_query_ref[...] = all_ref[own, :].astype(BF16)
    send_ref[:, :WIDE] = attended_ref[far, :].astype(F32)
    send_ref[:, WIDE:] = all_ref[far, :].astype(BF16).astype(F32)


def merge_first_body(attended2_ref, mine_ref, got_ref, attended_ref, grad_query_ref):
    mine, other = halves()
    own, _ = rows()
    attended_ref[:, mine] = attended2_ref[own, :]
    attended_ref[:, other] = got_ref[:, :WIDE].astype(BF16)
    grad_query_ref[:, mine] = mine_ref[...]
    grad_query_ref[:, other] = got_ref[:, WIDE:].astype(BF16)


def final_body(k2_ref, v2_ref, after_ref, second_ref, gk_ref, gv_ref, own_ref, send_ref, all_ref):
    own, far = rows()
    for h in range(HALF):
        value = pl.ds(WIDE + h * HEAD_DIM, HEAD_DIM)
        for b, at in BLOCKS:
            after = after_ref[head(h), :]
            after = (after if b else after + second_ref[head(h), :]).astype(BF16)
            all_ref[at, head(h)] = gk_ref[at, head(h)] + dot(v2_ref[at, head(h)], after, NT)
            all_ref[at, value] = gv_ref[at, head(h)] + dot(k2_ref[at, head(h)], after, NN)
    own_ref[...] = all_ref[own, :].astype(BF16)
    send_ref[...] = all_ref[far, :].astype(BF16).astype(F32)


def merge_last_body(own_ref, got_ref, grad_key_ref, grad_value_ref):
    mine, other = halves()
    grad_key_ref[:, mine] = own_ref[:, :WIDE]
    grad_key_ref[:, other] = got_ref[:, :WIDE].astype(BF16)
    grad_value_ref[:, mine] = own_ref[:, WIDE:]
    grad_value_ref[:, other] = got_ref[:, WIDE:].astype(BF16)


def swap(x):
    return lax.ppermute(x, "core", [(0, 1), (1, 0)])


def scan_states(state, reverse):
    plane = lax.axis_size("y") * lax.axis_size("x")
    piece = ROWS // plane
    groups = lax.axis_size("z")
    parts = lax.all_to_all(state.reshape(plane, piece, HEAD_DIM), ("y", "x"), 0, 0, tiled=True)
    (copies,) = call(total_body, [((groups, piece, HEAD_DIM), F32)])(parts)
    totals = lax.all_to_all(copies, "z", 0, 0, tiled=True)
    (scanned,) = call(
        functools.partial(scan_body, reverse), [((plane, piece, HEAD_DIM), F32)]
    )(parts, totals)
    back = lax.all_to_all(scanned, ("y", "x"), 0, 0, tiled=True)
    return back.reshape(ROWS, HEAD_DIM)


def per_device(queries, key_rows, value_rows, channel_gain, out_cotangent):
    own_shape = (TOK, HEADS * HEAD_DIM)
    pair_shape = (PAIR, WIDE)
    (kv_send,) = call(pack_body, [(own_shape, F32)])(key_rows, value_rows)
    kv_got = swap(kv_send)
    (qd_send,) = call(pack_body, [(own_shape, F32)])(queries, out_cotangent)
    qd_got = swap(qd_send)
    states = ((ROWS, HEAD_DIM), F32)
    k2, v2, state, first = call(
        state_body, [(pair_shape, BF16), (pair_shape, BF16), states, states]
    )(key_rows, value_rows, kv_got)
    q2, dy2, weights, intra = call(
        intra_body,
        [(pair_shape, BF16), (pair_shape, BF16), ((HALF, 2, TOK, TOK), BF16), (pair_shape, F32)],
    )(queries, out_cotangent, qd_got, k2, v2)
    before = scan_states(state, False)
    attended2, delta, grad_state, second = call(
        mid_body, [(pair_shape, BF16), (pair_shape, BF16), states, states]
    )(q2, dy2, intra, before, first, channel_gain.reshape(1, -1))
    send, own_query, gk_part, gv_part, _ = call(
        back_body,
        [(own_shape, F32), ((TOK, WIDE), BF16), (pair_shape, F32), (pair_shape, F32), (pair_shape, F32)],
    )(q2, k2, v2, weights, delta, before, first, attended2)
    got = swap(send)
    attended, grad_query = call(merge_first_body, [(own_shape, BF16), (own_shape, BF16)])(
        attended2, own_query, got
    )
    after = scan_states(grad_state, True)
    own_last, send_last, _ = call(
        final_body, [(own_shape, BF16), (own_shape, F32), ((PAIR, 2 * WIDE), F32)]
    )(k2, v2, after, second, gk_part, gv_part)
    grad_key, grad_value = call(merge_last_body, [(own_shape, BF16), (own_shape, BF16)])(
        own_last, swap(send_last)
    )
    return attended, grad_query, grad_key, grad_value


def solution(mesh):
    fine = Mesh(mesh.devices.reshape(8, 4, 4, 2), ("z", "y", "x", "core"))
    placed = P(("z", "y", "x", "core"), None)
    return jax.shard_map(
        per_device,
        mesh=fine,
        in_specs=(placed, placed, placed, P(), placed),
        out_specs=(placed, placed, placed, placed),
        check_vma=False,
    )
```

time: 583 us -> 97.2 us (0.17)
  waiting for transfers between devices: 449 us -> 15 us
  other arithmetic: 98.9 us -> 0 us
  blocking collectives: 0 us -> 36.4 us
  starting transfers between devices: 0.16 us -> 28.4 us
  between operations: 14.3 us -> 0.76 us
  Pallas kernels: 0 us -> 11.1 us
  matrix products: 6.16 us -> 0 us
    psum x2 -> x0, waiting for transfers between devices: 229 us -> none  [the longest x1 116 us: state_after(): total = lax.psum(local_state, 'seq')]
    all_gather x4 -> x0, waiting for transfers between devices: 218 us -> none  [entering(): everything = lax.all_gather(x, axis)]
    select_n x80 -> x0, other arithmetic: 98.3 us -> none  [step(): return jnp.where(reached, new, before)]
    all_to_all x0 -> x3, blocking collectives: none -> 36.4 us  [the longest x2 26.2 us: scan_states(): totals = lax.all_to_all(copies, 'z', 0, 0, tiled=True)]
    ppermute x0 -> x4, starting transfers between devices: none -> 16 us  [swap(): return lax.ppermute(x, 'core', [(0, 1), (1, 0)])]
    all_to_all x0 -> x3, waiting for transfers between devices: none -> 12.7 us  [the longest x1 7.31 us: scan_states(): lax.all_to_all(state.reshape(plane, piece, HEAD_DIM), ('y', 'x'), 0, 0, t...]
    all_to_all x0 -> x3, starting transfers between devices: none -> 12.3 us  [the longest x2 7.2 us: scan_states(): back = lax.all_to_all(scanned, ('y', 'x'), 0, 0, tiled=True)]
    pallas_call x0 -> x13, Pallas kernels: none -> 11.1 us  [the longest x1 2.39 us: per_device(): call(back_body, [(own_shape, F32), ((TOK, WIDE), BF16), (pair_shape, F32)...]
  transfers between devices with their start and end apart: 6 -> 7, of which waited for: 6 -> 4; matrix products, arithmetic and copies ran while one was open for 10% -> 0% of each run, Pallas kernels for 0% -> 7%
where the time goes in v1:
time: 97.2 us; the launch traced here: 96.5 us
  blocking collectives  36.4 us (37%)
  starting transfers between devices  28.4 us (29%)
  waiting for transfers between devices  15 us (15%)
  Pallas kernels  11.1 us (11%)
  local copies, waits for them, and re-layouts  4.93 us (5%)
    all_to_all x2, blocking collectives, scan_states(): totals = lax.all_to_all(copies, 'z', 0, 0, tiled=True)  26.2 us
    ppermute x4, starting transfers between devices, swap(): return lax.ppermute(x, 'core', [(0, 1), (1, 0)])  16 us
    all_to_all x1, blocking collectives, scan_states(): lax.all_to_all(state.reshape(plane, piece, HEAD_DIM), ('y', 'x'), 0, 0, t...  10.2 us
    all_to_all x1, waiting for transfers between devices, scan_states(): lax.all_to_all(state.reshape(plane, piece, HEAD_DIM), ('y', 'x'), 0, 0, t...  7.31 us
    all_to_all x2, starting transfers between devices, scan_states(): back = lax.all_to_all(scanned, ('y', 'x'), 0, 0, tiled=True)  7.2 us
    all_to_all x2, waiting for transfers between devices, scan_states(): back = lax.all_to_all(scanned, ('y', 'x'), 0, 0, tiled=True)  5.43 us
    all_to_all x1, starting transfers between devices, scan_states(): lax.all_to_all(state.reshape(plane, piece, HEAD_DIM), ('y', 'x'), 0, 0, t...  5.15 us
    unnamed x18, local copies, waits for them, and re-layouts  4.93 us
  transfers between devices with their start and end apart: 7, of which 4 were waited for; matrix products, arithmetic and copies ran while one was open for 0% of the time, Pallas kernels for 7%

profile of v1, /device:TPU:1, one launch (start us, length us, event | category | flops | bytes accessed | tf_op | source)
XLA Modules:
  0.0 96.5 jit_solution(8955200599092375430)
XLA Ops:
  0.6 0.0 copy-start
  0.6 0.9 copy-done
  1.6 0.0 copy-start.1
  1.6 0.9 copy-done.1
  2.6 3.3 %collective-permute-start.1 = (f32[128,1024]{1,0:T(8,128)S(1)}, f32[128,1024]{1,0:T(8,128)S(1)}, u32[]{:S(2)}, u32[]{:S(2)}) collective-permute-start(f32[128,1024]{1,0:T(8,128)S(1)} %shard_map.85), channel_id=1, source_target_pairs={{0,1},{1,0},{2,3},{3,2},{4,5},{5,4},{6,7},{7,6},{8,9},{9,8},{10,11... | collective-permute-start | bytes 1572872 | tf_op jit(solution)/shard_map/ppermute | solution.py:199
  5.9 1.5 %collective-permute-done.1.got_ref = f32[128,1024]{1,0:T(8,128)S(1)} collective-permute-done((f32[128,1024]{1,0:T(8,128)S(1)}, f32[128,1024]{1,0:T(8,128)S(1)}, u32[]{:S(2)}, u32[]{:S(2)}) %collective-permute-start.1) | collective-permute-done | bytes 524320 | tf_op jit(solution)/shard_map/ppermute | solution.py:199
  7.4 1.0 %shard_map.86 = (bf16[256,512]{1,0:T(8,128)(2,1)S(1)}, bf16[256,512]{1,0:T(8,128)(2,1)S(1)}, f32[512,128]{1,0:T(8,128)}, f32[512,128]{1,0:T(8,128)S(1)}) custom-call(bf16[128,1024]{1,0:T(8,128)(2,1)S(1)} %copy-done, bf16[128,1024]{1,0:T(8,128)(2,1)S(1)} %copy-done.1, f32[128,1024]{1,0:T(8,128)S(1)} %collective-permute-done.1.got_ref), custom_call_target="tpu_custom_call" | custom-call | tf_op jit(solution)/shard_map/pallas_call | solution.py:224
  8.5 0.0 copy-start.2
  8.5 0.0 copy-start.3
  8.5 5.2 %all-to-all-start = ((f32[16,32,128]{2,1,0:T(8,128)}), f32[16,32,128]{2,1,0:T(8,128)S(1)}, u32[]{:S(2)}, u32[]{:S(2)}) async-start(f32[16,32,128]{2,1,0:T(8,128)} %bitcast), calls=%async_computation | async-start | bytes 524288 | tf_op jit(solution)/shard_map/all_to_all | solution.py:206
  13.6 0.0 copy-done.2
  13.6 0.0 copy-done.3
  13.7 0.7 collective-permute-start
  14.4 7.3 %all-to-all-done.parts_ref = f32[16,32,128]{2,1,0:T(8,128)S(1)} async-done(((f32[16,32,128]{2,1,0:T(8,128)}), f32[16,32,128]{2,1,0:T(8,128)S(1)}, u32[]{:S(2)}, u32[]{:S(2)}) %all-to-all-start) | async-done | bytes 262176 | tf_op jit(solution)/shard_map/all_to_all | solution.py:206
  21.8 15.9 %all_to_all.30.totals_ref = f32[8,32,128]{2,1,0:T(8,128)S(1)} all-to-all(f32[8,32,128]{2,1,0:T(8,128)S(1)} %shard_map.88), channel_id=1, replica_groups=mesh['z'=8,'y'=4,'x'=4,'core'=2] {'z'}, dimensions={0} | all-to-all | bytes 262144 | tf_op jit(solution)/shard_map/all_to_all | solution.py:208
  37.7 0.7 shard_map.89
  38.4 3.5 %all-to-all-start.2 = ((f32[16,32,128]{2,1,0:T(8,128)}), f32[16,32,128]{2,1,0:T(8,128)S(1)}, u32[]{:S(2)}, u32[]{:S(2)}) async-start(f32[16,32,128]{2,1,0:T(8,128)} %shard_map.89), calls=%async_computation.2 | async-start | bytes 524288 | tf_op jit(solution)/shard_map/all_to_all | solution.py:212
  42.0 0.0 collective-permute-done.got_ref
  42.0 1.4 %shard_map.87 = (bf16[256,512]{1,0:T(8,128)(2,1)S(1)}, bf16[256,512]{1,0:T(8,128)(2,1)S(1)}, bf16[4,2,128,128]{3,2,1,0:T(8,128)(2,1)S(1)}, f32[256,512]{1,0:T(8,128)S(1)}) custom-call(bf16[128,1024]{1,0:T(8,128)(2,1)S(1)} %copy-done.2, bf16[128,1024]{1,0:T(8,128)(2,1)S(1)} %copy-done.3, f32[128,1024]{1,0:T(8,128)S(1)} %collective-permute-done.got_ref, ...), custom_call_target="tpu_custom_call" | custom-call | tf_op jit(solution)/shard_map/pallas_call | solution.py:227
  43.3 0.0 copy-start.4
  43.3 0.7 copy-done.4
  44.0 5.4 %all-to-all-done.2 = f32[16,32,128]{2,1,0:T(8,128)S(1)} async-done(((f32[16,32,128]{2,1,0:T(8,128)}), f32[16,32,128]{2,1,0:T(8,128)S(1)}, u32[]{:S(2)}, u32[]{:S(2)}) %all-to-all-start.2) | async-done | bytes 262176 | tf_op jit(solution)/shard_map/all_to_all | solution.py:212
  49.5 0.0 copy-start.8
  49.5 0.7 copy-done.8
  50.1 1.5 %shard_map.90 = (bf16[256,512]{1,0:T(8,128)(2,1)S(1)}, bf16[256,512]{1,0:T(8,128)(2,1)S(1)}, f32[512,128]{1,0:T(8,128)S(1)}, f32[512,128]{1,0:T(8,128)S(1)}) custom-call(bf16[256,512]{1,0:T(8,128)(2,1)S(1)} %get-tuple-element.28.q2_ref, bf16[256,512]{1,0:T(8,128)(2,1)S(1)} %get-tuple-element.29.dy2_ref, f32[256,512]{1,0:T(8,128)S(1)} %get-tuple-element.30.intra_ref, ...), custom_call_target="tpu_custom_call" | custom-call | tf_op jit(solution)/shard_map/pallas_call | solution.py:232
  51.7 0.0 copy-start.6
  51.7 0.7 copy-done.6
  52.4 10.2 %all_to_all.31.parts_ref = f32[16,32,128]{2,1,0:T(8,128)S(1)} all-to-all(f32[16,32,128]{2,1,0:T(8,128)S(1)} %bitcast.8), channel_id=1, replica_groups=mesh['z'=8,'y'=4,'x'=4,'core'=2] {'y','x'}, dimensions={0} | all-to-all | bytes 524288 | tf_op jit(solution)/shard_map/all_to_all | solution.py:206
  62.6 10.3 %all_to_all.32.totals_ref = f32[8,32,128]{2,1,0:T(8,128)S(1)} all-to-all(f32[8,32,128]{2,1,0:T(8,128)S(1)} %shard_map.93), channel_id=1, replica_groups=mesh['z'=8,'y'=4,'x'=4,'core'=2] {'z'}, dimensions={0} | all-to-all | bytes 262144 | tf_op jit(solution)/shard_map/all_to_all | solution.py:208
  72.9 0.7 shard_map.94
  73.6 0.0 copy-start.5
  73.6 3.7 %all-to-all-start.5 = ((f32[16,32,128]{2,1,0:T(8,128)}), f32[16,32,128]{2,1,0:T(8,128)S(1)}, u32[]{:S(2)}, u32[]{:S(2)}) async-start(f32[16,32,128]{2,1,0:T(8,128)} %shard_map.94), calls=%async_computation.5 | async-start | bytes 524288 | tf_op jit(solution)/shard_map/all_to_all | solution.py:212
  77.3 0.0 copy-done.5
  77.3 0.0 copy-start.7
  77.3 0.9 copy-done.7
  78.2 2.4 %shard_map.91 = (f32[128,1024]{1,0:T(8,128)}, bf16[128,512]{1,0:T(8,128)(2,1)S(1)}, f32[256,512]{1,0:T(8,128)S(1)}, f32[256,512]{1,0:T(8,128)S(1)}, f32[256,512]{1,0:T(8,128)}) custom-call(bf16[256,512]{1,0:T(8,128)(2,1)S(1)} %get-tuple-element.28.q2_ref, bf16[256,512]{1,0:T(8,128)(2,1)S(1)} %get-tuple-element.26.k2_ref, ...), custom_call_target="tpu_custom_call" | custom-call | tf_op jit(solution)/shard_map/pallas_call | solution.py:235
  80.6 6.7 %collective-permute-start.2 = (f32[128,1024]{1,0:T(8,128)}, f32[128,1024]{1,0:T(8,128)S(1)}, u32[]{:S(2)}, u32[]{:S(2)}) collective-permute-start(f32[128,1024]{1,0:T(8,128)} %get-tuple-element.37), channel_id=1, source_target_pairs={{0,1},{1,0},{2,3},{3,2},{4,5},{5,4},{6,7},{7,6},{8,9},{9,8},{10,11... | collective-permute-start | bytes 1572872 | tf_op jit(solution)/shard_map/ppermute | solution.py:199
  87.3 0.0 all-to-all-done.5
  87.3 1.6 %shard_map.95 = (bf16[128,1024]{1,0:T(8,128)(2,1)S(1)}, f32[128,1024]{1,0:T(8,128)S(1)}, f32[256,1024]{1,0:T(8,128)}) custom-call(bf16[256,512]{1,0:T(8,128)(2,1)S(1)} %get-tuple-element.26.k2_ref, bf16[256,512]{1,0:T(8,128)(2,1)S(1)} %get-tuple-element.27.v2_ref, f32[512,128]{1,0:T(8,128)S(1)} %bitcast.7, f32[512,128]{1,0:T(8,128)S(1)} %get-tuple-element.41.second_ref, ...), custom_call_target="tpu_custom_call" | custom-call | tf_op jit(solution)/shard_map/pallas_call | solution.py:244
  88.9 5.3 %collective-permute-start.3 = (f32[128,1024]{1,0:T(8,128)S(1)}, f32[128,1024]{1,0:T(8,128)S(1)}, u32[]{:S(2)}, u32[]{:S(2)}) collective-permute-start(f32[128,1024]{1,0:T(8,128)S(1)} %get-tuple-element.45), channel_id=1, source_target_pairs={{0,1},{1,0},{2,3},{3,2},{4,5},{5,4},{6,7},{7,6},{8,9},{9,8},{10,11... | collective-permute-start | bytes 1572872 | tf_op jit(solution)/shard_map/ppermute | solution.py:199
  94.2 0.0 collective-permute-done.2.got_ref
  94.2 0.8 shard_map.92
  95.0 0.7 collective-permute-done.3.got_ref
  95.7 0.8 shard_map.96
  (4 shorter events, 0.1 us)
Async XLA Ops:
  0.6 1.0 copy-start
  1.6 0.9 copy-start.1
  2.6 4.9 %collective-permute-start.1 = (f32[128,1024]{1,0:T(8,128)S(1)}, f32[128,1024]{1,0:T(8,128)S(1)}, u32[]{:S(2)}, u32[]{:S(2)}) collective-permute-start(f32[128,1024]{1,0:T(8,128)S(1)} %shard_map.85), channel_id=1, source_target_pairs={{0,1},{1,0},{2,3},{3,2},{4,5},{5,4},{6,7},{7,6},{8,9},{9,8},{10,11... | collective-permute-start | bytes 1572872 | tf_op jit(solution)/shard_map/ppermute | solution.py:199
  8.5 5.2 %copy-start.2 = (bf16[128,1024]{1,0:T(8,128)(2,1)S(1)}, bf16[128,1024]{1,0:T(8,128)(2,1)}, u32[]{:S(2)}) copy-start(bf16[128,1024]{1,0:T(8,128)(2,1)} %q_ref.1) | copy-start | bytes 786436
  8.5 5.2 %copy-start.3 = (bf16[128,1024]{1,0:T(8,128)(2,1)S(1)}, bf16[128,1024]{1,0:T(8,128)(2,1)}, u32[]{:S(2)}) copy-start(bf16[128,1024]{1,0:T(8,128)(2,1)} %dy_ref.1) | copy-start | bytes 786436
  8.5 13.3 %all-to-all-start = ((f32[16,32,128]{2,1,0:T(8,128)}), f32[16,32,128]{2,1,0:T(8,128)S(1)}, u32[]{:S(2)}, u32[]{:S(2)}) async-start(f32[16,32,128]{2,1,0:T(8,128)} %bitcast), calls=%async_computation | async-start | bytes 524288 | tf_op jit(solution)/shard_map/all_to_all | solution.py:206
  13.7 28.3 %collective-permute-start = (f32[128,1024]{1,0:T(8,128)S(1)}, f32[128,1024]{1,0:T(8,128)S(1)}, u32[]{:S(2)}, u32[]{:S(2)}) collective-permute-start(f32[128,1024]{1,0:T(8,128)S(1)} %shard_map.84), channel_id=1, source_target_pairs={{0,1},{1,0},{2,3},{3,2},{4,5},{5,4},{6,7},{7,6},{8,9},{9,8},{10,11... | collective-permute-start | bytes 1572872 | tf_op jit(solution)/shard_map/ppermute | solution.py:199
  38.4 11.0 %all-to-all-start.2 = ((f32[16,32,128]{2,1,0:T(8,128)}), f32[16,32,128]{2,1,0:T(8,128)S(1)}, u32[]{:S(2)}, u32[]{:S(2)}) async-start(f32[16,32,128]{2,1,0:T(8,128)} %shard_map.89), calls=%async_computation.2 | async-start | bytes 524288 | tf_op jit(solution)/shard_map/all_to_all | solution.py:212
  43.3 0.7 copy-start.4
  49.5 0.7 copy-start.8
  51.7 0.7 copy-start.6
  73.6 3.7 %copy-start.5 = (bf16[4,2,128,128]{3,2,1,0:T(8,128)(2,1)S(1)}, bf16[4,2,128,128]{3,2,1,0:T(8,128)(2,1)}, u32[]{:S(2)}) copy-start(bf16[4,2,128,128]{3,2,1,0:T(8,128)(2,1)} %copy-done.4) | copy-start | bytes 786436
  73.6 13.7 %all-to-all-start.5 = ((f32[16,32,128]{2,1,0:T(8,128)}), f32[16,32,128]{2,1,0:T(8,128)S(1)}, u32[]{:S(2)}, u32[]{:S(2)}) async-start(f32[16,32,128]{2,1,0:T(8,128)} %shard_map.94), calls=%async_computation.5 | async-start | bytes 524288 | tf_op jit(solution)/shard_map/all_to_all | solution.py:212
  77.3 1.0 copy-start.7
  80.6 13.5 %collective-permute-start.2 = (f32[128,1024]{1,0:T(8,128)}, f32[128,1024]{1,0:T(8,128)S(1)}, u32[]{:S(2)}, u32[]{:S(2)}) collective-permute-start(f32[128,1024]{1,0:T(8,128)} %get-tuple-element.37), channel_id=1, source_target_pairs={{0,1},{1,0},{2,3},{3,2},{4,5},{5,4},{6,7},{7,6},{8,9},{9,8},{10,11... | collective-permute-start | bytes 1572872 | tf_op jit(solution)/shard_map/ppermute | solution.py:199
  88.9 6.8 %collective-permute-start.3 = (f32[128,1024]{1,0:T(8,128)S(1)}, f32[128,1024]{1,0:T(8,128)S(1)}, u32[]{:S(2)}, u32[]{:S(2)}) collective-permute-start(f32[128,1024]{1,0:T(8,128)S(1)} %get-tuple-element.45), channel_id=1, source_target_pairs={{0,1},{1,0},{2,3},{3,2},{4,5},{5,4},{6,7},{7,6},{8,9},{9,8},{10,11... | collective-permute-start | bytes 1572872 | tf_op jit(solution)/shard_map/ppermute | solution.py:199

commit v2 on v0

v2 whole, which is shorter than its diff:
```python
import functools

import jax
import jax.numpy as jnp
from jax import lax
from jax.experimental import pallas as pl
from jax.experimental.pallas import tpu as pltpu
from jax.sharding import Mesh, PartitionSpec as P

HEADS = 8
HEAD_DIM = 128
TOK = 128
HALF = HEADS // 2
WIDE = HALF * HEAD_DIM
PAIR = 2 * TOK
SIDE, NZ = 4, 8
RUN = SIDE * PAIR
PIECE = HEAD_DIM // SIDE
EPSILON = 1e-06
F32, BF16 = jnp.float32, jnp.bfloat16

NT = (((1,), (1,)), ((), ()))
TN = (((0,), (0,)), ((), ()))
NN = (((1,), (0,)), ((), ()))


def dot(a, b, dims):
    return lax.dot_general(a, b, dims, preferred_element_type=F32)


def call(body, outs, scratch=(), spots=(), cost=None, kept=None, room=12):
    specs = [pl.BlockSpec(memory_space=spot) for spot in spots]
    return pl.pallas_call(
        body,
        out_shape=[jax.ShapeDtypeStruct(shape, dtype) for shape, dtype in outs],
        scratch_shapes=list(scratch),
        compiler_params=pltpu.CompilerParams(vmem_limit_bytes=room * 2**20),
        cost_estimate=cost and pl.CostEstimate(flops=cost, bytes_accessed=0, transcendentals=0),
        **({"in_specs": specs} if specs else {}),
        **({"out_specs": [pl.BlockSpec(memory_space=m) for m in kept]} if kept else {}),
    )


VM, ANY = pltpu.VMEM, pl.ANY


def halves():
    core = lax.axis_index("core")
    mine = pl.ds(pl.multiple_of(core * WIDE, WIDE), WIDE)
    other = pl.ds(pl.multiple_of((1 - core) * WIDE, WIDE), WIDE)
    return mine, other


def rows():
    core = lax.axis_index("core")
    mine = pl.ds(pl.multiple_of(core * TOK, TOK), TOK)
    other = pl.ds(pl.multiple_of((1 - core) * TOK, TOK), TOK)
    return mine, other


def head(h):
    return pl.ds(h * HEAD_DIM, HEAD_DIM)


def block(b):
    return pl.ds(b * TOK, TOK)


def quarter(i):
    return pl.ds(i * PIECE, PIECE)


def line(shift):
    core = lax.axis_index("core")
    place = lax.axis_index("x") * (1 - core) + lax.axis_index("y") * core
    return lax.rem(place + SIDE + shift, SIDE)


def cross(shift):
    core = lax.axis_index("core")
    place = lax.axis_index("y") * (1 - core) + lax.axis_index("x") * core
    return lax.rem(place + SIDE + shift, SIDE)


def chip(across, along):
    core = lax.axis_index("core")
    return across * (SIDE - core * (SIDE - 1)) + along * (1 + core * (SIDE - 1))


def causal():
    return lax.broadcasted_iota(jnp.int32, (TOK, TOK), 0) >= lax.broadcasted_iota(
        jnp.int32, (TOK, TOK), 1
    )


def pack_body(a_ref, b_ref, send_ref):
    _, other = halves()
    send_ref[:, :WIDE] = a_ref[:, other].astype(F32)
    send_ref[:, WIDE:] = b_ref[:, other].astype(F32)


def unpack(ref, got, out_ref):
    mine, _ = halves()
    at, far = rows()
    out_ref[at, :] = ref[:, mine]
    out_ref[far, :] = got.astype(BF16)


def state_body(k_ref, v_ref, got_ref, _, k2_ref, v2_ref, pieces_ref):
    unpack(k_ref, got_ref[:, :WIDE], k2_ref)
    unpack(v_ref, got_ref[:, WIDE:], v2_ref)
    for h in range(HALF):
        state = dot(k2_ref[:, head(h)], v2_ref[:, head(h)], TN)
        for i in range(SIDE):
            pieces_ref[chip(i, h)] = state[i * PIECE : (i + 1) * PIECE]


def spread_body(q_ref, dy_ref, got_ref, k2_ref, v2_ref, q2_ref, dy2_ref, *send_refs):
    unpack(q_ref, got_ref[:, :WIDE], q2_ref)
    unpack(dy_ref, got_ref[:, WIDE:], dy2_ref)
    for s, send_ref in enumerate(send_refs):
        channels = pl.ds(pl.multiple_of(line(s + 1) * HEAD_DIM, HEAD_DIM), HEAD_DIM)
        for i, ref in enumerate((k2_ref, v2_ref, q2_ref, dy2_ref)):
            send_ref[:, head(i)] = ref[:, channels].astype(F32)


def line_body(
    k2_ref, v2_ref, q2_ref, dy2_ref, gain_ref, got1_ref, got2_ref, got3_ref,
    q_ref, dy_ref, gain_out, intra_ref, first_ref, k_ref, v_ref,
):
    refs = (k_ref, v_ref, q_ref, dy_ref)
    place = line(0)
    channels = pl.ds(pl.multiple_of(place * HEAD_DIM, HEAD_DIM), HEAD_DIM)
    at = pl.ds(pl.multiple_of(place * PAIR, PAIR), PAIR)
    for ref, own_ref in zip(refs, (k2_ref, v2_ref, q2_ref, dy2_ref)):
        ref[at, :] = own_ref[:, channels]
    for s, got_ref in enumerate((got1_ref, got2_ref, got3_ref)):
        at = pl.ds(pl.multiple_of(line(-1 - s) * PAIR, PAIR), PAIR)
        for i, ref in enumerate(refs):
            ref[at, :] = got_ref[:, head(i)].astype(BF16)
    whole = lax.axis_index("core") * WIDE + place * HEAD_DIM
    gain = gain_ref[:, pl.ds(pl.multiple_of(whole, HEAD_DIM), HEAD_DIM)]
    gain_out[...] = jnp.broadcast_to(gain, gain_out.shape)
    mask = causal()
    for b in range(2 * SIDE):
        k, v = k_ref[block(b), :], v_ref[block(b), :]
        weights = jnp.where(mask, dot(q_ref[block(b), :], k, NT), 0.0).astype(BF16)
        intra_ref[block(b), :] = dot(weights, v, NN)
        if b % 2 == 0:
            first_ref[b // 2] = dot(k, v, TN)


def plane_body(parts_ref, _, total_ref, sums_ref):
    running = jnp.zeros(parts_ref.shape[1:], F32)
    for p in range(SIDE * SIDE):
        sums_ref[p] = running
        running = running + parts_ref[p]
    for g in range(NZ):
        total_ref[g] = running


def before_body(sums_ref, got_ref, *out_refs):
    z = lax.axis_index("z")
    base = jnp.zeros(got_ref.shape[1:], F32)
    for g in range(NZ - 1):
        base = base + jnp.where(g < z, got_ref[g], 0.0)
    for s, ref in enumerate(out_refs):
        for j in range(SIDE):
            ref[j] = sums_ref[chip(cross(s), j)] + base


def deltas(out, g):
    inverse = lax.rsqrt(jnp.mean(out * out, axis=-1, keepdims=True) + EPSILON)
    normed = out * inverse
    mean = jnp.mean(g * normed, axis=-1, keepdims=True)
    return normed, (inverse * (g - normed * mean)).astype(BF16)


def turn_body(
    q_ref, dy_ref, gain_ref, intra_ref, first_ref, w0, w1, w2, w3,
    p0, p1, p2, p3, before_ref, pairs_ref,
):
    for s, ref in enumerate((w0, w1, w2, w3)):
        at = pl.ds(pl.multiple_of(cross(-s) * PIECE, PIECE), PIECE)
        for j in range(SIDE):
            before_ref[j, at, :] = ref[j]
    gain = gain_ref[:1, :]
    for j in range(SIDE):
        before = before_ref[j]
        for b in range(2):
            at = block(2 * j + b)
            q = q_ref[at, :]
            if b:
                before = before + first_ref[j]
            out = intra_ref[at, :] + dot(q, before.astype(BF16), NN)
            _, delta = deltas(out, dy_ref[at, :].astype(F32) * gain)
            state = dot(q, delta, TN)
            pair = pair + state if b else state
        pairs_ref[j] = pair
    for s, ref in enumerate((p0, p1, p2, p3)):
        at = pl.ds(pl.multiple_of(cross(s) * PIECE, PIECE), PIECE)
        for j in range(SIDE):
            ref[j] = pairs_ref[j, at, :]


def gather_body(p0, p1, p2, p3, before_ref, total_ref, pairs_ref, b0, b1, b2, b3):
    total = jnp.zeros(p0.shape[1:], F32)
    for s, ref in enumerate((p0, p1, p2, p3)):
        for j in range(SIDE):
            pairs_ref[chip(cross(-s), j)] = ref[j]
            total = total + ref[j]
    for g in range(NZ):
        total_ref[g] = total
    for s, ref in enumerate((b0, b1, b2, b3)):
        ref[...] = before_ref[line(s)]


def later_body(pairs_ref, got_ref, _0, _1, _2, out_ref):
    z = lax.axis_index("z")
    running = jnp.zeros(got_ref.shape[1:], F32)
    for g in range(1, NZ):
        running = running + jnp.where(g > z, got_ref[g], 0.0)
    for p in reversed(range(SIDE * SIDE)):
        out_ref[p] = running
        running = running + pairs_ref[p]


def back_body(
    q2_ref, k2_ref, v2_ref, dy2_ref, gain_ref, b0, b1, b2, b3,
    send_ref, own_ref, gk_ref, gv_ref, second_ref, before_ref, all_ref,
):
    mine, _ = halves()
    own, far = rows()
    for s, ref in enumerate((b0, b1, b2, b3)):
        before_ref[line(-s)] = ref[...]
    mask = causal()
    gains = gain_ref[:, mine]
    for h in range(HALF):
        gain = gains[:, h * HEAD_DIM : (h + 1) * HEAD_DIM]
        query = pl.ds(WIDE + h * HEAD_DIM, HEAD_DIM)
        before = before_ref[h]
        for b in range(2):
            at = block(b)
            q, k, v = q2_ref[at, head(h)], k2_ref[at, head(h)], v2_ref[at, head(h)]
            before_b = before.astype(BF16)
            if b == 0:
                before = before + dot(k, v, TN)
            weights = jnp.where(mask, dot(q, k, NT), 0.0).astype(BF16)
            out = dot(weights, v, NN) + dot(q, before_b, NN)
            normed, delta = deltas(out, dy2_ref[at, head(h)].astype(F32) * gain)
            all_ref[at, head(h)] = normed * gain
            scores = jnp.where(mask, dot(delta, v, NT), 0.0).astype(BF16)
            all_ref[at, query] = dot(scores, k, NN) + dot(delta, before_b, NT)
            gk_ref[at, head(h)] = dot(scores, q, TN)
            gv_ref[at, head(h)] = dot(weights, delta, TN)
        second_ref[h] = dot(q, delta, TN)
    own_ref[...] = all_ref[own, :].astype(BF16)
    send_ref[...] = all_ref[far, :].astype(BF16).astype(F32)


def final_body(mine, k2_ref, v2_ref, later_ref, second_ref, gk_ref, gv_ref, out_ref):
    own, far = rows()
    at = own if mine else far
    core = lax.axis_index("core")
    b = core if mine else 1 - core
    for h in range(HALF):
        value = pl.ds(WIDE + h * HEAD_DIM, HEAD_DIM)
        later = jnp.concatenate([later_ref[chip(i, h)] for i in range(SIDE)], axis=0)
        after = (later + jnp.where(b == 0, second_ref[h], 0.0)).astype(BF16)
        gk = gk_ref[at, head(h)] + dot(v2_ref[at, head(h)], after, NT)
        gv = gv_ref[at, head(h)] + dot(k2_ref[at, head(h)], after, NN)
        out_ref[:, head(h)] = gk.astype(BF16).astype(out_ref.dtype)
        out_ref[:, value] = gv.astype(BF16).astype(out_ref.dtype)


def merge_body(own_ref, got_ref, a_ref, b_ref):
    mine, other = halves()
    a_ref[:, mine] = own_ref[:, :WIDE]
    a_ref[:, other] = got_ref[:, :WIDE].astype(BF16)
    b_ref[:, mine] = own_ref[:, WIDE:]
    b_ref[:, other] = got_ref[:, WIDE:].astype(BF16)


def swap(x):
    return lax.ppermute(x, "core", [(0, 1), (1, 0)])


AXES = ("z", "y", "x", "core")


def device(z, core, across, along):
    y, x = (along, across) if core else (across, along)
    return ((z * SIDE + y) * SIDE + x) * 2 + core


def places():
    return [
        (z, core, i, j) for z in range(NZ) for core in range(2) for i in range(SIDE) for j in range(SIDE)
    ]


def shift_line(arrays):
    return [
        lax.ppermute(
            a, AXES, [(device(z, c, i, j), device(z, c, i, (j + s) % SIDE)) for z, c, i, j in places()]
        )
        for s, a in enumerate(arrays, 1)
    ]


def shift_cross(arrays):
    return [
        lax.ppermute(
            a, AXES, [(device(z, c, i, j), device(z, c, (i + s) % SIDE, j)) for z, c, i, j in places()]
        )
        for s, a in enumerate(arrays, 1)
    ]


def per_device(queries, key_rows, value_rows, channel_gain, out_cotangent):
    own_shape = (TOK, HEADS * HEAD_DIM)
    pair = (PAIR, WIDE)
    slices = ((SIDE * SIDE, PIECE, HEAD_DIM), F32)
    copies = ((NZ, PIECE, HEAD_DIM), F32)
    some = ((SIDE, PIECE, HEAD_DIM), F32)
    states = ((SIDE, HEAD_DIM, HEAD_DIM), F32)
    square = ((HEAD_DIM, HEAD_DIM), F32)
    gain = channel_gain.reshape(1, -1)
    pack = call(pack_body, [(own_shape, F32)])
    kv_got = swap(pack(key_rows, value_rows)[0])
    qd_got = swap(pack(queries, out_cotangent)[0])
    k2, v2, pieces = call(state_body, [(pair, BF16), (pair, BF16), slices], spots=(VM,) * 3 + (ANY,))(
        key_rows, value_rows, kv_got, qd_got
    )
    parts = lax.all_to_all(pieces, ("y", "x"), 0, 0, tiled=True)
    q2, dy2, *sends = call(spread_body, [(pair, BF16)] * 2 + [(pair, F32)] * (SIDE - 1))(
        queries, out_cotangent, qd_got, k2, v2
    )
    run = (RUN, HEAD_DIM)
    qh, dyh, gain_h, intra_h, first = call(
        line_body,
        [(run, BF16), (run, BF16), ((8, HEAD_DIM), F32), (run, F32), states],
        [pltpu.VMEM(run, BF16), pltpu.VMEM(run, BF16)],
        cost=10**11,
    )(k2, v2, q2, dy2, gain, *shift_line(sends))
    total, sums = call(plane_body, [copies, slices], spots=(VM, ANY), cost=10**11)(parts, dy2)
    earlier = lax.all_to_all(total, "z", 0, 0, tiled=True)
    w_own, *w_sends = call(before_body, [some] * SIDE)(sums, earlier)
    p_own, p1, p2, p3, before = call(
        turn_body, [some] * SIDE + [states], [pltpu.VMEM(*states)]
    )(qh, dyh, gain_h, intra_h, first, w_own, *shift_cross(w_sends))
    total, pairs, b_own, *b_sends = call(gather_body, [copies, slices] + [square] * SIDE)(
        p_own, *shift_cross((p1, p2, p3)), before
    )
    totals = lax.all_to_all(total, "z", 0, 0, tiled=True)
    b_got = shift_line(b_sends)
    (later,) = call(later_body, [slices], spots=(VM,) * 2 + (ANY,) * 3)(pairs, totals, *b_got)
    send, own, gk, gv, second = call(
        back_body,
        [(own_shape, F32), (own_shape, BF16), (pair, F32), (pair, F32), states],
        [pltpu.VMEM(*states), pltpu.VMEM((PAIR, 2 * WIDE), F32)],
    )(q2, k2, v2, dy2, gain, b_own, *b_got)
    merge = call(merge_body, [(own_shape, BF16), (own_shape, BF16)])
    attended, grad_query = merge(own, swap(send))
    after = lax.all_to_all(later, ("y", "x"), 0, 0, tiled=True)
    last = (k2, v2, after, second, gk, gv)
    (last_send,) = call(functools.partial(final_body, False), [(own_shape, F32)])(*last)
    last_got = swap(last_send)
    (last_own,) = call(functools.partial(final_body, True), [(own_shape, BF16)])(*last)
    grad_key, grad_value = merge(last_own, last_got)
    return attended, grad_query, grad_key, grad_value


def solution(mesh):
    fine = Mesh(mesh.devices.reshape(NZ, SIDE, SIDE, 2), AXES)
    placed = P(AXES, None)
    return jax.shard_map(
        per_device,
        mesh=fine,
        in_specs=(placed, placed, placed, P(), placed),
        out_specs=(placed, placed, placed, placed),
        check_vma=False,
    )
```

time: 583 us -> 87.4 us (0.15)
  waiting for transfers between devices: 449 us -> 13.8 us
  other arithmetic: 98.9 us -> 0 us
  starting transfers between devices: 0.16 us -> 41.1 us
  blocking collectives: 0 us -> 15.9 us
  between operations: 14.3 us -> 0.77 us
  Pallas kernels: 0 us -> 13.3 us
  local copies, waits for them, and re-layouts: 8.84 us -> 1.92 us
  matrix products: 6.16 us -> 0 us
    psum x2 -> x0, waiting for transfers between devices: 229 us -> none  [the longest x1 116 us: state_after(): total = lax.psum(local_state, 'seq')]
    all_gather x4 -> x0, waiting for transfers between devices: 218 us -> none  [entering(): everything = lax.all_gather(x, axis)]
    select_n x80 -> x0, other arithmetic: 98.3 us -> none  [step(): return jnp.where(reached, new, before)]
    ppermute x0 -> x16, starting transfers between devices: none -> 29 us  [the longest x4 14.5 us: swap(): return lax.ppermute(x, 'core', [(0, 1), (1, 0)])]
    all_to_all x0 -> x1, blocking collectives: none -> 15.9 us  [per_device(): earlier = lax.all_to_all(total, 'z', 0, 0, tiled=True)]
    pallas_call x0 -> x15, Pallas kernels: none -> 13.3 us  [the longest x1 5.56 us: per_device(): call(back_body, [(own_shape, F32), (own_shape, BF16), (pair, F32), (pair,...]
    all_to_all x0 -> x3, starting transfers between devices: none -> 12.1 us  [the longest x1 5.02 us: per_device(): parts = lax.all_to_all(pieces, ('y', 'x'), 0, 0, tiled=True)]
    ppermute x0 -> x16, waiting for transfers between devices: none -> 9.74 us  [the longest x6 4.83 us: shift_cross(): lax.ppermute(a, AXES, [(device(z, c, i, j), device(z, c, (i + s) % SIDE,...]
  transfers between devices with their start and end apart: 6 -> 19, of which waited for: 6 -> 12; matrix products, arithmetic and copies ran while one was open for 10% -> 0% of each run, Pallas kernels for 0% -> 11%
where the time goes in v2:
time: 87.4 us; the launch traced here: 86.9 us
  starting transfers between devices  41.1 us (47%)
  blocking collectives  15.9 us (18%)
  waiting for transfers between devices  13.8 us (16%)
  Pallas kernels  13.3 us (15%)
  local copies, waits for them, and re-layouts  1.92 us (2%)
    all_to_all x1, blocking collectives, per_device(): earlier = lax.all_to_all(total, 'z', 0, 0, tiled=True)  15.9 us
    ppermute x4, starting transfers between devices, swap(): return lax.ppermute(x, 'core', [(0, 1), (1, 0)])  14.5 us
    ppermute x6, starting transfers between devices, shift_line(): lax.ppermute(a, AXES, [(device(z, c, i, j), device(z, c, i, (j + s) % SID...  7.7 us
    ppermute x6, starting transfers between devices, shift_cross(): lax.ppermute(a, AXES, [(device(z, c, i, j), device(z, c, (i + s) % SIDE,...  6.82 us
    pallas_call x1, Pallas kernels, per_device(): call(back_body, [(own_shape, F32), (own_shape, BF16), (pair, F32), (pair,...  5.56 us
    all_to_all x1, starting transfers between devices, per_device(): parts = lax.all_to_all(pieces, ('y', 'x'), 0, 0, tiled=True)  5.02 us
    ppermute x6, waiting for transfers between devices, shift_cross(): lax.ppermute(a, AXES, [(device(z, c, i, j), device(z, c, (i + s) % SIDE,...  4.83 us
    all_to_all x1, starting transfers between devices, per_device(): after = lax.all_to_all(later, ('y', 'x'), 0, 0, tiled=True)  3.71 us
  transfers between devices with their start and end apart: 19, of which 12 were waited for; matrix products, arithmetic and copies ran while one was open for 0% of the time, Pallas kernels for 11%

profile of v2, /device:TPU:1, one launch (start us, length us, event | category | flops | bytes accessed | tf_op | source)
XLA Modules:
  0.0 86.9 jit_solution(7498414323888923827)
XLA Ops:
  0.6 0.0 copy-start
  0.6 0.9 %copy-done = bf16[128,1024]{1,0:T(8,128)(2,1)S(1)} copy-done((bf16[128,1024]{1,0:T(8,128)(2,1)S(1)}, bf16[128,1024]{1,0:T(8,128)(2,1)}, u32[]{:S(2)}) %copy-start) | copy-done | bytes 262168
  1.6 0.0 copy-start.2
  1.6 0.9 %copy-done.2 = bf16[128,1024]{1,0:T(8,128)(2,1)S(1)} copy-done((bf16[128,1024]{1,0:T(8,128)(2,1)S(1)}, bf16[128,1024]{1,0:T(8,128)(2,1)}, u32[]{:S(2)}) %copy-start.2) | copy-done | bytes 262168
  2.5 0.0 copy-start.4
  2.5 0.0 copy-start.5
  2.6 0.0 copy-start.1
  2.6 0.0 copy-start.3
  2.6 3.3 %collective-permute-start.1 = (f32[128,1024]{1,0:T(8,128)S(1)}, f32[128,1024]{1,0:T(8,128)S(1)}, u32[]{:S(2)}, u32[]{:S(2)}) collective-permute-start(f32[128,1024]{1,0:T(8,128)S(1)} %shard_map.85), channel_id=1, source_target_pairs={{0,1},{1,0},{2,3},{3,2},{4,5},{5,4},{6,7},{7,6},{8,9},{9,8},{10,11... | collective-permute-start | bytes 1572872 | tf_op jit(solution)/shard_map/ppermute | solution.py:285
  5.9 0.0 copy-done.4
  5.9 0.0 copy-done.5
  6.0 1.0 %collective-permute-start = (f32[128,1024]{1,0:T(8,128)S(1)}, f32[128,1024]{1,0:T(8,128)S(1)}, u32[]{:S(2)}, u32[]{:S(2)}) collective-permute-start(f32[128,1024]{1,0:T(8,128)S(1)} %shard_map.84), channel_id=1, source_target_pairs={{0,1},{1,0},{2,3},{3,2},{4,5},{5,4},{6,7},{7,6},{8,9},{9,8},{10,11... | collective-permute-start | bytes 1572872 | tf_op jit(solution)/shard_map/ppermute | solution.py:285
  6.9 0.5 collective-permute-done.1.got_ref
  7.5 1.0 %collective-permute-done._.got_ref = f32[128,1024]{1,0:T(8,128)S(1)} collective-permute-done((f32[128,1024]{1,0:T(8,128)S(1)}, f32[128,1024]{1,0:T(8,128)S(1)}, u32[]{:S(2)}, u32[]{:S(2)}) %collective-permute-start) | collective-permute-done | bytes 524320 | tf_op jit(solution)/shard_map/ppermute | solution.py:285
  8.5 0.0 copy-done.1
  8.5 0.0 copy-done.3
  8.5 1.0 %shard_map.86 = (bf16[256,512]{1,0:T(8,128)(2,1)S(1)}, bf16[256,512]{1,0:T(8,128)(2,1)S(1)}, f32[16,32,128]{2,1,0:T(8,128)}) custom-call(bf16[128,1024]{1,0:T(8,128)(2,1)S(1)} %copy-done.1, bf16[128,1024]{1,0:T(8,128)(2,1)S(1)} %copy-done.3, f32[128,1024]{1,0:T(8,128)S(1)} %collective-permute-done.1.got_ref, f32[128,1024]{1,0:T(8,128)S(1)} %collective-permute-done._.got_ref), custom_call_target="tpu_custom_call" | custom-call | tf_op jit(solution)/shard_map/pallas_call | solution.py:332
  9.5 5.0 %all-to-all-start = ((f32[16,32,128]{2,1,0:T(8,128)}), f32[16,32,128]{2,1,0:T(8,128)S(1)}, u32[]{:S(2)}, u32[]{:S(2)}) async-start(f32[16,32,128]{2,1,0:T(8,128)} %get-tuple-element.55), calls=%async_computation | async-start | bytes 524288 | tf_op jit(solution)/shard_map/all_to_all | solution.py:335
  14.5 1.3 %shard_map.87 = (bf16[256,512]{1,0:T(8,128)(2,1)S(1)}, bf16[256,512]{1,0:T(8,128)(2,1)S(1)}, f32[256,512]{1,0:T(8,128)}, f32[256,512]{1,0:T(8,128)}, f32[256,512]{1,0:T(8,128)}) custom-call(bf16[128,1024]{1,0:T(8,128)(2,1)S(1)} %copy-done.4, bf16[128,1024]{1,0:T(8,128)(2,1)S(1)} %copy-done.5, f32[128,1024]{1,0:T(8,128)S(1)} %collective-permute-done._.got_ref, ...), custom_call_target="tpu_custom_call" | custom-call | tf_op jit(solution)/shard_map/pallas_call | solution.py:336
  15.8 1.4 %collective-permute-start.2 = (f32[256,512]{1,0:T(8,128)}, f32[256,512]{1,0:T(8,128)S(1)}, u32[]{:S(2)}, u32[]{:S(2)}) collective-permute-start(f32[256,512]{1,0:T(8,128)} %get-tuple-element.47), channel_id=1, source_target_pairs={{0,2},{2,4},{4,6},{6,0},{8,10},{10,12},{12,14},{14,8},{16,18},{18,... | collective-permute-start | bytes 1572872 | tf_op jit(solution)/shard_map/ppermute | solution.py:304
  17.2 2.4 %collective-permute-start.3 = (f32[256,512]{1,0:T(8,128)}, f32[256,512]{1,0:T(8,128)S(1)}, u32[]{:S(2)}, u32[]{:S(2)}) collective-permute-start(f32[256,512]{1,0:T(8,128)} %get-tuple-element.48), channel_id=1, source_target_pairs={{0,4},{2,6},{4,0},{6,2},{8,12},{10,14},{12,8},{14,10},{16,20},{18,... | collective-permute-start | bytes 1572872 | tf_op jit(solution)/shard_map/ppermute | solution.py:304
  19.6 1.2 %collective-permute-start.4 = (f32[256,512]{1,0:T(8,128)}, f32[256,512]{1,0:T(8,128)S(1)}, u32[]{:S(2)}, u32[]{:S(2)}) collective-permute-start(f32[256,512]{1,0:T(8,128)} %get-tuple-element.49), channel_id=1, source_target_pairs={{0,6},{2,0},{4,2},{6,4},{8,14},{10,8},{12,10},{14,12},{16,22},{18,... | collective-permute-start | bytes 1572872 | tf_op jit(solution)/shard_map/ppermute | solution.py:304
  20.7 1.9 %all-to-all-done.parts_ref = f32[16,32,128]{2,1,0:T(8,128)S(1)} async-done(((f32[16,32,128]{2,1,0:T(8,128)}), f32[16,32,128]{2,1,0:T(8,128)S(1)}, u32[]{:S(2)}, u32[]{:S(2)}) %all-to-all-start) | async-done | bytes 262176 | tf_op jit(solution)/shard_map/all_to_all | solution.py:335
  22.7 15.9 %all_to_all.20.got_ref = f32[8,32,128]{2,1,0:T(8,128)S(1)} all-to-all(f32[8,32,128]{2,1,0:T(8,128)S(1)} %get-tuple-element.57), channel_id=1, replica_groups=mesh['z'=8,'y'=4,'x'=4,'core'=2] {'z'}, dimensions={0} | all-to-all | bytes 262144 | tf_op jit(solution)/shard_map/all_to_all | solution.py:347
  38.6 0.0 copy-start.6
  38.6 0.4 collective-permute-start.5
  39.0 1.5 %collective-permute-start.6 = (f32[4,32,128]{2,1,0:T(8,128)S(1)}, f32[4,32,128]{2,1,0:T(8,128)S(1)}, u32[]{:S(2)}, u32[]{:S(2)}) collective-permute-start(f32[4,32,128]{2,1,0:T(8,128)S(1)} %get-tuple-element.60), channel_id=1, source_target_pairs={{0,16},{2,18},{4,20},{6,22},{8,24},{10,26},{12,28},{14,30},{16,0},... | collective-permute-start | bytes 196616 | tf_op jit(solution)/shard_map/ppermute | solution.py:313
  40.5 0.0 collective-permute-done.2.got1_ref
  40.5 1.1 %collective-permute-start.7 = (f32[4,32,128]{2,1,0:T(8,128)S(1)}, f32[4,32,128]{2,1,0:T(8,128)S(1)}, u32[]{:S(2)}, u32[]{:S(2)}) collective-permute-start(f32[4,32,128]{2,1,0:T(8,128)S(1)} %get-tuple-element.61), channel_id=1, source_target_pairs={{0,24},{2,26},{4,28},{6,30},{8,0},{10,2},{12,4},{14,6},{16,8},{18,... | collective-permute-start | bytes 196616 | tf_op jit(solution)/shard_map/ppermute | solution.py:313
  41.6 0.0 collective-permute-done.3.got2_ref
  41.6 0.0 collective-permute-done.4.got3_ref
  41.6 0.0 copy-done.6
  41.6 1.0 %shard_map.88 = (bf16[1024,128]{1,0:T(8,128)(2,1)S(1)}, bf16[1024,128]{1,0:T(8,128)(2,1)S(1)}, f32[8,128]{1,0:T(8,128)S(1)}, f32[1024,128]{1,0:T(8,128)S(1)}, f32[4,128,128]{2,1,0:T(8,128)S(1)}) custom-call(bf16[256,512]{1,0:T(8,128)(2,1)S(1)} %get-tuple-element.43.k2_ref, bf16[256,512]{1,0:T(8,128)(2,1)S(1)} %get-tuple-element.44.v2_ref, ...), custom_call_target="tpu_custom_call" | custom-call | flops 99999997952 | tf_op jit(solution)/shard_map/pallas_call | solution.py:340
  42.6 1.1 %collective-permute-done.5.w1 = f32[4,32,128]{2,1,0:T(8,128)S(1)} collective-permute-done((f32[4,32,128]{2,1,0:T(8,128)S(1)}, f32[4,32,128]{2,1,0:T(8,128)S(1)}, u32[]{:S(2)}, u32[]{:S(2)}) %collective-permute-start.5) | collective-permute-done | bytes 65568 | tf_op jit(solution)/shard_map/ppermute | solution.py:313
  43.7 0.0 collective-permute-done.6.w2
  43.7 0.6 collective-permute-done.7.w3
  44.3 0.7 shard_map.91
  45.1 0.8 collective-permute-start.8
  45.9 3.0 %collective-permute-start.9 = (f32[4,32,128]{2,1,0:T(8,128)S(1)}, f32[4,32,128]{2,1,0:T(8,128)S(1)}, u32[]{:S(2)}, u32[]{:S(2)}) collective-permute-start(f32[4,32,128]{2,1,0:T(8,128)S(1)} %get-tuple-element.64), channel_id=1, source_target_pairs={{0,16},{2,18},{4,20},{6,22},{8,24},{10,26},{12,28},{14,30},{16,0},... | collective-permute-start | bytes 196616 | tf_op jit(solution)/shard_map/ppermute | solution.py:313
  48.9 0.0 collective-permute-start.10
  48.9 0.5 collective-permute-done.8.p1
  49.5 1.8 %collective-permute-done.9.p2 = f32[4,32,128]{2,1,0:T(8,128)S(1)} collective-permute-done((f32[4,32,128]{2,1,0:T(8,128)S(1)}, f32[4,32,128]{2,1,0:T(8,128)S(1)}, u32[]{:S(2)}, u32[]{:S(2)}) %collective-permute-start.9) | collective-permute-done | bytes 65568 | tf_op jit(solution)/shard_map/ppermute | solution.py:313
  51.3 0.8 collective-permute-done.10.p3
  52.0 0.7 shard_map.92
  52.8 3.4 %all-to-all-start.2 = ((f32[8,32,128]{2,1,0:T(8,128)}), f32[8,32,128]{2,1,0:T(8,128)S(1)}, u32[]{:S(2)}, u32[]{:S(2)}) async-start(f32[8,32,128]{2,1,0:T(8,128)} %get-tuple-element.76), calls=%async_computation.2 | async-start | bytes 262144 | tf_op jit(solution)/shard_map/all_to_all | solution.py:355
  56.1 0.1 collective-permute-start.11
  56.2 1.4 %collective-permute-start.12 = (f32[128,128]{1,0:T(8,128)S(1)}, f32[128,128]{1,0:T(8,128)S(1)}, u32[]{:S(2)}, u32[]{:S(2)}) collective-permute-start(f32[128,128]{1,0:T(8,128)S(1)} %get-tuple-element.69), channel_id=1, source_target_pairs={{0,4},{2,6},{4,0},{6,2},{8,12},{10,14},{12,8},{14,10},{16,20},{18,... | collective-permute-start | bytes 196616 | tf_op jit(solution)/shard_map/ppermute | solution.py:304
  57.7 1.2 %collective-permute-start.13 = (f32[128,128]{1,0:T(8,128)S(1)}, f32[128,128]{1,0:T(8,128)S(1)}, u32[]{:S(2)}, u32[]{:S(2)}) collective-permute-start(f32[128,128]{1,0:T(8,128)S(1)} %get-tuple-element.70), channel_id=1, source_target_pairs={{0,6},{2,0},{4,2},{6,4},{8,14},{10,8},{12,10},{14,12},{16,22},{18,... | collective-permute-start | bytes 196616 | tf_op jit(solution)/shard_map/ppermute | solution.py:304
  58.9 2.3 %collective-permute-done.11.b1._0 = f32[128,128]{1,0:T(8,128)S(1)} collective-permute-done((f32[128,128]{1,0:T(8,128)S(1)}, f32[128,128]{1,0:T(8,128)S(1)}, u32[]{:S(2)}, u32[]{:S(2)}) %collective-permute-start.11) | collective-permute-done | bytes 65568 | tf_op jit(solution)/shard_map/ppermute | solution.py:304
  61.2 0.0 collective-permute-done.12.b2._1
  61.2 0.6 collective-permute-done.13.b3._2
  61.8 2.1 %all-to-all-done.2.got_ref = f32[8,32,128]{2,1,0:T(8,128)S(1)} async-done(((f32[8,32,128]{2,1,0:T(8,128)}), f32[8,32,128]{2,1,0:T(8,128)S(1)}, u32[]{:S(2)}, u32[]{:S(2)}) %all-to-all-start.2) | async-done | bytes 131104 | tf_op jit(solution)/shard_map/all_to_all | solution.py:355
  64.0 0.7 shard_map.95
  64.7 3.7 %all-to-all-start.3 = ((f32[16,32,128]{2,1,0:T(8,128)}), f32[16,32,128]{2,1,0:T(8,128)S(1)}, u32[]{:S(2)}, u32[]{:S(2)}) async-start(f32[16,32,128]{2,1,0:T(8,128)} %shard_map.95), calls=%async_computation.3 | async-start | bytes 524288 | tf_op jit(solution)/shard_map/all_to_all | solution.py:365
  68.4 5.6 %shard_map.93 = (f32[128,1024]{1,0:T(8,128)}, bf16[128,1024]{1,0:T(8,128)(2,1)S(1)}, f32[256,512]{1,0:T(8,128)S(1)}, f32[256,512]{1,0:T(8,128)S(1)}, f32[4,128,128]{2,1,0:T(8,128)S(1)}) custom-call(bf16[256,512]{1,0:T(8,128)(2,1)S(1)} %get-tuple-element.45.q2_ref, bf16[256,512]{1,0:T(8,128)(2,1)S(1)} %get-tuple-element.43.k2_ref, ...), custom_call_target="tpu_custom_call" | custom-call | tf_op jit(solution)/shard_map/pallas_call | solution.py:358
  74.0 7.1 %collective-permute-start.14 = (f32[128,1024]{1,0:T(8,128)}, f32[128,1024]{1,0:T(8,128)S(1)}, u32[]{:S(2)}, u32[]{:S(2)}) collective-permute-start(f32[128,1024]{1,0:T(8,128)} %get-tuple-element.72), channel_id=1, source_target_pairs={{0,1},{1,0},{2,3},{3,2},{4,5},{5,4},{6,7},{7,6},{8,9},{9,8},{10,11... | collective-permute-start | bytes 1572872 | tf_op jit(solution)/shard_map/ppermute | solution.py:285
  81.1 0.0 all-to-all-done.3.later_ref
  81.1 0.2 shard_map.97
  81.3 3.2 %collective-permute-start.15 = (f32[128,1024]{1,0:T(8,128)S(1)}, f32[128,1024]{1,0:T(8,128)S(1)}, u32[]{:S(2)}, u32[]{:S(2)}) collective-permute-start(f32[128,1024]{1,0:T(8,128)S(1)} %shard_map.97), channel_id=1, source_target_pairs={{0,1},{1,0},{2,3},{3,2},{4,5},{5,4},{6,7},{7,6},{8,9},{9,8},{10,11... | collective-permute-start | bytes 1572872 | tf_op jit(solution)/shard_map/ppermute | solution.py:285
  84.5 0.2 shard_map.96.own_ref
  84.7 0.0 collective-permute-done.14.got_ref
  84.8 0.8 shard_map.94
  85.6 0.4 collective-permute-done.15.got_ref
  86.0 0.8 shard_map.98
  (4 shorter events, 0.1 us)
Async XLA Ops:
  0.6 1.0 %copy-start = (bf16[128,1024]{1,0:T(8,128)(2,1)S(1)}, bf16[128,1024]{1,0:T(8,128)(2,1)}, u32[]{:S(2)}) copy-start(bf16[128,1024]{1,0:T(8,128)(2,1)} %k_ref.1) | copy-start | bytes 786436
  1.6 0.9 %copy-start.2 = (bf16[128,1024]{1,0:T(8,128)(2,1)S(1)}, bf16[128,1024]{1,0:T(8,128)(2,1)}, u32[]{:S(2)}) copy-start(bf16[128,1024]{1,0:T(8,128)(2,1)} %v_ref.1) | copy-start | bytes 786436
  2.5 3.4 %copy-start.4 = (bf16[128,1024]{1,0:T(8,128)(2,1)S(1)}, bf16[128,1024]{1,0:T(8,128)(2,1)}, u32[]{:S(2)}) copy-start(bf16[128,1024]{1,0:T(8,128)(2,1)} %q_ref.1) | copy-start | bytes 786436
  2.5 3.4 %copy-start.5 = (bf16[128,1024]{1,0:T(8,128)(2,1)S(1)}, bf16[128,1024]{1,0:T(8,128)(2,1)}, u32[]{:S(2)}) copy-start(bf16[128,1024]{1,0:T(8,128)(2,1)} %dy_ref.1) | copy-start | bytes 786436
  2.6 5.9 %copy-start.1 = (bf16[128,1024]{1,0:T(8,128)(2,1)S(1)}, bf16[128,1024]{1,0:T(8,128)(2,1)}, u32[]{:S(2)}) copy-start(bf16[128,1024]{1,0:T(8,128)(2,1)} %k_ref.1) | copy-start | bytes 786436
  2.6 5.9 %copy-start.3 = (bf16[128,1024]{1,0:T(8,128)(2,1)S(1)}, bf16[128,1024]{1,0:T(8,128)(2,1)}, u32[]{:S(2)}) copy-start(bf16[128,1024]{1,0:T(8,128)(2,1)} %v_ref.1) | copy-start | bytes 786436
  2.6 4.9 %collective-permute-start.1 = (f32[128,1024]{1,0:T(8,128)S(1)}, f32[128,1024]{1,0:T(8,128)S(1)}, u32[]{:S(2)}, u32[]{:S(2)}) collective-permute-start(f32[128,1024]{1,0:T(8,128)S(1)} %shard_map.85), channel_id=1, source_target_pairs={{0,1},{1,0},{2,3},{3,2},{4,5},{5,4},{6,7},{7,6},{8,9},{9,8},{10,11... | collective-permute-start | bytes 1572872 | tf_op jit(solution)/shard_map/ppermute | solution.py:285
  6.0 2.5 %collective-permute-start = (f32[128,1024]{1,0:T(8,128)S(1)}, f32[128,1024]{1,0:T(8,128)S(1)}, u32[]{:S(2)}, u32[]{:S(2)}) collective-permute-start(f32[128,1024]{1,0:T(8,128)S(1)} %shard_map.84), channel_id=1, source_target_pairs={{0,1},{1,0},{2,3},{3,2},{4,5},{5,4},{6,7},{7,6},{8,9},{9,8},{10,11... | collective-permute-start | bytes 1572872 | tf_op jit(solution)/shard_map/ppermute | solution.py:285
  9.5 13.1 %all-to-all-start = ((f32[16,32,128]{2,1,0:T(8,128)}), f32[16,32,128]{2,1,0:T(8,128)S(1)}, u32[]{:S(2)}, u32[]{:S(2)}) async-start(f32[16,32,128]{2,1,0:T(8,128)} %get-tuple-element.55), calls=%async_computation | async-start | bytes 524288 | tf_op jit(solution)/shard_map/all_to_all | solution.py:335
  15.8 24.7 %collective-permute-start.2 = (f32[256,512]{1,0:T(8,128)}, f32[256,512]{1,0:T(8,128)S(1)}, u32[]{:S(2)}, u32[]{:S(2)}) collective-permute-start(f32[256,512]{1,0:T(8,128)} %get-tuple-element.47), channel_id=1, source_target_pairs={{0,2},{2,4},{4,6},{6,0},{8,10},{10,12},{12,14},{14,8},{16,18},{18,... | collective-permute-start | bytes 1572872 | tf_op jit(solution)/shard_map/ppermute | solution.py:304
  17.2 24.4 %collective-permute-start.3 = (f32[256,512]{1,0:T(8,128)}, f32[256,512]{1,0:T(8,128)S(1)}, u32[]{:S(2)}, u32[]{:S(2)}) collective-permute-start(f32[256,512]{1,0:T(8,128)} %get-tuple-element.48), channel_id=1, source_target_pairs={{0,4},{2,6},{4,0},{6,2},{8,12},{10,14},{12,8},{14,10},{16,20},{18,... | collective-permute-start | bytes 1572872 | tf_op jit(solution)/shard_map/ppermute | solution.py:304
  19.6 22.0 %collective-permute-start.4 = (f32[256,512]{1,0:T(8,128)}, f32[256,512]{1,0:T(8,128)S(1)}, u32[]{:S(2)}, u32[]{:S(2)}) collective-permute-start(f32[256,512]{1,0:T(8,128)} %get-tuple-element.49), channel_id=1, source_target_pairs={{0,6},{2,0},{4,2},{6,4},{8,14},{10,8},{12,10},{14,12},{16,22},{18,... | collective-permute-start | bytes 1572872 | tf_op jit(solution)/shard_map/ppermute | solution.py:304
  38.6 3.0 %copy-start.6 = (f32[1024]{0:T(1024)S(1)}, f32[1024]{0:T(1024)}, u32[]{:S(2)}) copy-start(f32[1024]{0:T(1024)} %param.8) | copy-start | bytes 12292
  38.6 5.1 %collective-permute-start.5 = (f32[4,32,128]{2,1,0:T(8,128)S(1)}, f32[4,32,128]{2,1,0:T(8,128)S(1)}, u32[]{:S(2)}, u32[]{:S(2)}) collective-permute-start(f32[4,32,128]{2,1,0:T(8,128)S(1)} %get-tuple-element.59), channel_id=1, source_target_pairs={{0,8},{2,10},{4,12},{6,14},{8,16},{10,18},{12,20},{14,22},{16,24},... | collective-permute-start | bytes 196616 | tf_op jit(solution)/shard_map/ppermute | solution.py:313
  39.0 4.7 %collective-permute-start.6 = (f32[4,32,128]{2,1,0:T(8,128)S(1)}, f32[4,32,128]{2,1,0:T(8,128)S(1)}, u32[]{:S(2)}, u32[]{:S(2)}) collective-permute-start(f32[4,32,128]{2,1,0:T(8,128)S(1)} %get-tuple-element.60), channel_id=1, source_target_pairs={{0,16},{2,18},{4,20},{6,22},{8,24},{10,26},{12,28},{14,30},{16,0},... | collective-permute-start | bytes 196616 | tf_op jit(solution)/shard_map/ppermute | solution.py:313
  40.5 3.8 %collective-permute-start.7 = (f32[4,32,128]{2,1,0:T(8,128)S(1)}, f32[4,32,128]{2,1,0:T(8,128)S(1)}, u32[]{:S(2)}, u32[]{:S(2)}) collective-permute-start(f32[4,32,128]{2,1,0:T(8,128)S(1)} %get-tuple-element.61), channel_id=1, source_target_pairs={{0,24},{2,26},{4,28},{6,30},{8,0},{10,2},{12,4},{14,6},{16,8},{18,... | collective-permute-start | bytes 196616 | tf_op jit(solution)/shard_map/ppermute | solution.py:313
  45.1 4.4 %collective-permute-start.8 = (f32[4,32,128]{2,1,0:T(8,128)S(1)}, f32[4,32,128]{2,1,0:T(8,128)S(1)}, u32[]{:S(2)}, u32[]{:S(2)}) collective-permute-start(f32[4,32,128]{2,1,0:T(8,128)S(1)} %get-tuple-element.63), channel_id=1, source_target_pairs={{0,8},{2,10},{4,12},{6,14},{8,16},{10,18},{12,20},{14,22},{16,24},... | collective-permute-start | bytes 196616 | tf_op jit(solution)/shard_map/ppermute | solution.py:313
  45.9 5.4 %collective-permute-start.9 = (f32[4,32,128]{2,1,0:T(8,128)S(1)}, f32[4,32,128]{2,1,0:T(8,128)S(1)}, u32[]{:S(2)}, u32[]{:S(2)}) collective-permute-start(f32[4,32,128]{2,1,0:T(8,128)S(1)} %get-tuple-element.64), channel_id=1, source_target_pairs={{0,16},{2,18},{4,20},{6,22},{8,24},{10,26},{12,28},{14,30},{16,0},... | collective-permute-start | bytes 196616 | tf_op jit(solution)/shard_map/ppermute | solution.py:313
  48.9 3.1 %collective-permute-start.10 = (f32[4,32,128]{2,1,0:T(8,128)S(1)}, f32[4,32,128]{2,1,0:T(8,128)S(1)}, u32[]{:S(2)}, u32[]{:S(2)}) collective-permute-start(f32[4,32,128]{2,1,0:T(8,128)S(1)} %get-tuple-element.65), channel_id=1, source_target_pairs={{0,24},{2,26},{4,28},{6,30},{8,0},{10,2},{12,4},{14,6},{16,8},{18,... | collective-permute-start | bytes 196616 | tf_op jit(solution)/shard_map/ppermute | solution.py:313
  52.8 11.2 %all-to-all-start.2 = ((f32[8,32,128]{2,1,0:T(8,128)}), f32[8,32,128]{2,1,0:T(8,128)S(1)}, u32[]{:S(2)}, u32[]{:S(2)}) async-start(f32[8,32,128]{2,1,0:T(8,128)} %get-tuple-element.76), calls=%async_computation.2 | async-start | bytes 262144 | tf_op jit(solution)/shard_map/all_to_all | solution.py:355
  56.1 5.1 %collective-permute-start.11 = (f32[128,128]{1,0:T(8,128)S(1)}, f32[128,128]{1,0:T(8,128)S(1)}, u32[]{:S(2)}, u32[]{:S(2)}) collective-permute-start(f32[128,128]{1,0:T(8,128)S(1)} %get-tuple-element.68), channel_id=1, source_target_pairs={{0,2},{2,4},{4,6},{6,0},{8,10},{10,12},{12,14},{14,8},{16,18},{18,... | collective-permute-start | bytes 196616 | tf_op jit(solution)/shard_map/ppermute | solution.py:304
  56.2 5.0 %collective-permute-start.12 = (f32[128,128]{1,0:T(8,128)S(1)}, f32[128,128]{1,0:T(8,128)S(1)}, u32[]{:S(2)}, u32[]{:S(2)}) collective-permute-start(f32[128,128]{1,0:T(8,128)S(1)} %get-tuple-element.69), channel_id=1, source_target_pairs={{0,4},{2,6},{4,0},{6,2},{8,12},{10,14},{12,8},{14,10},{16,20},{18,... | collective-permute-start | bytes 196616 | tf_op jit(solution)/shard_map/ppermute | solution.py:304
  57.7 4.1 %collective-permute-start.13 = (f32[128,128]{1,0:T(8,128)S(1)}, f32[128,128]{1,0:T(8,128)S(1)}, u32[]{:S(2)}, u32[]{:S(2)}) collective-permute-start(f32[128,128]{1,0:T(8,128)S(1)} %get-tuple-element.70), channel_id=1, source_target_pairs={{0,6},{2,0},{4,2},{6,4},{8,14},{10,8},{12,10},{14,12},{16,22},{18,... | collective-permute-start | bytes 196616 | tf_op jit(solution)/shard_map/ppermute | solution.py:304
  64.7 16.3 %all-to-all-start.3 = ((f32[16,32,128]{2,1,0:T(8,128)}), f32[16,32,128]{2,1,0:T(8,128)S(1)}, u32[]{:S(2)}, u32[]{:S(2)}) async-start(f32[16,32,128]{2,1,0:T(8,128)} %shard_map.95), calls=%async_computation.3 | async-start | bytes 524288 | tf_op jit(solution)/shard_map/all_to_all | solution.py:365
  74.0 10.8 %collective-permute-start.14 = (f32[128,1024]{1,0:T(8,128)}, f32[128,1024]{1,0:T(8,128)S(1)}, u32[]{:S(2)}, u32[]{:S(2)}) collective-permute-start(f32[128,1024]{1,0:T(8,128)} %get-tuple-element.72), channel_id=1, source_target_pairs={{0,1},{1,0},{2,3},{3,2},{4,5},{5,4},{6,7},{7,6},{8,9},{9,8},{10,11... | collective-permute-start | bytes 1572872 | tf_op jit(solution)/shard_map/ppermute | solution.py:285
  81.3 4.7 %collective-permute-start.15 = (f32[128,1024]{1,0:T(8,128)S(1)}, f32[128,1024]{1,0:T(8,128)S(1)}, u32[]{:S(2)}, u32[]{:S(2)}) collective-permute-start(f32[128,1024]{1,0:T(8,128)S(1)} %shard_map.97), channel_id=1, source_target_pairs={{0,1},{1,0},{2,3},{3,2},{4,5},{5,4},{6,7},{7,6},{8,9},{9,8},{10,11... | collective-permute-start | bytes 1572872 | tf_op jit(solution)/shard_map/ppermute | solution.py:285

commit v3 on v2

--- a/solution.py
+++ b/solution.py
@@ -41,7 +41,12 @@
     )
 
 
-VM, ANY = pltpu.VMEM, pl.ANY
+VM, HBM = pltpu.VMEM, pltpu.HBM
+MARK = ((8, HEAD_DIM), jnp.float32)
+
+
+def mark(ref):
+    ref[...] = jnp.zeros_like(ref)
 
 
 def halves():
@@ -93,8 +98,10 @@
     )
 
 
-def pack_body(a_ref, b_ref, send_ref):
+def pack_body(a_ref, b_ref, send_ref, *mark_refs):
     _, other = halves()
+    for ref in mark_refs:
+        mark(ref)
     send_ref[:, :WIDE] = a_ref[:, other].astype(F32)
     send_ref[:, WIDE:] = b_ref[:, other].astype(F32)
 
@@ -115,13 +122,22 @@
             pieces_ref[chip(i, h)] = state[i * PIECE : (i + 1) * PIECE]
 
 
-def spread_body(q_ref, dy_ref, got_ref, k2_ref, v2_ref, q2_ref, dy2_ref, *send_refs):
+def spread_body(
+    q_ref, dy_ref, got_ref, k2_ref, v2_ref,
+    q2_ref, dy2_ref, mark_ref, s1, s2, s3, held_ref, sems,
+):
+    mark(mark_ref)
     unpack(q_ref, got_ref[:, :WIDE], q2_ref)
     unpack(dy_ref, got_ref[:, WIDE:], dy2_ref)
-    for s, send_ref in enumerate(send_refs):
+    copies = []
+    for s, send_ref in enumerate((s1, s2, s3)):
         channels = pl.ds(pl.multiple_of(line(s + 1) * HEAD_DIM, HEAD_DIM), HEAD_DIM)
         for i, ref in enumerate((k2_ref, v2_ref, q2_ref, dy2_ref)):
-            send_ref[:, head(i)] = ref[:, channels].astype(F32)
+            held_ref[s, :, head(i)] = ref[:, channels].astype(F32)
+        copies.append(pltpu.make_async_copy(held_ref.at[s], send_ref, sems.at[s]))
+        copies[-1].start()
+    for copy in copies:
+        copy.wait()
 
 
 def line_body(
@@ -178,7 +194,7 @@
 
 def turn_body(
     q_ref, dy_ref, gain_ref, intra_ref, first_ref, w0, w1, w2, w3,
-    p0, p1, p2, p3, before_ref, pairs_ref,
+    p0, p1, p2, p3, b0, b1, b2, b3, before_ref, pairs_ref,
 ):
     for s, ref in enumerate((w0, w1, w2, w3)):
         at = pl.ds(pl.multiple_of(cross(-s) * PIECE, PIECE), PIECE)
@@ -201,9 +217,11 @@
         at = pl.ds(pl.multiple_of(cross(s) * PIECE, PIECE), PIECE)
         for j in range(SIDE):
             ref[j] = pairs_ref[j, at, :]
-
-
-def gather_body(p0, p1, p2, p3, before_ref, total_ref, pairs_ref, b0, b1, b2, b3):
+    for s, ref in enumerate((b0, b1, b2, b3)):
+        ref[...] = before_ref[line(s)]
+
+
+def gather_body(p0, p1, p2, p3, total_ref, pairs_ref):
     total = jnp.zeros(p0.shape[1:], F32)
     for s, ref in enumerate((p0, p1, p2, p3)):
         for j in range(SIDE):
@@ -211,11 +229,9 @@
             total = total + ref[j]
     for g in range(NZ):
         total_ref[g] = total
-    for s, ref in enumerate((b0, b1, b2, b3)):
-        ref[...] = before_ref[line(s)]
-
-
-def later_body(pairs_ref, got_ref, _0, _1, _2, out_ref):
+
+
+def later_body(pairs_ref, got_ref, _, out_ref):
     z = lax.axis_index("z")
     running = jnp.zeros(got_ref.shape[1:], F32)
     for g in range(1, NZ):
@@ -225,10 +241,11 @@
         running = running + pairs_ref[p]
 
 
-def back_body(
+def query_body(
     q2_ref, k2_ref, v2_ref, dy2_ref, gain_ref, b0, b1, b2, b3,
-    send_ref, own_ref, gk_ref, gv_ref, second_ref, before_ref, all_ref,
+    mark_ref, send_ref, own_ref, delta_ref, before_ref, all_ref,
 ):
+    mark(mark_ref)
     mine, _ = halves()
     own, far = rows()
     for s, ref in enumerate((b0, b1, b2, b3)):
@@ -248,14 +265,26 @@
             weights = jnp.where(mask, dot(q, k, NT), 0.0).astype(BF16)
             out = dot(weights, v, NN) + dot(q, before_b, NN)
             normed, delta = deltas(out, dy2_ref[at, head(h)].astype(F32) * gain)
+            delta_ref[at, head(h)] = delta
             all_ref[at, head(h)] = normed * gain
             scores = jnp.where(mask, dot(delta, v, NT), 0.0).astype(BF16)
             all_ref[at, query] = dot(scores, k, NN) + dot(delta, before_b, NT)
+    own_ref[...] = all_ref[own, :].astype(BF16)
+    send_ref[...] = all_ref[far, :].astype(BF16).astype(F32)
+
+
+def keys_body(q2_ref, k2_ref, v2_ref, delta_ref, gk_ref, gv_ref, second_ref):
+    mask = causal()
+    for h in range(HALF):
+        for b in range(2):
+            at = block(b)
+            q, k, v = q2_ref[at, head(h)], k2_ref[at, head(h)], v2_ref[at, head(h)]
+            delta = delta_ref[at, head(h)]
+            weights = jnp.where(mask, dot(q, k, NT), 0.0).astype(BF16)
+            scores = jnp.where(mask, dot(delta, v, NT), 0.0).astype(BF16)
             gk_ref[at, head(h)] = dot(scores, q, TN)
             gv_ref[at, head(h)] = dot(weights, delta, TN)
         second_ref[h] = dot(q, delta, TN)
-    own_ref[...] = all_ref[own, :].astype(BF16)
-    send_ref[...] = all_ref[far, :].astype(BF16).astype(F32)
 
 
 def final_body(mine, k2_ref, v2_ref, later_ref, second_ref, gk_ref, gv_ref, out_ref):
@@ -326,16 +355,23 @@
     states = ((SIDE, HEAD_DIM, HEAD_DIM), F32)
     square = ((HEAD_DIM, HEAD_DIM), F32)
     gain = channel_gain.reshape(1, -1)
-    pack = call(pack_body, [(own_shape, F32)])
-    kv_got = swap(pack(key_rows, value_rows)[0])
-    qd_got = swap(pack(queries, out_cotangent)[0])
-    k2, v2, pieces = call(state_body, [(pair, BF16), (pair, BF16), slices], spots=(VM,) * 3 + (ANY,))(
-        key_rows, value_rows, kv_got, qd_got
+    start = (1 - lax.axis_index("core")) * WIDE
+    kv_send = jnp.concatenate(
+        [lax.dynamic_slice_in_dim(a, start, WIDE, 1) for a in (key_rows, value_rows)], axis=1
+    ).astype(F32)
+    kv_got = swap(kv_send)
+    qd_send, pack_done = call(pack_body, [(own_shape, F32), MARK])(queries, out_cotangent)
+    qd_got = swap(qd_send)
+    k2, v2, pieces = call(state_body, [(pair, BF16), (pair, BF16), slices], spots=(VM,) * 4)(
+        key_rows, value_rows, kv_got, pack_done
     )
     parts = lax.all_to_all(pieces, ("y", "x"), 0, 0, tiled=True)
-    q2, dy2, *sends = call(spread_body, [(pair, BF16)] * 2 + [(pair, F32)] * (SIDE - 1))(
-        queries, out_cotangent, qd_got, k2, v2
-    )
+    q2, dy2, spread_done, *sends = call(
+        spread_body,
+        [(pair, BF16)] * 2 + [MARK] + [(pair, F32)] * (SIDE - 1),
+        [pltpu.VMEM((SIDE - 1,) + pair, F32), pltpu.SemaphoreType.DMA((SIDE - 1,))],
+        kept=(VM,) * 3 + (HBM,) * 3,
+    )(queries, out_cotangent, qd_got, k2, v2)
     run = (RUN, HEAD_DIM)
     qh, dyh, gain_h, intra_h, first = call(
         line_body,
@@ -343,23 +379,25 @@
         [pltpu.VMEM(run, BF16), pltpu.VMEM(run, BF16)],
         cost=10**11,
     )(k2, v2, q2, dy2, gain, *shift_line(sends))
-    total, sums = call(plane_body, [copies, slices], spots=(VM, ANY), cost=10**11)(parts, dy2)
+    total, sums = call(plane_body, [copies, slices], spots=(VM, VM), cost=10**11)(parts, spread_done)
     earlier = lax.all_to_all(total, "z", 0, 0, tiled=True)
     w_own, *w_sends = call(before_body, [some] * SIDE)(sums, earlier)
-    p_own, p1, p2, p3, before = call(
-        turn_body, [some] * SIDE + [states], [pltpu.VMEM(*states)]
+    p_own, p1, p2, p3, b_own, *b_sends = call(
+        turn_body,
+        [some] * SIDE + [square] * SIDE,
+        [pltpu.VMEM(*states), pltpu.VMEM(*states)],
     )(qh, dyh, gain_h, intra_h, first, w_own, *shift_cross(w_sends))
-    total, pairs, b_own, *b_sends = call(gather_body, [copies, slices] + [square] * SIDE)(
-        p_own, *shift_cross((p1, p2, p3)), before
-    )
+    b_got = shift_line(b_sends)
+    total, pairs = call(gather_body, [copies, slices])(p_own, *shift_cross((p1, p2, p3)))
     totals = lax.all_to_all(total, "z", 0, 0, tiled=True)
-    b_got = shift_line(b_sends)
-    (later,) = call(later_body, [slices], spots=(VM,) * 2 + (ANY,) * 3)(pairs, totals, *b_got)
-    send, own, gk, gv, second = call(
-        back_body,
-        [(own_shape, F32), (own_shape, BF16), (pair, F32), (pair, F32), states],
+    query_done, send, own, delta = call(
+        query_body,
+        [MARK, (own_shape, F32), (own_shape, BF16), (pair, BF16)],
         [pltpu.VMEM(*states), pltpu.VMEM((PAIR, 2 * WIDE), F32)],
+        cost=10**11,
     )(q2, k2, v2, dy2, gain, b_own, *b_got)
+    (later,) = call(later_body, [slices], spots=(VM,) * 3)(pairs, totals, query_done)
+    gk, gv, second = call(keys_body, [(pair, F32), (pair, F32), states])(q2, k2, v2, delta)
     merge = call(merge_body, [(own_shape, BF16), (own_shape, BF16)])
     attended, grad_query = merge(own, swap(send))
     after = lax.all_to_all(later, ("y", "x"), 0, 0, tiled=True)

time: 87.4 us -> 86.6 us (level)
  waiting for transfers between devices: 13.8 us -> 6.96 us
  starting transfers between devices: 41.1 us -> 46.2 us
  Pallas kernels: 13.3 us -> 15 us
  local copies, waits for them, and re-layouts: 1.92 us -> 1.03 us
    ppermute x4, starting transfers between devices: 14.5 us -> 18.6 us  [swap(): return lax.ppermute(x, 'core', [(0, 1), (1, 0)])]
    ppermute x6, waiting for transfers between devices: 4.83 us -> 0.91 us  [shift_cross(): lax.ppermute(a, AXES, [(device(z, c, i, j), device(z, c, (i + s) % SIDE,...]
    ppermute x6, waiting for transfers between devices: 2.93 us -> 0.02 us  [shift_line(): lax.ppermute(a, AXES, [(device(z, c, i, j), device(z, c, i, (j + s) % SID...]
    unnamed x14, local copies, waits for them, and re-layouts: 1.92 us -> 0.04 us
    pallas_call x1, Pallas kernels: 0.99 us -> 2.03 us  [per_device(): call(line_body, [(run, BF16), (run, BF16), ((8, HEAD_DIM), F32), (run, F3...]
    dynamic_slice x0 -> x1, local copies, waits for them, and re-layouts: none -> 0.99 us  [per_device(): lax.dynamic_slice_in_dim(a, start, WIDE, 1)]
    all_to_all x1, starting transfers between devices: 3.71 us -> 4.69 us  [per_device(): after = lax.all_to_all(later, ('y', 'x'), 0, 0, tiled=True)]
    ppermute x4, waiting for transfers between devices: 1.98 us -> 1.01 us  [swap(): return lax.ppermute(x, 'core', [(0, 1), (1, 0)])]
  transfers between devices with their start and end apart: 19 -> 19, of which waited for: 12 -> 7; matrix products, arithmetic and copies ran while one was open for 0% -> 0% of each run, Pallas kernels for 11% -> 15%
where the time goes in v3:
time: 86.6 us; the launch traced here: 86 us
  starting transfers between devices  46.2 us (53%)
  blocking collectives  15.9 us (18%)
  Pallas kernels  15 us (17%)
  waiting for transfers between devices  6.96 us (8%)
  local copies, waits for them, and re-layouts  1.03 us (1%)
    ppermute x4, starting transfers between devices, swap(): return lax.ppermute(x, 'core', [(0, 1), (1, 0)])  18.6 us
    all_to_all x1, blocking collectives, per_device(): earlier = lax.all_to_all(total, 'z', 0, 0, tiled=True)  15.9 us
    ppermute x6, starting transfers between devices, shift_line(): lax.ppermute(a, AXES, [(device(z, c, i, j), device(z, c, i, (j + s) % SID...  7.77 us
    ppermute x6, starting transfers between devices, shift_cross(): lax.ppermute(a, AXES, [(device(z, c, i, j), device(z, c, (i + s) % SIDE,...  6.54 us
    all_to_all x1, starting transfers between devices, per_device(): parts = lax.all_to_all(pieces, ('y', 'x'), 0, 0, tiled=True)  5.02 us
    pallas_call x1, Pallas kernels, per_device(): call(query_body, [MARK, (own_shape, F32), (own_shape, BF16), (pair, BF16)...  4.73 us
    all_to_all x1, starting transfers between devices, per_device(): after = lax.all_to_all(later, ('y', 'x'), 0, 0, tiled=True)  4.69 us
    all_to_all x1, starting transfers between devices, per_device(): totals = lax.all_to_all(total, 'z', 0, 0, tiled=True)  3.55 us
  transfers between devices with their start and end apart: 19, of which 7 were waited for; matrix products, arithmetic and copies ran while one was open for 0% of the time, Pallas kernels for 15%

profile of v3, /device:TPU:1, one launch (start us, length us, event | category | flops | bytes accessed | tf_op | source)
XLA Modules:
  0.0 86.0 jit_solution(7079070882597523495)
XLA Ops:
  0.6 1.0 %constant_dynamic-slice_fusion = (bf16[128,512]{1,0:T(8,128)(2,1)S(1)}, bf16[128,512]{1,0:T(8,128)(2,1)S(1)}) fusion(bf16[128,1024]{1,0:T(8,128)(2,1)} %v_ref.1, s32[]{:T(128)S(6)} %select_n.4, bf16[128,1024]{1,0:T(8,128)(2,1)} %k_ref.1), kind=kLoop, calls=%fused_computation.1 | loop fusion | bytes 524292 | tf_op jit(solution)/shard_map/dynamic_slice | solution.py:360
  1.6 0.0 copy-start
  1.6 0.0 copy-start.1
  1.7 0.0 copy-start.2
  1.7 0.0 copy-start.3
  1.7 3.3 %collective-permute-start.1 = (f32[128,1024]{1,0:T(8,128)S(1)}, f32[128,1024]{1,0:T(8,128)S(1)}, u32[]{:S(2)}, u32[]{:S(2)}) collective-permute-start(f32[128,1024]{1,0:T(8,128)S(1)} %maximum_convert_fusion), channel_id=1, source_target_pairs={{0,1},{1,0},{2,3},{3,2},{4,5},{5,4},{6,7},{7,6},{8,9},{9,8},{10,11... | collective-permute-start | bytes 1572872 | tf_op jit(solution)/shard_map/ppermute | solution.py:314
  5.1 0.0 copy-done
  5.1 0.0 copy-done.1
  5.1 0.9 %collective-permute-start = (f32[128,1024]{1,0:T(8,128)S(1)}, f32[128,1024]{1,0:T(8,128)S(1)}, u32[]{:S(2)}, u32[]{:S(2)}) collective-permute-start(f32[128,1024]{1,0:T(8,128)S(1)} %get-tuple-element.47), channel_id=1, source_target_pairs={{0,1},{1,0},{2,3},{3,2},{4,5},{5,4},{6,7},{7,6},{8,9},{9,8},{10,11... | collective-permute-start | bytes 1572872 | tf_op jit(solution)/shard_map/ppermute | solution.py:314
  6.0 0.6 collective-permute-done.1.got_ref
  6.6 0.0 copy-done.2
  6.6 0.0 copy-done.3
  6.6 1.0 %shard_map.85 = (bf16[256,512]{1,0:T(8,128)(2,1)S(1)}, bf16[256,512]{1,0:T(8,128)(2,1)S(1)}, f32[16,32,128]{2,1,0:T(8,128)}) custom-call(bf16[128,1024]{1,0:T(8,128)(2,1)S(1)} %copy-done.2, bf16[128,1024]{1,0:T(8,128)(2,1)S(1)} %copy-done.3, f32[128,1024]{1,0:T(8,128)S(1)} %collective-permute-done.1.got_ref, f32[8,128]{1,0:T(8,128)S(1)} %get-tuple-element.48._), custom_call_target="tpu_custom_call" | custom-call | tf_op jit(solution)/shard_map/pallas_call | solution.py:365
  7.6 5.0 %all-to-all-start = ((f32[16,32,128]{2,1,0:T(8,128)}), f32[16,32,128]{2,1,0:T(8,128)S(1)}, u32[]{:S(2)}, u32[]{:S(2)}) async-start(f32[16,32,128]{2,1,0:T(8,128)} %get-tuple-element.61), calls=%async_computation | async-start | bytes 524288 | tf_op jit(solution)/shard_map/all_to_all | solution.py:368
  12.7 0.0 collective-permute-done.got_ref
  12.7 0.9 %shard_map.86 = (bf16[256,512]{1,0:T(8,128)(2,1)S(1)}, bf16[256,512]{1,0:T(8,128)(2,1)S(1)}, f32[8,128]{1,0:T(8,128)S(1)}, f32[256,512]{1,0:T(8,128)}, f32[256,512]{1,0:T(8,128)S(1)}, /*index=5*/f32[256,512]{1,0:T(8,128)S(1)}) custom-call(bf16[128,1024]{1,0:T(8,128)(2,1)S(1)} %copy-done, bf16[128,1024]{1,0:T(8,128)(2,1)S(1)} %copy-done.1, ...), custom_call_target="tpu_custom_call" | custom-call | tf_op jit(solution)/shard_map/pallas_call | solution.py:369
  13.6 0.0 copy-start.4
  13.6 1.4 %collective-permute-start.2 = (f32[256,512]{1,0:T(8,128)}, f32[256,512]{1,0:T(8,128)S(1)}, u32[]{:S(2)}, u32[]{:S(2)}) collective-permute-start(f32[256,512]{1,0:T(8,128)} %get-tuple-element.53), channel_id=1, source_target_pairs={{0,2},{2,4},{4,6},{6,0},{8,10},{10,12},{12,14},{14,8},{16,18},{18,... | collective-permute-start | bytes 1572872 | tf_op jit(solution)/shard_map/ppermute | solution.py:333
  15.1 2.4 %collective-permute-start.3 = (f32[256,512]{1,0:T(8,128)S(1)}, f32[256,512]{1,0:T(8,128)S(1)}, u32[]{:S(2)}, u32[]{:S(2)}) collective-permute-start(f32[256,512]{1,0:T(8,128)S(1)} %get-tuple-element.54), channel_id=1, source_target_pairs={{0,4},{2,6},{4,0},{6,2},{8,12},{10,14},{12,8},{14,10},{16,20},{18,... | collective-permute-start | bytes 1572872 | tf_op jit(solution)/shard_map/ppermute | solution.py:333
  17.5 1.2 %collective-permute-start.4 = (f32[256,512]{1,0:T(8,128)S(1)}, f32[256,512]{1,0:T(8,128)}, u32[]{:S(2)}, u32[]{:S(2)}) collective-permute-start(f32[256,512]{1,0:T(8,128)S(1)} %get-tuple-element.55), channel_id=1, source_target_pairs={{0,6},{2,0},{4,2},{6,4},{8,14},{10,8},{12,10},{14,12},{16,22},{18,... | collective-permute-start | bytes 1572872 | tf_op jit(solution)/shard_map/ppermute | solution.py:333
  18.6 2.1 %all-to-all-done.parts_ref = f32[16,32,128]{2,1,0:T(8,128)S(1)} async-done(((f32[16,32,128]{2,1,0:T(8,128)}), f32[16,32,128]{2,1,0:T(8,128)S(1)}, u32[]{:S(2)}, u32[]{:S(2)}) %all-to-all-start) | async-done | bytes 262176 | tf_op jit(solution)/shard_map/all_to_all | solution.py:368
  20.8 15.9 %all_to_all.20.got_ref = f32[8,32,128]{2,1,0:T(8,128)S(1)} all-to-all(f32[8,32,128]{2,1,0:T(8,128)S(1)} %get-tuple-element.64), channel_id=1, replica_groups=mesh['z'=8,'y'=4,'x'=4,'core'=2] {'z'}, dimensions={0} | all-to-all | bytes 262144 | tf_op jit(solution)/shard_map/all_to_all | solution.py:383
  36.8 0.4 collective-permute-start.5
  37.1 1.3 %collective-permute-start.6 = (f32[4,32,128]{2,1,0:T(8,128)S(1)}, f32[4,32,128]{2,1,0:T(8,128)S(1)}, u32[]{:S(2)}, u32[]{:S(2)}) collective-permute-start(f32[4,32,128]{2,1,0:T(8,128)S(1)} %get-tuple-element.67), channel_id=1, source_target_pairs={{0,16},{2,18},{4,20},{6,22},{8,24},{10,26},{12,28},{14,30},{16,0},... | collective-permute-start | bytes 196616 | tf_op jit(solution)/shard_map/ppermute | solution.py:342
  38.4 0.0 collective-permute-done.2.got1_ref
  38.4 1.2 %collective-permute-start.7 = (f32[4,32,128]{2,1,0:T(8,128)S(1)}, f32[4,32,128]{2,1,0:T(8,128)S(1)}, u32[]{:S(2)}, u32[]{:S(2)}) collective-permute-start(f32[4,32,128]{2,1,0:T(8,128)S(1)} %get-tuple-element.68), channel_id=1, source_target_pairs={{0,24},{2,26},{4,28},{6,30},{8,0},{10,2},{12,4},{14,6},{16,8},{18,... | collective-permute-start | bytes 196616 | tf_op jit(solution)/shard_map/ppermute | solution.py:342
  39.6 0.0 collective-permute-done.3.got2_ref
  39.6 0.0 collective-permute-done.4.got3_ref
  39.6 0.0 copy-done.4
  39.6 0.0 copy-done.6
  39.6 2.0 %shard_map.87 = (bf16[1024,128]{1,0:T(8,128)(2,1)S(1)}, bf16[1024,128]{1,0:T(8,128)(2,1)S(1)}, f32[8,128]{1,0:T(8,128)S(1)}, f32[1024,128]{1,0:T(8,128)S(1)}, f32[4,128,128]{2,1,0:T(8,128)S(1)}) custom-call(bf16[256,512]{1,0:T(8,128)(2,1)S(1)} %get-tuple-element.49.k2_ref, bf16[256,512]{1,0:T(8,128)(2,1)S(1)} %get-tuple-element.50.v2_ref, ...), custom_call_target="tpu_custom_call" | custom-call | flops 99999997952 | tf_op jit(solution)/shard_map/pallas_call | solution.py:376
  41.7 0.2 collective-permute-done.5.w1
  41.9 0.0 collective-permute-done.6.w2
  41.9 0.6 collective-permute-done.7.w3
  42.4 0.7 shard_map.90
  43.2 0.8 collective-permute-start.12
  44.0 2.6 %collective-permute-start.13 = (f32[4,32,128]{2,1,0:T(8,128)S(1)}, f32[4,32,128]{2,1,0:T(8,128)S(1)}, u32[]{:S(2)}, u32[]{:S(2)}) collective-permute-start(f32[4,32,128]{2,1,0:T(8,128)S(1)} %get-tuple-element.79), channel_id=1, source_target_pairs={{0,16},{2,18},{4,20},{6,22},{8,24},{10,26},{12,28},{14,30},{16,0},... | collective-permute-start | bytes 196616 | tf_op jit(solution)/shard_map/ppermute | solution.py:342
  46.7 0.2 collective-permute-start.14
  46.9 0.0 collective-permute-start.8
  46.9 1.8 %collective-permute-start.9 = (f32[128,128]{1,0:T(8,128)S(1)}, f32[128,128]{1,0:T(8,128)S(1)}, u32[]{:S(2)}, u32[]{:S(2)}) collective-permute-start(f32[128,128]{1,0:T(8,128)S(1)} %get-tuple-element.71), channel_id=1, source_target_pairs={{0,4},{2,6},{4,0},{6,2},{8,12},{10,14},{12,8},{14,10},{16,20},{18,... | collective-permute-start | bytes 196616 | tf_op jit(solution)/shard_map/ppermute | solution.py:333
  48.7 0.0 collective-permute-done.12.p1
  48.7 0.9 %collective-permute-start.10 = (f32[128,128]{1,0:T(8,128)S(1)}, f32[128,128]{1,0:T(8,128)S(1)}, u32[]{:S(2)}, u32[]{:S(2)}) collective-permute-start(f32[128,128]{1,0:T(8,128)S(1)} %get-tuple-element.72), channel_id=1, source_target_pairs={{0,6},{2,0},{4,2},{6,4},{8,14},{10,8},{12,10},{14,12},{16,22},{18,... | collective-permute-start | bytes 196616 | tf_op jit(solution)/shard_map/ppermute | solution.py:333
  49.6 0.0 collective-permute-done.13.p2
  49.6 0.1 collective-permute-done.14.p3
  49.8 0.7 shard_map.93
  50.5 3.6 %all-to-all-start.2 = ((f32[8,32,128]{2,1,0:T(8,128)}), f32[8,32,128]{2,1,0:T(8,128)S(1)}, u32[]{:S(2)}, u32[]{:S(2)}) async-start(f32[8,32,128]{2,1,0:T(8,128)} %get-tuple-element.82), calls=%async_computation.2 | async-start | bytes 262144 | tf_op jit(solution)/shard_map/all_to_all | solution.py:392
  54.0 0.0 collective-permute-done.8.b1
  54.0 0.0 collective-permute-done.9.b2
  54.0 0.0 collective-permute-done.10.b3
  54.1 0.0 copy-done.5
  54.1 4.7 %shard_map.91 = (f32[8,128]{1,0:T(8,128)S(1)}, f32[128,1024]{1,0:T(8,128)}, bf16[128,1024]{1,0:T(8,128)(2,1)S(1)}, bf16[256,512]{1,0:T(8,128)(2,1)S(1)}) custom-call(bf16[256,512]{1,0:T(8,128)(2,1)S(1)} %get-tuple-element.51.q2_ref, bf16[256,512]{1,0:T(8,128)(2,1)S(1)} %get-tuple-element.49.k2_ref, bf16[256,512]{1,0:T(8,128)(2,1)S(1)} %get-tuple-element.50.v2_ref, ...), custom_call_target="tpu_custom_call" | custom-call | flops 99999997952 | tf_op jit(solution)/shard_map/pallas_call | solution.py:393
  58.8 2.9 %all-to-all-done.2.got_ref = f32[8,32,128]{2,1,0:T(8,128)S(1)} async-done(((f32[8,32,128]{2,1,0:T(8,128)}), f32[8,32,128]{2,1,0:T(8,128)S(1)}, u32[]{:S(2)}, u32[]{:S(2)}) %all-to-all-start.2) | async-done | bytes 131104 | tf_op jit(solution)/shard_map/all_to_all | solution.py:392
  61.7 0.7 shard_map.94
  62.4 4.7 %all-to-all-start.3 = ((f32[16,32,128]{2,1,0:T(8,128)}), f32[16,32,128]{2,1,0:T(8,128)S(1)}, u32[]{:S(2)}, u32[]{:S(2)}) async-start(f32[16,32,128]{2,1,0:T(8,128)} %shard_map.94), calls=%async_computation.3 | async-start | bytes 524288 | tf_op jit(solution)/shard_map/all_to_all | solution.py:403
  67.1 7.6 %collective-permute-start.11 = (f32[128,1024]{1,0:T(8,128)}, f32[128,1024]{1,0:T(8,128)S(1)}, u32[]{:S(2)}, u32[]{:S(2)}) collective-permute-start(f32[128,1024]{1,0:T(8,128)} %get-tuple-element.74), channel_id=1, source_target_pairs={{0,1},{1,0},{2,3},{3,2},{4,5},{5,4},{6,7},{7,6},{8,9},{9,8},{10,11... | collective-permute-start | bytes 1572872 | tf_op jit(solution)/shard_map/ppermute | solution.py:314
  74.7 1.9 %shard_map.95 = (f32[256,512]{1,0:T(8,128)S(1)}, f32[256,512]{1,0:T(8,128)S(1)}, f32[4,128,128]{2,1,0:T(8,128)S(1)}) custom-call(bf16[256,512]{1,0:T(8,128)(2,1)S(1)} %get-tuple-element.51.q2_ref, bf16[256,512]{1,0:T(8,128)(2,1)S(1)} %get-tuple-element.49.k2_ref, bf16[256,512]{1,0:T(8,128)(2,1)S(1)} %get-tuple-element.50.v2_ref, ...), custom_call_target="tpu_custom_call" | custom-call | tf_op jit(solution)/shard_map/pallas_call | solution.py:400
  76.6 0.0 all-to-all-done.3.later_ref
  76.6 0.3 shard_map.97
  76.9 6.8 %collective-permute-start.15 = (f32[128,1024]{1,0:T(8,128)S(1)}, f32[128,1024]{1,0:T(8,128)S(1)}, u32[]{:S(2)}, u32[]{:S(2)}) collective-permute-start(f32[128,1024]{1,0:T(8,128)S(1)} %shard_map.97), channel_id=1, source_target_pairs={{0,1},{1,0},{2,3},{3,2},{4,5},{5,4},{6,7},{7,6},{8,9},{9,8},{10,11... | collective-permute-start | bytes 1572872 | tf_op jit(solution)/shard_map/ppermute | solution.py:314
  83.7 0.2 shard_map.96.own_ref
  83.9 0.0 collective-permute-done.11.got_ref
  83.9 0.8 shard_map.92
  84.8 0.4 collective-permute-done.15.got_ref
  85.2 0.8 shard_map.98
  (6 shorter events, 0.1 us)
Async XLA Ops:
  1.6 3.4 %copy-start = (bf16[128,1024]{1,0:T(8,128)(2,1)S(1)}, bf16[128,1024]{1,0:T(8,128)(2,1)}, u32[]{:S(2)}) copy-start(bf16[128,1024]{1,0:T(8,128)(2,1)} %q_ref.1) | copy-start | bytes 786436
  1.6 3.4 %copy-start.1 = (bf16[128,1024]{1,0:T(8,128)(2,1)S(1)}, bf16[128,1024]{1,0:T(8,128)(2,1)}, u32[]{:S(2)}) copy-start(bf16[128,1024]{1,0:T(8,128)(2,1)} %dy_ref.1) | copy-start | bytes 786436
  1.7 4.9 %copy-start.2 = (bf16[128,1024]{1,0:T(8,128)(2,1)S(1)}, bf16[128,1024]{1,0:T(8,128)(2,1)}, u32[]{:S(2)}) copy-start(bf16[128,1024]{1,0:T(8,128)(2,1)} %k_ref.1) | copy-start | bytes 786436
  1.7 4.9 %copy-start.3 = (bf16[128,1024]{1,0:T(8,128)(2,1)S(1)}, bf16[128,1024]{1,0:T(8,128)(2,1)}, u32[]{:S(2)}) copy-start(bf16[128,1024]{1,0:T(8,128)(2,1)} %v_ref.1) | copy-start | bytes 786436
  1.7 4.9 %collective-permute-start.1 = (f32[128,1024]{1,0:T(8,128)S(1)}, f32[128,1024]{1,0:T(8,128)S(1)}, u32[]{:S(2)}, u32[]{:S(2)}) collective-permute-start(f32[128,1024]{1,0:T(8,128)S(1)} %maximum_convert_fusion), channel_id=1, source_target_pairs={{0,1},{1,0},{2,3},{3,2},{4,5},{5,4},{6,7},{7,6},{8,9},{9,8},{10,11... | collective-permute-start | bytes 1572872 | tf_op jit(solution)/shard_map/ppermute | solution.py:314
  5.1 7.6 %collective-permute-start = (f32[128,1024]{1,0:T(8,128)S(1)}, f32[128,1024]{1,0:T(8,128)S(1)}, u32[]{:S(2)}, u32[]{:S(2)}) collective-permute-start(f32[128,1024]{1,0:T(8,128)S(1)} %get-tuple-element.47), channel_id=1, source_target_pairs={{0,1},{1,0},{2,3},{3,2},{4,5},{5,4},{6,7},{7,6},{8,9},{9,8},{10,11... | collective-permute-start | bytes 1572872 | tf_op jit(solution)/shard_map/ppermute | solution.py:314
  7.6 13.1 %all-to-all-start = ((f32[16,32,128]{2,1,0:T(8,128)}), f32[16,32,128]{2,1,0:T(8,128)S(1)}, u32[]{:S(2)}, u32[]{:S(2)}) async-start(f32[16,32,128]{2,1,0:T(8,128)} %get-tuple-element.61), calls=%async_computation | async-start | bytes 524288 | tf_op jit(solution)/shard_map/all_to_all | solution.py:368
  13.6 26.0 %copy-start.4 = (bf16[256,512]{1,0:T(8,128)(2,1)}, bf16[256,512]{1,0:T(8,128)(2,1)S(1)}, u32[]{:S(2)}) copy-start(bf16[256,512]{1,0:T(8,128)(2,1)S(1)} %get-tuple-element.52.dy2_ref) | copy-start | bytes 786436
  13.6 24.8 %collective-permute-start.2 = (f32[256,512]{1,0:T(8,128)}, f32[256,512]{1,0:T(8,128)S(1)}, u32[]{:S(2)}, u32[]{:S(2)}) collective-permute-start(f32[256,512]{1,0:T(8,128)} %get-tuple-element.53), channel_id=1, source_target_pairs={{0,2},{2,4},{4,6},{6,0},{8,10},{10,12},{12,14},{14,8},{16,18},{18,... | collective-permute-start | bytes 1572872 | tf_op jit(solution)/shard_map/ppermute | solution.py:333
  15.1 24.6 %collective-permute-start.3 = (f32[256,512]{1,0:T(8,128)S(1)}, f32[256,512]{1,0:T(8,128)S(1)}, u32[]{:S(2)}, u32[]{:S(2)}) collective-permute-start(f32[256,512]{1,0:T(8,128)S(1)} %get-tuple-element.54), channel_id=1, source_target_pairs={{0,4},{2,6},{4,0},{6,2},{8,12},{10,14},{12,8},{14,10},{16,20},{18,... | collective-permute-start | bytes 1572872 | tf_op jit(solution)/shard_map/ppermute | solution.py:333
  17.5 22.2 %collective-permute-start.4 = (f32[256,512]{1,0:T(8,128)S(1)}, f32[256,512]{1,0:T(8,128)}, u32[]{:S(2)}, u32[]{:S(2)}) collective-permute-start(f32[256,512]{1,0:T(8,128)S(1)} %get-tuple-element.55), channel_id=1, source_target_pairs={{0,6},{2,0},{4,2},{6,4},{8,14},{10,8},{12,10},{14,12},{16,22},{18,... | collective-permute-start | bytes 1572872 | tf_op jit(solution)/shard_map/ppermute | solution.py:333
  36.8 5.1 %collective-permute-start.5 = (f32[4,32,128]{2,1,0:T(8,128)S(1)}, f32[4,32,128]{2,1,0:T(8,128)S(1)}, u32[]{:S(2)}, u32[]{:S(2)}) collective-permute-start(f32[4,32,128]{2,1,0:T(8,128)S(1)} %get-tuple-element.66), channel_id=1, source_target_pairs={{0,8},{2,10},{4,12},{6,14},{8,16},{10,18},{12,20},{14,22},{16,24},... | collective-permute-start | bytes 196616 | tf_op jit(solution)/shard_map/ppermute | solution.py:342
  37.1 2.5 %copy-start.6 = (f32[1024]{0:T(1024)S(1)}, f32[1024]{0:T(1024)}, u32[]{:S(2)}) copy-start(f32[1024]{0:T(1024)} %param.8) | copy-start | bytes 12292
  37.1 4.7 %collective-permute-start.6 = (f32[4,32,128]{2,1,0:T(8,128)S(1)}, f32[4,32,128]{2,1,0:T(8,128)S(1)}, u32[]{:S(2)}, u32[]{:S(2)}) collective-permute-start(f32[4,32,128]{2,1,0:T(8,128)S(1)} %get-tuple-element.67), channel_id=1, source_target_pairs={{0,16},{2,18},{4,20},{6,22},{8,24},{10,26},{12,28},{14,30},{16,0},... | collective-permute-start | bytes 196616 | tf_op jit(solution)/shard_map/ppermute | solution.py:342
  38.4 4.1 %collective-permute-start.7 = (f32[4,32,128]{2,1,0:T(8,128)S(1)}, f32[4,32,128]{2,1,0:T(8,128)S(1)}, u32[]{:S(2)}, u32[]{:S(2)}) collective-permute-start(f32[4,32,128]{2,1,0:T(8,128)S(1)} %get-tuple-element.68), channel_id=1, source_target_pairs={{0,24},{2,26},{4,28},{6,30},{8,0},{10,2},{12,4},{14,6},{16,8},{18,... | collective-permute-start | bytes 196616 | tf_op jit(solution)/shard_map/ppermute | solution.py:342
  43.2 5.5 %collective-permute-start.12 = (f32[4,32,128]{2,1,0:T(8,128)S(1)}, f32[4,32,128]{2,1,0:T(8,128)S(1)}, u32[]{:S(2)}, u32[]{:S(2)}) collective-permute-start(f32[4,32,128]{2,1,0:T(8,128)S(1)} %get-tuple-element.78), channel_id=1, source_target_pairs={{0,8},{2,10},{4,12},{6,14},{8,16},{10,18},{12,20},{14,22},{16,24},... | collective-permute-start | bytes 196616 | tf_op jit(solution)/shard_map/ppermute | solution.py:342
  44.0 5.6 %collective-permute-start.13 = (f32[4,32,128]{2,1,0:T(8,128)S(1)}, f32[4,32,128]{2,1,0:T(8,128)S(1)}, u32[]{:S(2)}, u32[]{:S(2)}) collective-permute-start(f32[4,32,128]{2,1,0:T(8,128)S(1)} %get-tuple-element.79), channel_id=1, source_target_pairs={{0,16},{2,18},{4,20},{6,22},{8,24},{10,26},{12,28},{14,30},{16,0},... | collective-permute-start | bytes 196616 | tf_op jit(solution)/shard_map/ppermute | solution.py:342
  46.7 3.1 %collective-permute-start.14 = (f32[4,32,128]{2,1,0:T(8,128)S(1)}, f32[4,32,128]{2,1,0:T(8,128)S(1)}, u32[]{:S(2)}, u32[]{:S(2)}) collective-permute-start(f32[4,32,128]{2,1,0:T(8,128)S(1)} %get-tuple-element.80), channel_id=1, source_target_pairs={{0,24},{2,26},{4,28},{6,30},{8,0},{10,2},{12,4},{14,6},{16,8},{18,... | collective-permute-start | bytes 196616 | tf_op jit(solution)/shard_map/ppermute | solution.py:342
  46.9 7.2 %collective-permute-start.8 = (f32[128,128]{1,0:T(8,128)S(1)}, f32[128,128]{1,0:T(8,128)S(1)}, u32[]{:S(2)}, u32[]{:S(2)}) collective-permute-start(f32[128,128]{1,0:T(8,128)S(1)} %get-tuple-element.70), channel_id=1, source_target_pairs={{0,2},{2,4},{4,6},{6,0},{8,10},{10,12},{12,14},{14,8},{16,18},{18,... | collective-permute-start | bytes 196616 | tf_op jit(solution)/shard_map/ppermute | solution.py:333
  46.9 7.2 %collective-permute-start.9 = (f32[128,128]{1,0:T(8,128)S(1)}, f32[128,128]{1,0:T(8,128)S(1)}, u32[]{:S(2)}, u32[]{:S(2)}) collective-permute-start(f32[128,128]{1,0:T(8,128)S(1)} %get-tuple-element.71), channel_id=1, source_target_pairs={{0,4},{2,6},{4,0},{6,2},{8,12},{10,14},{12,8},{14,10},{16,20},{18,... | collective-permute-start | bytes 196616 | tf_op jit(solution)/shard_map/ppermute | solution.py:333
  48.7 5.4 %collective-permute-start.10 = (f32[128,128]{1,0:T(8,128)S(1)}, f32[128,128]{1,0:T(8,128)S(1)}, u32[]{:S(2)}, u32[]{:S(2)}) collective-permute-start(f32[128,128]{1,0:T(8,128)S(1)} %get-tuple-element.72), channel_id=1, source_target_pairs={{0,6},{2,0},{4,2},{6,4},{8,14},{10,8},{12,10},{14,12},{16,22},{18,... | collective-permute-start | bytes 196616 | tf_op jit(solution)/shard_map/ppermute | solution.py:333
  49.8 4.3 %copy-start.5 = (bf16[256,512]{1,0:T(8,128)(2,1)S(1)}, bf16[256,512]{1,0:T(8,128)(2,1)}, u32[]{:S(2)}) copy-start(bf16[256,512]{1,0:T(8,128)(2,1)} %copy-done.4) | copy-start | bytes 786436
  50.5 11.2 %all-to-all-start.2 = ((f32[8,32,128]{2,1,0:T(8,128)}), f32[8,32,128]{2,1,0:T(8,128)S(1)}, u32[]{:S(2)}, u32[]{:S(2)}) async-start(f32[8,32,128]{2,1,0:T(8,128)} %get-tuple-element.82), calls=%async_computation.2 | async-start | bytes 262144 | tf_op jit(solution)/shard_map/all_to_all | solution.py:392
  62.4 14.2 %all-to-all-start.3 = ((f32[16,32,128]{2,1,0:T(8,128)}), f32[16,32,128]{2,1,0:T(8,128)S(1)}, u32[]{:S(2)}, u32[]{:S(2)}) async-start(f32[16,32,128]{2,1,0:T(8,128)} %shard_map.94), calls=%async_computation.3 | async-start | bytes 524288 | tf_op jit(solution)/shard_map/all_to_all | solution.py:403
  67.1 16.8 %collective-permute-start.11 = (f32[128,1024]{1,0:T(8,128)}, f32[128,1024]{1,0:T(8,128)S(1)}, u32[]{:S(2)}, u32[]{:S(2)}) collective-permute-start(f32[128,1024]{1,0:T(8,128)} %get-tuple-element.74), channel_id=1, source_target_pairs={{0,1},{1,0},{2,3},{3,2},{4,5},{5,4},{6,7},{7,6},{8,9},{9,8},{10,11... | collective-permute-start | bytes 1572872 | tf_op jit(solution)/shard_map/ppermute | solution.py:314
  76.9 8.3 %collective-permute-start.15 = (f32[128,1024]{1,0:T(8,128)S(1)}, f32[128,1024]{1,0:T(8,128)S(1)}, u32[]{:S(2)}, u32[]{:S(2)}) collective-permute-start(f32[128,1024]{1,0:T(8,128)S(1)} %shard_map.97), channel_id=1, source_target_pairs={{0,1},{1,0},{2,3},{3,2},{4,5},{5,4},{6,7},{7,6},{8,9},{9,8},{10,11... | collective-permute-start | bytes 1572872 | tf_op jit(solution)/shard_map/ppermute | solution.py:314

commit v4 on v3

--- a/solution.py
+++ b/solution.py
@@ -194,7 +194,7 @@
 
 def turn_body(
     q_ref, dy_ref, gain_ref, intra_ref, first_ref, w0, w1, w2, w3,
-    p0, p1, p2, p3, b0, b1, b2, b3, before_ref, pairs_ref,
+    p0, p1, p2, p3, before_ref, pairs_ref,
 ):
     for s, ref in enumerate((w0, w1, w2, w3)):
         at = pl.ds(pl.multiple_of(cross(-s) * PIECE, PIECE), PIECE)
@@ -217,11 +217,9 @@
         at = pl.ds(pl.multiple_of(cross(s) * PIECE, PIECE), PIECE)
         for j in range(SIDE):
             ref[j] = pairs_ref[j, at, :]
-    for s, ref in enumerate((b0, b1, b2, b3)):
-        ref[...] = before_ref[line(s)]
-
-
-def gather_body(p0, p1, p2, p3, total_ref, pairs_ref):
+
+
+def gather_body(p0, p1, p2, p3, before_ref, total_ref, pairs_ref, b0, b1, b2, b3):
     total = jnp.zeros(p0.shape[1:], F32)
     for s, ref in enumerate((p0, p1, p2, p3)):
         for j in range(SIDE):
@@ -229,9 +227,11 @@
             total = total + ref[j]
     for g in range(NZ):
         total_ref[g] = total
-
-
-def later_body(pairs_ref, got_ref, _, out_ref):
+    for s, ref in enumerate((b0, b1, b2, b3)):
+        ref[...] = before_ref[line(s)]
+
+
+def later_body(pairs_ref, got_ref, out_ref):
     z = lax.axis_index("z")
     running = jnp.zeros(got_ref.shape[1:], F32)
     for g in range(1, NZ):
@@ -241,11 +241,10 @@
         running = running + pairs_ref[p]
 
 
-def query_body(
+def back_body(
     q2_ref, k2_ref, v2_ref, dy2_ref, gain_ref, b0, b1, b2, b3,
-    mark_ref, send_ref, own_ref, delta_ref, before_ref, all_ref,
+    send_ref, own_ref, gk_ref, gv_ref, second_ref, before_ref, all_ref,
 ):
-    mark(mark_ref)
     mine, _ = halves()
     own, far = rows()
     for s, ref in enumerate((b0, b1, b2, b3)):
@@ -265,26 +264,14 @@
             weights = jnp.where(mask, dot(q, k, NT), 0.0).astype(BF16)
             out = dot(weights, v, NN) + dot(q, before_b, NN)
             normed, delta = deltas(out, dy2_ref[at, head(h)].astype(F32) * gain)
-            delta_ref[at, head(h)] = delta
             all_ref[at, head(h)] = normed * gain
             scores = jnp.where(mask, dot(delta, v, NT), 0.0).astype(BF16)
             all_ref[at, query] = dot(scores, k, NN) + dot(delta, before_b, NT)
-    own_ref[...] = all_ref[own, :].astype(BF16)
-    send_ref[...] = all_ref[far, :].astype(BF16).astype(F32)
-
-
-def keys_body(q2_ref, k2_ref, v2_ref, delta_ref, gk_ref, gv_ref, second_ref):
-    mask = causal()
-    for h in range(HALF):
-        for b in range(2):
-            at = block(b)
-            q, k, v = q2_ref[at, head(h)], k2_ref[at, head(h)], v2_ref[at, head(h)]
-            delta = delta_ref[at, head(h)]
-            weights = jnp.where(mask, dot(q, k, NT), 0.0).astype(BF16)
-            scores = jnp.where(mask, dot(delta, v, NT), 0.0).astype(BF16)
             gk_ref[at, head(h)] = dot(scores, q, TN)
             gv_ref[at, head(h)] = dot(weights, delta, TN)
         second_ref[h] = dot(q, delta, TN)
+    own_ref[...] = all_ref[own, :].astype(BF16)
+    send_ref[...] = all_ref[far, :].astype(BF16).astype(F32)
 
 
 def final_body(mine, k2_ref, v2_ref, later_ref, second_ref, gk_ref, gv_ref, out_ref):
@@ -382,22 +369,21 @@
     total, sums = call(plane_body, [copies, slices], spots=(VM, VM), cost=10**11)(parts, spread_done)
     earlier = lax.all_to_all(total, "z", 0, 0, tiled=True)
     w_own, *w_sends = call(before_body, [some] * SIDE)(sums, earlier)
-    p_own, p1, p2, p3, b_own, *b_sends = call(
-        turn_body,
-        [some] * SIDE + [square] * SIDE,
-        [pltpu.VMEM(*states), pltpu.VMEM(*states)],
+    p_own, p1, p2, p3, before = call(
+        turn_body, [some] * SIDE + [states], [pltpu.VMEM(*states)]
     )(qh, dyh, gain_h, intra_h, first, w_own, *shift_cross(w_sends))
+    total, pairs, b_own, *b_sends = call(gather_body, [copies, slices] + [square] * SIDE)(
+        p_own, *shift_cross((p1, p2, p3)), before
+    )
+    totals = lax.all_to_all(total, "z", 0, 0, tiled=True)
     b_got = shift_line(b_sends)
-    total, pairs = call(gather_body, [copies, slices])(p_own, *shift_cross((p1, p2, p3)))
-    totals = lax.all_to_all(total, "z", 0, 0, tiled=True)
-    query_done, send, own, delta = call(
-        query_body,
-        [MARK, (own_shape, F32), (own_shape, BF16), (pair, BF16)],
+    (later,) = call(later_body, [slices], cost=10**11)(pairs, totals)
+    send, own, gk, gv, second = call(
+        back_body,
+        [(own_shape, F32), (own_shape, BF16), (pair, F32), (pair, F32), states],
         [pltpu.VMEM(*states), pltpu.VMEM((PAIR, 2 * WIDE), F32)],
         cost=10**11,
     )(q2, k2, v2, dy2, gain, b_own, *b_got)
-    (later,) = call(later_body, [slices], spots=(VM,) * 3)(pairs, totals, query_done)
-    gk, gv, second = call(keys_body, [(pair, F32), (pair, F32), states])(q2, k2, v2, delta)
     merge = call(merge_body, [(own_shape, BF16), (own_shape, BF16)])
     attended, grad_query = merge(own, swap(send))
     after = lax.all_to_all(later, ("y", "x"), 0, 0, tiled=True)

time: 86.6 us -> 86.5 us (level)
  starting transfers between devices: 46.2 us -> 40.3 us
  local copies, waits for them, and re-layouts: 1.03 us -> 5.37 us
  waiting for transfers between devices: 6.96 us -> 10 us
  Pallas kernels: 15 us -> 13.3 us
    ppermute x4, starting transfers between devices: 18.6 us -> 12.6 us  [swap(): return lax.ppermute(x, 'core', [(0, 1), (1, 0)])]
    unnamed x14 -> x30, local copies, waits for them, and re-layouts: 0.04 us -> 4.38 us
    ppermute x6, waiting for transfers between devices: 0.91 us -> 3.12 us  [shift_cross(): lax.ppermute(a, AXES, [(device(z, c, i, j), device(z, c, (i + s) % SIDE,...]
    all_to_all x1, waiting for transfers between devices: 2.89 us -> 5.08 us  [per_device(): totals = lax.all_to_all(total, 'z', 0, 0, tiled=True)]
    pallas_call x5 -> x4, Pallas kernels: 8.78 us -> 7.01 us  [the longest x1 4.81 us: per_device(): call(back_body, [(own_shape, F32), (own_shape, BF16), (pair, F32), (pair,...]
    ppermute x6, starting transfers between devices: 6.54 us -> 7.91 us  [shift_cross(): lax.ppermute(a, AXES, [(device(z, c, i, j), device(z, c, (i + s) % SIDE,...]
    all_to_all x1, waiting for transfers between devices: 2.13 us -> 0.8 us  [per_device(): parts = lax.all_to_all(pieces, ('y', 'x'), 0, 0, tiled=True)]
    all_to_all x1, starting transfers between devices: 4.69 us -> 3.66 us  [per_device(): after = lax.all_to_all(later, ('y', 'x'), 0, 0, tiled=True)]
  transfers between devices with their start and end apart: 19 -> 19, of which waited for: 7 -> 8; matrix products, arithmetic and copies ran while one was open for 0% -> 0% of each run, Pallas kernels for 15% -> 13%
where the time goes in v4:
time: 86.5 us; the launch traced here: 85.9 us
  starting transfers between devices  40.3 us (47%)
  blocking collectives  16 us (18%)
  Pallas kernels  13.3 us (15%)
  waiting for transfers between devices  10 us (12%)
  local copies, waits for them, and re-layouts  5.37 us (6%)
  between operations  0.87 us (1%)
    all_to_all x1, blocking collectives, per_device(): earlier = lax.all_to_all(total, 'z', 0, 0, tiled=True)  16 us
    ppermute x4, starting transfers between devices, swap(): return lax.ppermute(x, 'core', [(0, 1), (1, 0)])  12.6 us
    ppermute x6, starting transfers between devices, shift_cross(): lax.ppermute(a, AXES, [(device(z, c, i, j), device(z, c, (i + s) % SIDE,...  7.91 us
    ppermute x6, starting transfers between devices, shift_line(): lax.ppermute(a, AXES, [(device(z, c, i, j), device(z, c, i, (j + s) % SID...  7.69 us
    all_to_all x1, waiting for transfers between devices, per_device(): totals = lax.all_to_all(total, 'z', 0, 0, tiled=True)  5.08 us
    all_to_all x1, starting transfers between devices, per_device(): parts = lax.all_to_all(pieces, ('y', 'x'), 0, 0, tiled=True)  5.02 us
    pallas_call x1, Pallas kernels, per_device(): call(back_body, [(own_shape, F32), (own_shape, BF16), (pair, F32), (pair,...  4.81 us
    unnamed x30, local copies, waits for them, and re-layouts  4.38 us
  transfers between devices with their start and end apart: 19, of which 8 were waited for; matrix products, arithmetic and copies ran while one was open for 0% of the time, Pallas kernels for 13%

profile of v4, /device:TPU:1, one launch (start us, length us, event | category | flops | bytes accessed | tf_op | source)
XLA Modules:
  0.0 85.9 jit_solution(17080858436639327183)
XLA Ops:
  0.6 1.0 %constant_dynamic-slice_fusion = (bf16[128,512]{1,0:T(8,128)(2,1)S(1)}, bf16[128,512]{1,0:T(8,128)(2,1)S(1)}) fusion(bf16[128,1024]{1,0:T(8,128)(2,1)} %v_ref.1, s32[]{:T(128)S(6)} %select_n.4, bf16[128,1024]{1,0:T(8,128)(2,1)} %k_ref.1), kind=kLoop, calls=%fused_computation.1 | loop fusion | bytes 524292 | tf_op jit(solution)/shard_map/dynamic_slice | solution.py:347
  1.6 0.0 copy-start
  1.6 0.0 copy-start.1
  1.7 0.0 copy-start.2
  1.7 0.0 copy-start.3
  1.7 3.3 %collective-permute-start.1 = (f32[128,1024]{1,0:T(8,128)S(1)}, f32[128,1024]{1,0:T(8,128)S(1)}, u32[]{:S(2)}, u32[]{:S(2)}) collective-permute-start(f32[128,1024]{1,0:T(8,128)S(1)} %maximum_convert_fusion), channel_id=1, source_target_pairs={{0,1},{1,0},{2,3},{3,2},{4,5},{5,4},{6,7},{7,6},{8,9},{9,8},{10,11... | collective-permute-start | bytes 1572872 | tf_op jit(solution)/shard_map/ppermute | solution.py:301
  5.1 0.9 %collective-permute-start = (f32[128,1024]{1,0:T(8,128)S(1)}, f32[128,1024]{1,0:T(8,128)S(1)}, u32[]{:S(2)}, u32[]{:S(2)}) collective-permute-start(f32[128,1024]{1,0:T(8,128)S(1)} %get-tuple-element.46), channel_id=1, source_target_pairs={{0,1},{1,0},{2,3},{3,2},{4,5},{5,4},{6,7},{7,6},{8,9},{9,8},{10,11... | collective-permute-start | bytes 1572872 | tf_op jit(solution)/shard_map/ppermute | solution.py:301
  6.0 0.6 collective-permute-done.1.got_ref
  6.6 1.0 %shard_map.85 = (bf16[256,512]{1,0:T(8,128)(2,1)S(1)}, bf16[256,512]{1,0:T(8,128)(2,1)S(1)}, f32[16,32,128]{2,1,0:T(8,128)}) custom-call(bf16[128,1024]{1,0:T(8,128)(2,1)S(1)} %copy-done.2, bf16[128,1024]{1,0:T(8,128)(2,1)S(1)} %copy-done.3, f32[128,1024]{1,0:T(8,128)S(1)} %collective-permute-done.1.got_ref, f32[8,128]{1,0:T(8,128)S(1)} %get-tuple-element.47._), custom_call_target="tpu_custom_call" | custom-call | tf_op jit(solution)/shard_map/pallas_call | solution.py:352
  7.6 5.0 %all-to-all-start = ((f32[16,32,128]{2,1,0:T(8,128)}), f32[16,32,128]{2,1,0:T(8,128)S(1)}, u32[]{:S(2)}, u32[]{:S(2)}) async-start(f32[16,32,128]{2,1,0:T(8,128)} %get-tuple-element.60), calls=%async_computation | async-start | bytes 524288 | tf_op jit(solution)/shard_map/all_to_all | solution.py:355
  12.7 0.0 collective-permute-done.got_ref
  12.7 1.0 %shard_map.86 = (bf16[256,512]{1,0:T(8,128)(2,1)S(1)}, bf16[256,512]{1,0:T(8,128)(2,1)S(1)}, f32[8,128]{1,0:T(8,128)S(1)}, f32[256,512]{1,0:T(8,128)}, f32[256,512]{1,0:T(8,128)S(1)}, /*index=5*/f32[256,512]{1,0:T(8,128)S(1)}) custom-call(bf16[128,1024]{1,0:T(8,128)(2,1)S(1)} %copy-done, bf16[128,1024]{1,0:T(8,128)(2,1)S(1)} %copy-done.1, ...), custom_call_target="tpu_custom_call" | custom-call | tf_op jit(solution)/shard_map/pallas_call | solution.py:356
  13.6 0.0 copy-start.4
  13.6 0.7 copy-done.4
  14.3 0.7 copy-done.7
  15.0 1.4 %collective-permute-start.2 = (f32[256,512]{1,0:T(8,128)}, f32[256,512]{1,0:T(8,128)S(1)}, u32[]{:S(2)}, u32[]{:S(2)}) collective-permute-start(f32[256,512]{1,0:T(8,128)} %get-tuple-element.52), channel_id=1, source_target_pairs={{0,2},{2,4},{4,6},{6,0},{8,10},{10,12},{12,14},{14,8},{16,18},{18,... | collective-permute-start | bytes 1572872 | tf_op jit(solution)/shard_map/ppermute | solution.py:320
  16.4 2.4 %collective-permute-start.3 = (f32[256,512]{1,0:T(8,128)S(1)}, f32[256,512]{1,0:T(8,128)S(1)}, u32[]{:S(2)}, u32[]{:S(2)}) collective-permute-start(f32[256,512]{1,0:T(8,128)S(1)} %get-tuple-element.53), channel_id=1, source_target_pairs={{0,4},{2,6},{4,0},{6,2},{8,12},{10,14},{12,8},{14,10},{16,20},{18,... | collective-permute-start | bytes 1572872 | tf_op jit(solution)/shard_map/ppermute | solution.py:320
  18.8 1.2 %collective-permute-start.4 = (f32[256,512]{1,0:T(8,128)S(1)}, f32[256,512]{1,0:T(8,128)}, u32[]{:S(2)}, u32[]{:S(2)}) collective-permute-start(f32[256,512]{1,0:T(8,128)S(1)} %get-tuple-element.54), channel_id=1, source_target_pairs={{0,6},{2,0},{4,2},{6,4},{8,14},{10,8},{12,10},{14,12},{16,22},{18,... | collective-permute-start | bytes 1572872 | tf_op jit(solution)/shard_map/ppermute | solution.py:320
  20.0 0.8 all-to-all-done.parts_ref
  20.8 0.0 copy-start.8
  20.8 16.0 %all_to_all.20.got_ref = f32[8,32,128]{2,1,0:T(8,128)S(1)} all-to-all(f32[8,32,128]{2,1,0:T(8,128)S(1)} %get-tuple-element.63), channel_id=1, replica_groups=mesh['z'=8,'y'=4,'x'=4,'core'=2] {'z'}, dimensions={0} | all-to-all | bytes 262144 | tf_op jit(solution)/shard_map/all_to_all | solution.py:370
  36.9 0.5 collective-permute-start.5
  37.4 2.3 %collective-permute-start.6 = (f32[4,32,128]{2,1,0:T(8,128)S(1)}, f32[4,32,128]{2,1,0:T(8,128)S(1)}, u32[]{:S(2)}, u32[]{:S(2)}) collective-permute-start(f32[4,32,128]{2,1,0:T(8,128)S(1)} %get-tuple-element.66), channel_id=1, source_target_pairs={{0,16},{2,18},{4,20},{6,22},{8,24},{10,26},{12,28},{14,30},{16,0},... | collective-permute-start | bytes 196616 | tf_op jit(solution)/shard_map/ppermute | solution.py:329
  39.6 0.0 collective-permute-done.2.got1_ref
  39.6 1.4 %collective-permute-start.7 = (f32[4,32,128]{2,1,0:T(8,128)S(1)}, f32[4,32,128]{2,1,0:T(8,128)S(1)}, u32[]{:S(2)}, u32[]{:S(2)}) collective-permute-start(f32[4,32,128]{2,1,0:T(8,128)S(1)} %get-tuple-element.67), channel_id=1, source_target_pairs={{0,24},{2,26},{4,28},{6,30},{8,0},{10,2},{12,4},{14,6},{16,8},{18,... | collective-permute-start | bytes 196616 | tf_op jit(solution)/shard_map/ppermute | solution.py:329
  41.0 0.0 collective-permute-done.3.got2_ref
  41.0 0.0 collective-permute-done.4.got3_ref
  41.1 2.0 %shard_map.87 = (bf16[1024,128]{1,0:T(8,128)(2,1)S(1)}, bf16[1024,128]{1,0:T(8,128)(2,1)S(1)}, f32[8,128]{1,0:T(8,128)S(1)}, f32[1024,128]{1,0:T(8,128)S(1)}, f32[4,128,128]{2,1,0:T(8,128)S(1)}) custom-call(bf16[256,512]{1,0:T(8,128)(2,1)S(1)} %get-tuple-element.48.k2_ref, bf16[256,512]{1,0:T(8,128)(2,1)S(1)} %get-tuple-element.49.v2_ref, ...), custom_call_target="tpu_custom_call" | custom-call | flops 99999997952 | tf_op jit(solution)/shard_map/pallas_call | solution.py:363
  43.1 0.0 collective-permute-done.5.w1
  43.1 0.0 collective-permute-done.6.w2
  43.1 0.0 collective-permute-done.7.w3
  43.1 0.7 shard_map.90
  43.9 0.9 %collective-permute-start.8 = (f32[4,32,128]{2,1,0:T(8,128)S(1)}, f32[4,32,128]{2,1,0:T(8,128)S(1)}, u32[]{:S(2)}, u32[]{:S(2)}) collective-permute-start(f32[4,32,128]{2,1,0:T(8,128)S(1)} %get-tuple-element.69), channel_id=1, source_target_pairs={{0,8},{2,10},{4,12},{6,14},{8,16},{10,18},{12,20},{14,22},{16,24},... | collective-permute-start | bytes 196616 | tf_op jit(solution)/shard_map/ppermute | solution.py:329
  44.8 2.9 %collective-permute-start.9 = (f32[4,32,128]{2,1,0:T(8,128)S(1)}, f32[4,32,128]{2,1,0:T(8,128)S(1)}, u32[]{:S(2)}, u32[]{:S(2)}) collective-permute-start(f32[4,32,128]{2,1,0:T(8,128)S(1)} %get-tuple-element.70), channel_id=1, source_target_pairs={{0,16},{2,18},{4,20},{6,22},{8,24},{10,26},{12,28},{14,30},{16,0},... | collective-permute-start | bytes 196616 | tf_op jit(solution)/shard_map/ppermute | solution.py:329
  47.7 0.0 collective-permute-start.10
  47.7 0.6 collective-permute-done.8.p1
  48.3 1.7 %collective-permute-done.9.p2 = f32[4,32,128]{2,1,0:T(8,128)S(1)} collective-permute-done((f32[4,32,128]{2,1,0:T(8,128)S(1)}, f32[4,32,128]{2,1,0:T(8,128)S(1)}, u32[]{:S(2)}, u32[]{:S(2)}) %collective-permute-start.9) | collective-permute-done | bytes 65568 | tf_op jit(solution)/shard_map/ppermute | solution.py:329
  50.0 0.8 collective-permute-done.10.p3
  50.8 0.7 shard_map.91
  51.5 3.4 %all-to-all-start.2 = ((f32[8,32,128]{2,1,0:T(8,128)}), f32[8,32,128]{2,1,0:T(8,128)S(1)}, u32[]{:S(2)}, u32[]{:S(2)}) async-start(f32[8,32,128]{2,1,0:T(8,128)} %get-tuple-element.82), calls=%async_computation.2 | async-start | bytes 262144 | tf_op jit(solution)/shard_map/all_to_all | solution.py:378
  54.9 0.1 collective-permute-start.11
  55.0 1.1 %collective-permute-start.12 = (f32[128,128]{1,0:T(8,128)S(1)}, f32[128,128]{1,0:T(8,128)S(1)}, u32[]{:S(2)}, u32[]{:S(2)}) collective-permute-start(f32[128,128]{1,0:T(8,128)S(1)} %get-tuple-element.75), channel_id=1, source_target_pairs={{0,4},{2,6},{4,0},{6,2},{8,12},{10,14},{12,8},{14,10},{16,20},{18,... | collective-permute-start | bytes 196616 | tf_op jit(solution)/shard_map/ppermute | solution.py:320
  56.1 1.5 %collective-permute-start.13 = (f32[128,128]{1,0:T(8,128)S(1)}, f32[128,128]{1,0:T(8,128)S(1)}, u32[]{:S(2)}, u32[]{:S(2)}) collective-permute-start(f32[128,128]{1,0:T(8,128)S(1)} %get-tuple-element.76), channel_id=1, source_target_pairs={{0,6},{2,0},{4,2},{6,4},{8,14},{10,8},{12,10},{14,12},{16,22},{18,... | collective-permute-start | bytes 196616 | tf_op jit(solution)/shard_map/ppermute | solution.py:320
  57.6 5.1 %all-to-all-done.2.got_ref = f32[8,32,128]{2,1,0:T(8,128)S(1)} async-done(((f32[8,32,128]{2,1,0:T(8,128)}), f32[8,32,128]{2,1,0:T(8,128)S(1)}, u32[]{:S(2)}, u32[]{:S(2)}) %all-to-all-start.2) | async-done | bytes 131104 | tf_op jit(solution)/shard_map/all_to_all | solution.py:378
  62.7 0.7 shard_map.94
  63.4 3.7 %all-to-all-start.3 = ((f32[16,32,128]{2,1,0:T(8,128)}), f32[16,32,128]{2,1,0:T(8,128)S(1)}, u32[]{:S(2)}, u32[]{:S(2)}) async-start(f32[16,32,128]{2,1,0:T(8,128)} %shard_map.94), calls=%async_computation.3 | async-start | bytes 524288 | tf_op jit(solution)/shard_map/all_to_all | solution.py:389
  67.1 0.0 collective-permute-done.11.b1
  67.1 0.0 collective-permute-done.12.b2
  67.1 0.0 copy-start.10
  67.1 0.6 copy-done.10
  67.8 0.0 collective-permute-done.13.b3
  67.8 0.6 copy-done.12
  68.4 0.8 copy-done.11
  69.3 0.8 copy-done.13
  70.1 4.8 %shard_map.92 = (f32[128,1024]{1,0:T(8,128)S(1)}, bf16[128,1024]{1,0:T(8,128)(2,1)S(1)}, f32[256,512]{1,0:T(8,128)S(1)}, f32[256,512]{1,0:T(8,128)S(1)}, f32[4,128,128]{2,1,0:T(8,128)S(1)}) custom-call(bf16[256,512]{1,0:T(8,128)(2,1)S(1)} %copy-done.6, bf16[256,512]{1,0:T(8,128)(2,1)S(1)} %get-tuple-element.48.k2_ref, ...), custom_call_target="tpu_custom_call" | custom-call | flops 99999997952 | tf_op jit(solution)/shard_map/pallas_call | solution.py:381
  74.9 7.5 %collective-permute-start.14 = (f32[128,1024]{1,0:T(8,128)S(1)}, f32[128,1024]{1,0:T(8,128)S(1)}, u32[]{:S(2)}, u32[]{:S(2)}) collective-permute-start(f32[128,1024]{1,0:T(8,128)S(1)} %get-tuple-element.78), channel_id=1, source_target_pairs={{0,1},{1,0},{2,3},{3,2},{4,5},{5,4},{6,7},{7,6},{8,9},{9,8},{10,11... | collective-permute-start | bytes 1572872 | tf_op jit(solution)/shard_map/ppermute | solution.py:301
  82.4 0.0 all-to-all-done.3.later_ref
  82.4 0.2 shard_map.96
  82.7 0.9 %collective-permute-start.15 = (f32[128,1024]{1,0:T(8,128)S(1)}, f32[128,1024]{1,0:T(8,128)S(1)}, u32[]{:S(2)}, u32[]{:S(2)}) collective-permute-start(f32[128,1024]{1,0:T(8,128)S(1)} %shard_map.96), channel_id=1, source_target_pairs={{0,1},{1,0},{2,3},{3,2},{4,5},{5,4},{6,7},{7,6},{8,9},{9,8},{10,11... | collective-permute-start | bytes 1572872 | tf_op jit(solution)/shard_map/ppermute | solution.py:301
  83.5 0.2 shard_map.95.own_ref
  83.8 0.2 collective-permute-done.14.got_ref
  83.9 0.8 shard_map.93
  84.8 0.3 collective-permute-done.15.got_ref
  85.1 0.8 shard_map.97
  (21 shorter events, 0.2 us)
Async XLA Ops:
  1.6 3.4 %copy-start = (bf16[128,1024]{1,0:T(8,128)(2,1)S(1)}, bf16[128,1024]{1,0:T(8,128)(2,1)}, u32[]{:S(2)}) copy-start(bf16[128,1024]{1,0:T(8,128)(2,1)} %q_ref.1) | copy-start | bytes 786436
  1.6 3.4 %copy-start.1 = (bf16[128,1024]{1,0:T(8,128)(2,1)S(1)}, bf16[128,1024]{1,0:T(8,128)(2,1)}, u32[]{:S(2)}) copy-start(bf16[128,1024]{1,0:T(8,128)(2,1)} %dy_ref.1) | copy-start | bytes 786436
  1.7 4.9 %copy-start.2 = (bf16[128,1024]{1,0:T(8,128)(2,1)S(1)}, bf16[128,1024]{1,0:T(8,128)(2,1)}, u32[]{:S(2)}) copy-start(bf16[128,1024]{1,0:T(8,128)(2,1)} %k_ref.1) | copy-start | bytes 786436
  1.7 4.9 %copy-start.3 = (bf16[128,1024]{1,0:T(8,128)(2,1)S(1)}, bf16[128,1024]{1,0:T(8,128)(2,1)}, u32[]{:S(2)}) copy-start(bf16[128,1024]{1,0:T(8,128)(2,1)} %v_ref.1) | copy-start | bytes 786436
  1.7 4.9 %collective-permute-start.1 = (f32[128,1024]{1,0:T(8,128)S(1)}, f32[128,1024]{1,0:T(8,128)S(1)}, u32[]{:S(2)}, u32[]{:S(2)}) collective-permute-start(f32[128,1024]{1,0:T(8,128)S(1)} %maximum_convert_fusion), channel_id=1, source_target_pairs={{0,1},{1,0},{2,3},{3,2},{4,5},{5,4},{6,7},{7,6},{8,9},{9,8},{10,11... | collective-permute-start | bytes 1572872 | tf_op jit(solution)/shard_map/ppermute | solution.py:301
  5.1 7.5 %collective-permute-start = (f32[128,1024]{1,0:T(8,128)S(1)}, f32[128,1024]{1,0:T(8,128)S(1)}, u32[]{:S(2)}, u32[]{:S(2)}) collective-permute-start(f32[128,1024]{1,0:T(8,128)S(1)} %get-tuple-element.46), channel_id=1, source_target_pairs={{0,1},{1,0},{2,3},{3,2},{4,5},{5,4},{6,7},{7,6},{8,9},{9,8},{10,11... | collective-permute-start | bytes 1572872 | tf_op jit(solution)/shard_map/ppermute | solution.py:301
  7.6 13.1 %all-to-all-start = ((f32[16,32,128]{2,1,0:T(8,128)}), f32[16,32,128]{2,1,0:T(8,128)S(1)}, u32[]{:S(2)}, u32[]{:S(2)}) async-start(f32[16,32,128]{2,1,0:T(8,128)} %get-tuple-element.60), calls=%async_computation | async-start | bytes 524288 | tf_op jit(solution)/shard_map/all_to_all | solution.py:355
  13.6 0.7 copy-start.4
  14.3 0.7 copy-start.7
  15.0 24.6 %collective-permute-start.2 = (f32[256,512]{1,0:T(8,128)}, f32[256,512]{1,0:T(8,128)S(1)}, u32[]{:S(2)}, u32[]{:S(2)}) collective-permute-start(f32[256,512]{1,0:T(8,128)} %get-tuple-element.52), channel_id=1, source_target_pairs={{0,2},{2,4},{4,6},{6,0},{8,10},{10,12},{12,14},{14,8},{16,18},{18,... | collective-permute-start | bytes 1572872 | tf_op jit(solution)/shard_map/ppermute | solution.py:320
  16.4 24.6 %collective-permute-start.3 = (f32[256,512]{1,0:T(8,128)S(1)}, f32[256,512]{1,0:T(8,128)S(1)}, u32[]{:S(2)}, u32[]{:S(2)}) collective-permute-start(f32[256,512]{1,0:T(8,128)S(1)} %get-tuple-element.53), channel_id=1, source_target_pairs={{0,4},{2,6},{4,0},{6,2},{8,12},{10,14},{12,8},{14,10},{16,20},{18,... | collective-permute-start | bytes 1572872 | tf_op jit(solution)/shard_map/ppermute | solution.py:320
  18.8 22.2 %collective-permute-start.4 = (f32[256,512]{1,0:T(8,128)S(1)}, f32[256,512]{1,0:T(8,128)}, u32[]{:S(2)}, u32[]{:S(2)}) collective-permute-start(f32[256,512]{1,0:T(8,128)S(1)} %get-tuple-element.54), channel_id=1, source_target_pairs={{0,6},{2,0},{4,2},{6,4},{8,14},{10,8},{12,10},{14,12},{16,22},{18,... | collective-permute-start | bytes 1572872 | tf_op jit(solution)/shard_map/ppermute | solution.py:320
  20.8 20.2 %copy-start.8 = (bf16[256,512]{1,0:T(8,128)(2,1)S(1)}, bf16[256,512]{1,0:T(8,128)(2,1)}, u32[]{:S(2)}) copy-start(bf16[256,512]{1,0:T(8,128)(2,1)} %copy-done.7) | copy-start | bytes 786436
  36.9 4.2 %copy-start.5 = (bf16[256,512]{1,0:T(8,128)(2,1)S(1)}, bf16[256,512]{1,0:T(8,128)(2,1)}, u32[]{:S(2)}) copy-start(bf16[256,512]{1,0:T(8,128)(2,1)} %copy-done.4) | copy-start | bytes 786436
  36.9 6.2 %collective-permute-start.5 = (f32[4,32,128]{2,1,0:T(8,128)S(1)}, f32[4,32,128]{2,1,0:T(8,128)S(1)}, u32[]{:S(2)}, u32[]{:S(2)}) collective-permute-start(f32[4,32,128]{2,1,0:T(8,128)S(1)} %get-tuple-element.65), channel_id=1, source_target_pairs={{0,8},{2,10},{4,12},{6,14},{8,16},{10,18},{12,20},{14,22},{16,24},... | collective-permute-start | bytes 196616 | tf_op jit(solution)/shard_map/ppermute | solution.py:329
  37.4 3.7 %copy-start.14 = (f32[1024]{0:T(1024)S(1)}, f32[1024]{0:T(1024)}, u32[]{:S(2)}) copy-start(f32[1024]{0:T(1024)} %param.8) | copy-start | bytes 12292
  37.4 5.7 %collective-permute-start.6 = (f32[4,32,128]{2,1,0:T(8,128)S(1)}, f32[4,32,128]{2,1,0:T(8,128)S(1)}, u32[]{:S(2)}, u32[]{:S(2)}) collective-permute-start(f32[4,32,128]{2,1,0:T(8,128)S(1)} %get-tuple-element.66), channel_id=1, source_target_pairs={{0,16},{2,18},{4,20},{6,22},{8,24},{10,26},{12,28},{14,30},{16,0},... | collective-permute-start | bytes 196616 | tf_op jit(solution)/shard_map/ppermute | solution.py:329
  39.6 3.5 %collective-permute-start.7 = (f32[4,32,128]{2,1,0:T(8,128)S(1)}, f32[4,32,128]{2,1,0:T(8,128)S(1)}, u32[]{:S(2)}, u32[]{:S(2)}) collective-permute-start(f32[4,32,128]{2,1,0:T(8,128)S(1)} %get-tuple-element.67), channel_id=1, source_target_pairs={{0,24},{2,26},{4,28},{6,30},{8,0},{10,2},{12,4},{14,6},{16,8},{18,... | collective-permute-start | bytes 196616 | tf_op jit(solution)/shard_map/ppermute | solution.py:329
  43.9 4.4 %collective-permute-start.8 = (f32[4,32,128]{2,1,0:T(8,128)S(1)}, f32[4,32,128]{2,1,0:T(8,128)S(1)}, u32[]{:S(2)}, u32[]{:S(2)}) collective-permute-start(f32[4,32,128]{2,1,0:T(8,128)S(1)} %get-tuple-element.69), channel_id=1, source_target_pairs={{0,8},{2,10},{4,12},{6,14},{8,16},{10,18},{12,20},{14,22},{16,24},... | collective-permute-start | bytes 196616 | tf_op jit(solution)/shard_map/ppermute | solution.py:329
  44.8 5.2 %collective-permute-start.9 = (f32[4,32,128]{2,1,0:T(8,128)S(1)}, f32[4,32,128]{2,1,0:T(8,128)S(1)}, u32[]{:S(2)}, u32[]{:S(2)}) collective-permute-start(f32[4,32,128]{2,1,0:T(8,128)S(1)} %get-tuple-element.70), channel_id=1, source_target_pairs={{0,16},{2,18},{4,20},{6,22},{8,24},{10,26},{12,28},{14,30},{16,0},... | collective-permute-start | bytes 196616 | tf_op jit(solution)/shard_map/ppermute | solution.py:329
  47.7 3.1 %collective-permute-start.10 = (f32[4,32,128]{2,1,0:T(8,128)S(1)}, f32[4,32,128]{2,1,0:T(8,128)S(1)}, u32[]{:S(2)}, u32[]{:S(2)}) collective-permute-start(f32[4,32,128]{2,1,0:T(8,128)S(1)} %get-tuple-element.71), channel_id=1, source_target_pairs={{0,24},{2,26},{4,28},{6,30},{8,0},{10,2},{12,4},{14,6},{16,8},{18,... | collective-permute-start | bytes 196616 | tf_op jit(solution)/shard_map/ppermute | solution.py:329
  51.5 11.2 %all-to-all-start.2 = ((f32[8,32,128]{2,1,0:T(8,128)}), f32[8,32,128]{2,1,0:T(8,128)S(1)}, u32[]{:S(2)}, u32[]{:S(2)}) async-start(f32[8,32,128]{2,1,0:T(8,128)} %get-tuple-element.82), calls=%async_computation.2 | async-start | bytes 262144 | tf_op jit(solution)/shard_map/all_to_all | solution.py:378
  54.9 12.3 %collective-permute-start.11 = (f32[128,128]{1,0:T(8,128)S(1)}, f32[128,128]{1,0:T(8,128)S(1)}, u32[]{:S(2)}, u32[]{:S(2)}) collective-permute-start(f32[128,128]{1,0:T(8,128)S(1)} %get-tuple-element.74), channel_id=1, source_target_pairs={{0,2},{2,4},{4,6},{6,0},{8,10},{10,12},{12,14},{14,8},{16,18},{18,... | collective-permute-start | bytes 196616 | tf_op jit(solution)/shard_map/ppermute | solution.py:320
  55.0 12.1 %collective-permute-start.12 = (f32[128,128]{1,0:T(8,128)S(1)}, f32[128,128]{1,0:T(8,128)S(1)}, u32[]{:S(2)}, u32[]{:S(2)}) collective-permute-start(f32[128,128]{1,0:T(8,128)S(1)} %get-tuple-element.75), channel_id=1, source_target_pairs={{0,4},{2,6},{4,0},{6,2},{8,12},{10,14},{12,8},{14,10},{16,20},{18,... | collective-permute-start | bytes 196616 | tf_op jit(solution)/shard_map/ppermute | solution.py:320
  56.1 11.6 %collective-permute-start.13 = (f32[128,128]{1,0:T(8,128)S(1)}, f32[128,128]{1,0:T(8,128)S(1)}, u32[]{:S(2)}, u32[]{:S(2)}) collective-permute-start(f32[128,128]{1,0:T(8,128)S(1)} %get-tuple-element.76), channel_id=1, source_target_pairs={{0,6},{2,0},{4,2},{6,4},{8,14},{10,8},{12,10},{14,12},{16,22},{18,... | collective-permute-start | bytes 196616 | tf_op jit(solution)/shard_map/ppermute | solution.py:320
  63.4 5.0 %copy-start.6 = (bf16[256,512]{1,0:T(8,128)(2,1)S(1)}, bf16[256,512]{1,0:T(8,128)(2,1)}, u32[]{:S(2)}) copy-start(bf16[256,512]{1,0:T(8,128)(2,1)} %copy-done.4) | copy-start | bytes 786436
  63.4 5.0 %copy-start.9 = (bf16[256,512]{1,0:T(8,128)(2,1)S(1)}, bf16[256,512]{1,0:T(8,128)(2,1)}, u32[]{:S(2)}) copy-start(bf16[256,512]{1,0:T(8,128)(2,1)} %copy-done.7) | copy-start | bytes 786436
  63.4 19.0 %all-to-all-start.3 = ((f32[16,32,128]{2,1,0:T(8,128)}), f32[16,32,128]{2,1,0:T(8,128)S(1)}, u32[]{:S(2)}, u32[]{:S(2)}) async-start(f32[16,32,128]{2,1,0:T(8,128)} %shard_map.94), calls=%async_computation.3 | async-start | bytes 524288 | tf_op jit(solution)/shard_map/all_to_all | solution.py:389
  67.1 0.6 copy-start.10
  67.8 0.6 copy-start.12
  68.4 0.8 copy-start.11
  69.2 0.8 copy-start.13
  74.9 9.0 %collective-permute-start.14 = (f32[128,1024]{1,0:T(8,128)S(1)}, f32[128,1024]{1,0:T(8,128)S(1)}, u32[]{:S(2)}, u32[]{:S(2)}) collective-permute-start(f32[128,1024]{1,0:T(8,128)S(1)} %get-tuple-element.78), channel_id=1, source_target_pairs={{0,1},{1,0},{2,3},{3,2},{4,5},{5,4},{6,7},{7,6},{8,9},{9,8},{10,11... | collective-permute-start | bytes 1572872 | tf_op jit(solution)/shard_map/ppermute | solution.py:301
  82.7 2.4 %collective-permute-start.15 = (f32[128,1024]{1,0:T(8,128)S(1)}, f32[128,1024]{1,0:T(8,128)S(1)}, u32[]{:S(2)}, u32[]{:S(2)}) collective-permute-start(f32[128,1024]{1,0:T(8,128)S(1)} %shard_map.96), channel_id=1, source_target_pairs={{0,1},{1,0},{2,3},{3,2},{4,5},{5,4},{6,7},{7,6},{8,9},{9,8},{10,11... | collective-permute-start | bytes 1572872 | tf_op jit(solution)/shard_map/ppermute | solution.py:301

commit v5 on v4

--- a/solution.py
+++ b/solution.py
@@ -241,9 +241,9 @@
         running = running + pairs_ref[p]
 
 
-def back_body(
+def query_body(
     q2_ref, k2_ref, v2_ref, dy2_ref, gain_ref, b0, b1, b2, b3,
-    send_ref, own_ref, gk_ref, gv_ref, second_ref, before_ref, all_ref,
+    send_ref, own_ref, delta_ref, before_ref, all_ref,
 ):
     mine, _ = halves()
     own, far = rows()
@@ -264,14 +264,26 @@
             weights = jnp.where(mask, dot(q, k, NT), 0.0).astype(BF16)
             out = dot(weights, v, NN) + dot(q, before_b, NN)
             normed, delta = deltas(out, dy2_ref[at, head(h)].astype(F32) * gain)
+            delta_ref[at, head(h)] = delta
             all_ref[at, head(h)] = normed * gain
             scores = jnp.where(mask, dot(delta, v, NT), 0.0).astype(BF16)
             all_ref[at, query] = dot(scores, k, NN) + dot(delta, before_b, NT)
+    own_ref[...] = all_ref[own, :].astype(BF16)
+    send_ref[...] = all_ref[far, :].astype(BF16).astype(F32)
+
+
+def keys_body(q2_ref, k2_ref, v2_ref, delta_ref, gk_ref, gv_ref, second_ref):
+    mask = causal()
+    for h in range(HALF):
+        for b in range(2):
+            at = block(b)
+            q, k, v = q2_ref[at, head(h)], k2_ref[at, head(h)], v2_ref[at, head(h)]
+            delta = delta_ref[at, head(h)]
+            weights = jnp.where(mask, dot(q, k, NT), 0.0).astype(BF16)
+            scores = jnp.where(mask, dot(delta, v, NT), 0.0).astype(BF16)
             gk_ref[at, head(h)] = dot(scores, q, TN)
             gv_ref[at, head(h)] = dot(weights, delta, TN)
         second_ref[h] = dot(q, delta, TN)
-    own_ref[...] = all_ref[own, :].astype(BF16)
-    send_ref[...] = all_ref[far, :].astype(BF16).astype(F32)
 
 
 def final_body(mine, k2_ref, v2_ref, later_ref, second_ref, gk_ref, gv_ref, out_ref):
@@ -378,12 +390,13 @@
     totals = lax.all_to_all(total, "z", 0, 0, tiled=True)
     b_got = shift_line(b_sends)
     (later,) = call(later_body, [slices], cost=10**11)(pairs, totals)
-    send, own, gk, gv, second = call(
-        back_body,
-        [(own_shape, F32), (own_shape, BF16), (pair, F32), (pair, F32), states],
+    send, own, delta = call(
+        query_body,
+        [(own_shape, F32), (own_shape, BF16), (pair, BF16)],
         [pltpu.VMEM(*states), pltpu.VMEM((PAIR, 2 * WIDE), F32)],
         cost=10**11,
     )(q2, k2, v2, dy2, gain, b_own, *b_got)
+    gk, gv, second = call(keys_body, [(pair, F32), (pair, F32), states])(q2, k2, v2, delta)
     merge = call(merge_body, [(own_shape, BF16), (own_shape, BF16)])
     attended, grad_query = merge(own, swap(send))
     after = lax.all_to_all(later, ("y", "x"), 0, 0, tiled=True)

time: 86.5 us -> 85.5 us (0.988)
  local copies, waits for them, and re-layouts: 5.37 us -> 1.02 us
  Pallas kernels: 13.3 us -> 15.1 us
  waiting for transfers between devices: 10 us -> 11.7 us
    unnamed x30 -> x10, local copies, waits for them, and re-layouts: 4.38 us -> 0.03 us
    pallas_call x1 -> x2, Pallas kernels: 4.81 us -> 6.62 us  [the longest x1 4.74 us: per_device(): call(query_body, [(own_shape, F32), (own_shape, BF16), (pair, BF16)], [pl...]
    ppermute x6, starting transfers between devices: 7.91 us -> 6.53 us  [shift_cross(): lax.ppermute(a, AXES, [(device(z, c, i, j), device(z, c, (i + s) % SIDE,...]
    all_to_all x1, waiting for transfers between devices: 0.8 us -> 2.14 us  [per_device(): parts = lax.all_to_all(pieces, ('y', 'x'), 0, 0, tiled=True)]
    ppermute x4, starting transfers between devices: 12.6 us -> 13.8 us  [swap(): return lax.ppermute(x, 'core', [(0, 1), (1, 0)])]
  transfers between devices with their start and end apart: 19 -> 19, of which waited for: 8 -> 9; matrix products, arithmetic and copies ran while one was open for 0% -> 0% of each run, Pallas kernels for 13% -> 15%
where the time goes in v5:
time: 85.5 us; the launch traced here: 85 us
  starting transfers between devices  40.4 us (47%)
  blocking collectives  15.9 us (19%)
  Pallas kernels  15.1 us (18%)
  waiting for transfers between devices  11.7 us (14%)
  local copies, waits for them, and re-layouts  1.02 us (1%)
    all_to_all x1, blocking collectives, per_device(): earlier = lax.all_to_all(total, 'z', 0, 0, tiled=True)  15.9 us
    ppermute x4, starting transfers between devices, swap(): return lax.ppermute(x, 'core', [(0, 1), (1, 0)])  13.8 us
    ppermute x6, starting transfers between devices, shift_line(): lax.ppermute(a, AXES, [(device(z, c, i, j), device(z, c, i, (j + s) % SID...  7.98 us
    ppermute x6, starting transfers between devices, shift_cross(): lax.ppermute(a, AXES, [(device(z, c, i, j), device(z, c, (i + s) % SIDE,...  6.53 us
    all_to_all x1, starting transfers between devices, per_device(): parts = lax.all_to_all(pieces, ('y', 'x'), 0, 0, tiled=True)  5.02 us
    all_to_all x1, waiting for transfers between devices, per_device(): totals = lax.all_to_all(total, 'z', 0, 0, tiled=True)  4.86 us
    pallas_call x1, Pallas kernels, per_device(): call(query_body, [(own_shape, F32), (own_shape, BF16), (pair, BF16)], [pl...  4.74 us
    all_to_all x1, starting transfers between devices, per_device(): after = lax.all_to_all(later, ('y', 'x'), 0, 0, tiled=True)  3.71 us
  transfers between devices with their start and end apart: 19, of which 9 were waited for; matrix products, arithmetic and copies ran while one was open for 0% of the time, Pallas kernels for 15%

profile of v5, /device:TPU:1, one launch (start us, length us, event | category | flops | bytes accessed | tf_op | source)
XLA Modules:
  0.0 85.0 jit_solution(12472598369603245954)
XLA Ops:
  0.6 1.0 %constant_dynamic-slice_fusion = (bf16[128,512]{1,0:T(8,128)(2,1)S(1)}, bf16[128,512]{1,0:T(8,128)(2,1)S(1)}) fusion(bf16[128,1024]{1,0:T(8,128)(2,1)} %v_ref.1, s32[]{:T(128)S(6)} %select_n.4, bf16[128,1024]{1,0:T(8,128)(2,1)} %k_ref.1), kind=kLoop, calls=%fused_computation.1 | loop fusion | bytes 524292 | tf_op jit(solution)/shard_map/dynamic_slice | solution.py:359
  1.6 0.0 copy-start
  1.6 0.0 copy-start.1
  1.7 0.0 copy-start.2
  1.7 0.0 copy-start.3
  1.7 3.3 %collective-permute-start.1 = (f32[128,1024]{1,0:T(8,128)S(1)}, f32[128,1024]{1,0:T(8,128)S(1)}, u32[]{:S(2)}, u32[]{:S(2)}) collective-permute-start(f32[128,1024]{1,0:T(8,128)S(1)} %maximum_convert_fusion), channel_id=1, source_target_pairs={{0,1},{1,0},{2,3},{3,2},{4,5},{5,4},{6,7},{7,6},{8,9},{9,8},{10,11... | collective-permute-start | bytes 1572872 | tf_op jit(solution)/shard_map/ppermute | solution.py:313
  5.1 0.0 copy-done
  5.1 0.0 copy-done.1
  5.1 0.9 %collective-permute-start = (f32[128,1024]{1,0:T(8,128)S(1)}, f32[128,1024]{1,0:T(8,128)S(1)}, u32[]{:S(2)}, u32[]{:S(2)}) collective-permute-start(f32[128,1024]{1,0:T(8,128)S(1)} %get-tuple-element.47), channel_id=1, source_target_pairs={{0,1},{1,0},{2,3},{3,2},{4,5},{5,4},{6,7},{7,6},{8,9},{9,8},{10,11... | collective-permute-start | bytes 1572872 | tf_op jit(solution)/shard_map/ppermute | solution.py:313
  6.0 0.6 collective-permute-done.1.got_ref
  6.6 0.0 copy-done.2
  6.6 0.0 copy-done.3
  6.6 1.0 %shard_map.85 = (bf16[256,512]{1,0:T(8,128)(2,1)S(1)}, bf16[256,512]{1,0:T(8,128)(2,1)S(1)}, f32[16,32,128]{2,1,0:T(8,128)}) custom-call(bf16[128,1024]{1,0:T(8,128)(2,1)S(1)} %copy-done.2, bf16[128,1024]{1,0:T(8,128)(2,1)S(1)} %copy-done.3, f32[128,1024]{1,0:T(8,128)S(1)} %collective-permute-done.1.got_ref, f32[8,128]{1,0:T(8,128)S(1)} %get-tuple-element.48._), custom_call_target="tpu_custom_call" | custom-call | tf_op jit(solution)/shard_map/pallas_call | solution.py:364
  7.6 5.0 %all-to-all-start = ((f32[16,32,128]{2,1,0:T(8,128)}), f32[16,32,128]{2,1,0:T(8,128)S(1)}, u32[]{:S(2)}, u32[]{:S(2)}) async-start(f32[16,32,128]{2,1,0:T(8,128)} %get-tuple-element.61), calls=%async_computation | async-start | bytes 524288 | tf_op jit(solution)/shard_map/all_to_all | solution.py:367
  12.7 0.0 collective-permute-done.got_ref
  12.7 0.9 %shard_map.86 = (bf16[256,512]{1,0:T(8,128)(2,1)S(1)}, bf16[256,512]{1,0:T(8,128)(2,1)S(1)}, f32[8,128]{1,0:T(8,128)S(1)}, f32[256,512]{1,0:T(8,128)}, f32[256,512]{1,0:T(8,128)S(1)}, /*index=5*/f32[256,512]{1,0:T(8,128)S(1)}) custom-call(bf16[128,1024]{1,0:T(8,128)(2,1)S(1)} %copy-done, bf16[128,1024]{1,0:T(8,128)(2,1)S(1)} %copy-done.1, ...), custom_call_target="tpu_custom_call" | custom-call | tf_op jit(solution)/shard_map/pallas_call | solution.py:368
  13.6 1.4 %collective-permute-start.2 = (f32[256,512]{1,0:T(8,128)}, f32[256,512]{1,0:T(8,128)S(1)}, u32[]{:S(2)}, u32[]{:S(2)}) collective-permute-start(f32[256,512]{1,0:T(8,128)} %get-tuple-element.53), channel_id=1, source_target_pairs={{0,2},{2,4},{4,6},{6,0},{8,10},{10,12},{12,14},{14,8},{16,18},{18,... | collective-permute-start | bytes 1572872 | tf_op jit(solution)/shard_map/ppermute | solution.py:332
  15.1 2.4 %collective-permute-start.3 = (f32[256,512]{1,0:T(8,128)S(1)}, f32[256,512]{1,0:T(8,128)S(1)}, u32[]{:S(2)}, u32[]{:S(2)}) collective-permute-start(f32[256,512]{1,0:T(8,128)S(1)} %get-tuple-element.54), channel_id=1, source_target_pairs={{0,4},{2,6},{4,0},{6,2},{8,12},{10,14},{12,8},{14,10},{16,20},{18,... | collective-permute-start | bytes 1572872 | tf_op jit(solution)/shard_map/ppermute | solution.py:332
  17.5 1.2 %collective-permute-start.4 = (f32[256,512]{1,0:T(8,128)S(1)}, f32[256,512]{1,0:T(8,128)}, u32[]{:S(2)}, u32[]{:S(2)}) collective-permute-start(f32[256,512]{1,0:T(8,128)S(1)} %get-tuple-element.55), channel_id=1, source_target_pairs={{0,6},{2,0},{4,2},{6,4},{8,14},{10,8},{12,10},{14,12},{16,22},{18,... | collective-permute-start | bytes 1572872 | tf_op jit(solution)/shard_map/ppermute | solution.py:332
  18.6 2.1 %all-to-all-done.parts_ref = f32[16,32,128]{2,1,0:T(8,128)S(1)} async-done(((f32[16,32,128]{2,1,0:T(8,128)}), f32[16,32,128]{2,1,0:T(8,128)S(1)}, u32[]{:S(2)}, u32[]{:S(2)}) %all-to-all-start) | async-done | bytes 262176 | tf_op jit(solution)/shard_map/all_to_all | solution.py:367
  20.8 15.9 %all_to_all.20.got_ref = f32[8,32,128]{2,1,0:T(8,128)S(1)} all-to-all(f32[8,32,128]{2,1,0:T(8,128)S(1)} %get-tuple-element.64), channel_id=1, replica_groups=mesh['z'=8,'y'=4,'x'=4,'core'=2] {'z'}, dimensions={0} | all-to-all | bytes 262144 | tf_op jit(solution)/shard_map/all_to_all | solution.py:382
  36.8 0.4 collective-permute-start.5
  37.1 0.0 copy-start.4
  37.1 1.3 %collective-permute-start.6 = (f32[4,32,128]{2,1,0:T(8,128)S(1)}, f32[4,32,128]{2,1,0:T(8,128)S(1)}, u32[]{:S(2)}, u32[]{:S(2)}) collective-permute-start(f32[4,32,128]{2,1,0:T(8,128)S(1)} %get-tuple-element.67), channel_id=1, source_target_pairs={{0,16},{2,18},{4,20},{6,22},{8,24},{10,26},{12,28},{14,30},{16,0},... | collective-permute-start | bytes 196616 | tf_op jit(solution)/shard_map/ppermute | solution.py:341
  38.4 0.0 collective-permute-done.2.got1_ref
  38.4 1.2 %collective-permute-start.7 = (f32[4,32,128]{2,1,0:T(8,128)S(1)}, f32[4,32,128]{2,1,0:T(8,128)S(1)}, u32[]{:S(2)}, u32[]{:S(2)}) collective-permute-start(f32[4,32,128]{2,1,0:T(8,128)S(1)} %get-tuple-element.68), channel_id=1, source_target_pairs={{0,24},{2,26},{4,28},{6,30},{8,0},{10,2},{12,4},{14,6},{16,8},{18,... | collective-permute-start | bytes 196616 | tf_op jit(solution)/shard_map/ppermute | solution.py:341
  39.6 0.0 collective-permute-done.3.got2_ref
  39.6 0.0 collective-permute-done.4.got3_ref
  39.6 0.0 copy-done.4
  39.6 2.0 %shard_map.87 = (bf16[1024,128]{1,0:T(8,128)(2,1)S(1)}, bf16[1024,128]{1,0:T(8,128)(2,1)S(1)}, f32[8,128]{1,0:T(8,128)S(1)}, f32[1024,128]{1,0:T(8,128)S(1)}, f32[4,128,128]{2,1,0:T(8,128)S(1)}) custom-call(bf16[256,512]{1,0:T(8,128)(2,1)S(1)} %get-tuple-element.49.k2_ref, bf16[256,512]{1,0:T(8,128)(2,1)S(1)} %get-tuple-element.50.v2_ref, ...), custom_call_target="tpu_custom_call" | custom-call | flops 99999997952 | tf_op jit(solution)/shard_map/pallas_call | solution.py:375
  41.7 0.2 collective-permute-done.5.w1
  41.9 0.0 collective-permute-done.6.w2
  41.9 0.6 collective-permute-done.7.w3
  42.4 0.7 shard_map.90
  43.2 0.8 collective-permute-start.8
  44.0 2.6 %collective-permute-start.9 = (f32[4,32,128]{2,1,0:T(8,128)S(1)}, f32[4,32,128]{2,1,0:T(8,128)S(1)}, u32[]{:S(2)}, u32[]{:S(2)}) collective-permute-start(f32[4,32,128]{2,1,0:T(8,128)S(1)} %get-tuple-element.71), channel_id=1, source_target_pairs={{0,16},{2,18},{4,20},{6,22},{8,24},{10,26},{12,28},{14,30},{16,0},... | collective-permute-start | bytes 196616 | tf_op jit(solution)/shard_map/ppermute | solution.py:341
  46.7 0.2 collective-permute-start.10
  46.9 0.7 collective-permute-done.8.p1
  47.6 1.4 %collective-permute-done.9.p2 = f32[4,32,128]{2,1,0:T(8,128)S(1)} collective-permute-done((f32[4,32,128]{2,1,0:T(8,128)S(1)}, f32[4,32,128]{2,1,0:T(8,128)S(1)}, u32[]{:S(2)}, u32[]{:S(2)}) %collective-permute-start.9) | collective-permute-done | bytes 65568 | tf_op jit(solution)/shard_map/ppermute | solution.py:341
  49.0 0.8 collective-permute-done.10.p3
  49.8 0.7 shard_map.91
  50.5 3.4 %all-to-all-start.2 = ((f32[8,32,128]{2,1,0:T(8,128)}), f32[8,32,128]{2,1,0:T(8,128)S(1)}, u32[]{:S(2)}, u32[]{:S(2)}) async-start(f32[8,32,128]{2,1,0:T(8,128)} %get-tuple-element.83), calls=%async_computation.2 | async-start | bytes 262144 | tf_op jit(solution)/shard_map/all_to_all | solution.py:390
  53.9 0.1 collective-permute-start.11
  54.0 1.8 %collective-permute-start.12 = (f32[128,128]{1,0:T(8,128)S(1)}, f32[128,128]{1,0:T(8,128)S(1)}, u32[]{:S(2)}, u32[]{:S(2)}) collective-permute-start(f32[128,128]{1,0:T(8,128)S(1)} %get-tuple-element.76), channel_id=1, source_target_pairs={{0,4},{2,6},{4,0},{6,2},{8,12},{10,14},{12,8},{14,10},{16,20},{18,... | collective-permute-start | bytes 196616 | tf_op jit(solution)/shard_map/ppermute | solution.py:332
  55.8 1.1 %collective-permute-start.13 = (f32[128,128]{1,0:T(8,128)S(1)}, f32[128,128]{1,0:T(8,128)S(1)}, u32[]{:S(2)}, u32[]{:S(2)}) collective-permute-start(f32[128,128]{1,0:T(8,128)S(1)} %get-tuple-element.77), channel_id=1, source_target_pairs={{0,6},{2,0},{4,2},{6,4},{8,14},{10,8},{12,10},{14,12},{16,22},{18,... | collective-permute-start | bytes 196616 | tf_op jit(solution)/shard_map/ppermute | solution.py:332
  56.8 4.9 %all-to-all-done.2.got_ref = f32[8,32,128]{2,1,0:T(8,128)S(1)} async-done(((f32[8,32,128]{2,1,0:T(8,128)}), f32[8,32,128]{2,1,0:T(8,128)S(1)}, u32[]{:S(2)}, u32[]{:S(2)}) %all-to-all-start.2) | async-done | bytes 131104 | tf_op jit(solution)/shard_map/all_to_all | solution.py:390
  61.7 0.7 shard_map.94
  62.4 3.7 %all-to-all-start.3 = ((f32[16,32,128]{2,1,0:T(8,128)}), f32[16,32,128]{2,1,0:T(8,128)S(1)}, u32[]{:S(2)}, u32[]{:S(2)}) async-start(f32[16,32,128]{2,1,0:T(8,128)} %shard_map.94), calls=%async_computation.3 | async-start | bytes 524288 | tf_op jit(solution)/shard_map/all_to_all | solution.py:402
  66.2 0.0 collective-permute-done.11.b1
  66.2 0.0 collective-permute-done.12.b2
  66.2 0.0 collective-permute-done.13.b3
  66.2 4.7 %shard_map.92 = (f32[128,1024]{1,0:T(8,128)}, bf16[128,1024]{1,0:T(8,128)(2,1)S(1)}, bf16[256,512]{1,0:T(8,128)(2,1)S(1)}) custom-call(bf16[256,512]{1,0:T(8,128)(2,1)S(1)} %get-tuple-element.51.q2_ref, bf16[256,512]{1,0:T(8,128)(2,1)S(1)} %get-tuple-element.49.k2_ref, bf16[256,512]{1,0:T(8,128)(2,1)S(1)} %get-tuple-element.50.v2_ref, ...), custom_call_target="tpu_custom_call" | custom-call | flops 99999997952 | tf_op jit(solution)/shard_map/pallas_call | solution.py:393
  70.9 7.5 %collective-permute-start.14 = (f32[128,1024]{1,0:T(8,128)}, f32[128,1024]{1,0:T(8,128)S(1)}, u32[]{:S(2)}, u32[]{:S(2)}) collective-permute-start(f32[128,1024]{1,0:T(8,128)} %get-tuple-element.79), channel_id=1, source_target_pairs={{0,1},{1,0},{2,3},{3,2},{4,5},{5,4},{6,7},{7,6},{8,9},{9,8},{10,11... | collective-permute-start | bytes 1572872 | tf_op jit(solution)/shard_map/ppermute | solution.py:313
  78.4 1.9 %shard_map.95 = (f32[256,512]{1,0:T(8,128)S(1)}, f32[256,512]{1,0:T(8,128)S(1)}, f32[4,128,128]{2,1,0:T(8,128)S(1)}) custom-call(bf16[256,512]{1,0:T(8,128)(2,1)S(1)} %get-tuple-element.51.q2_ref, bf16[256,512]{1,0:T(8,128)(2,1)S(1)} %get-tuple-element.49.k2_ref, bf16[256,512]{1,0:T(8,128)(2,1)S(1)} %get-tuple-element.50.v2_ref, ...), custom_call_target="tpu_custom_call" | custom-call | tf_op jit(solution)/shard_map/pallas_call | solution.py:399
  80.3 0.0 all-to-all-done.3.later_ref
  80.3 0.3 shard_map.97
  80.6 2.1 %collective-permute-start.15 = (f32[128,1024]{1,0:T(8,128)S(1)}, f32[128,1024]{1,0:T(8,128)S(1)}, u32[]{:S(2)}, u32[]{:S(2)}) collective-permute-start(f32[128,1024]{1,0:T(8,128)S(1)} %shard_map.97), channel_id=1, source_target_pairs={{0,1},{1,0},{2,3},{3,2},{4,5},{5,4},{6,7},{7,6},{8,9},{9,8},{10,11... | collective-permute-start | bytes 1572872 | tf_op jit(solution)/shard_map/ppermute | solution.py:313
  82.6 0.2 shard_map.96.own_ref
  82.9 0.0 collective-permute-done.14.got_ref
  82.9 0.8 shard_map.93
  83.7 0.4 collective-permute-done.15.got_ref
  84.2 0.8 shard_map.98
  (4 shorter events, 0.1 us)
Async XLA Ops:
  1.6 3.4 %copy-start = (bf16[128,1024]{1,0:T(8,128)(2,1)S(1)}, bf16[128,1024]{1,0:T(8,128)(2,1)}, u32[]{:S(2)}) copy-start(bf16[128,1024]{1,0:T(8,128)(2,1)} %q_ref.1) | copy-start | bytes 786436
  1.6 3.4 %copy-start.1 = (bf16[128,1024]{1,0:T(8,128)(2,1)S(1)}, bf16[128,1024]{1,0:T(8,128)(2,1)}, u32[]{:S(2)}) copy-start(bf16[128,1024]{1,0:T(8,128)(2,1)} %dy_ref.1) | copy-start | bytes 786436
  1.7 4.9 %copy-start.2 = (bf16[128,1024]{1,0:T(8,128)(2,1)S(1)}, bf16[128,1024]{1,0:T(8,128)(2,1)}, u32[]{:S(2)}) copy-start(bf16[128,1024]{1,0:T(8,128)(2,1)} %k_ref.1) | copy-start | bytes 786436
  1.7 4.9 %copy-start.3 = (bf16[128,1024]{1,0:T(8,128)(2,1)S(1)}, bf16[128,1024]{1,0:T(8,128)(2,1)}, u32[]{:S(2)}) copy-start(bf16[128,1024]{1,0:T(8,128)(2,1)} %v_ref.1) | copy-start | bytes 786436
  1.7 4.9 %collective-permute-start.1 = (f32[128,1024]{1,0:T(8,128)S(1)}, f32[128,1024]{1,0:T(8,128)S(1)}, u32[]{:S(2)}, u32[]{:S(2)}) collective-permute-start(f32[128,1024]{1,0:T(8,128)S(1)} %maximum_convert_fusion), channel_id=1, source_target_pairs={{0,1},{1,0},{2,3},{3,2},{4,5},{5,4},{6,7},{7,6},{8,9},{9,8},{10,11... | collective-permute-start | bytes 1572872 | tf_op jit(solution)/shard_map/ppermute | solution.py:313
  5.1 7.6 %collective-permute-start = (f32[128,1024]{1,0:T(8,128)S(1)}, f32[128,1024]{1,0:T(8,128)S(1)}, u32[]{:S(2)}, u32[]{:S(2)}) collective-permute-start(f32[128,1024]{1,0:T(8,128)S(1)} %get-tuple-element.47), channel_id=1, source_target_pairs={{0,1},{1,0},{2,3},{3,2},{4,5},{5,4},{6,7},{7,6},{8,9},{9,8},{10,11... | collective-permute-start | bytes 1572872 | tf_op jit(solution)/shard_map/ppermute | solution.py:313
  7.6 13.1 %all-to-all-start = ((f32[16,32,128]{2,1,0:T(8,128)}), f32[16,32,128]{2,1,0:T(8,128)S(1)}, u32[]{:S(2)}, u32[]{:S(2)}) async-start(f32[16,32,128]{2,1,0:T(8,128)} %get-tuple-element.61), calls=%async_computation | async-start | bytes 524288 | tf_op jit(solution)/shard_map/all_to_all | solution.py:367
  13.6 24.8 %collective-permute-start.2 = (f32[256,512]{1,0:T(8,128)}, f32[256,512]{1,0:T(8,128)S(1)}, u32[]{:S(2)}, u32[]{:S(2)}) collective-permute-start(f32[256,512]{1,0:T(8,128)} %get-tuple-element.53), channel_id=1, source_target_pairs={{0,2},{2,4},{4,6},{6,0},{8,10},{10,12},{12,14},{14,8},{16,18},{18,... | collective-permute-start | bytes 1572872 | tf_op jit(solution)/shard_map/ppermute | solution.py:332
  15.1 24.6 %collective-permute-start.3 = (f32[256,512]{1,0:T(8,128)S(1)}, f32[256,512]{1,0:T(8,128)S(1)}, u32[]{:S(2)}, u32[]{:S(2)}) collective-permute-start(f32[256,512]{1,0:T(8,128)S(1)} %get-tuple-element.54), channel_id=1, source_target_pairs={{0,4},{2,6},{4,0},{6,2},{8,12},{10,14},{12,8},{14,10},{16,20},{18,... | collective-permute-start | bytes 1572872 | tf_op jit(solution)/shard_map/ppermute | solution.py:332
  17.5 22.2 %collective-permute-start.4 = (f32[256,512]{1,0:T(8,128)S(1)}, f32[256,512]{1,0:T(8,128)}, u32[]{:S(2)}, u32[]{:S(2)}) collective-permute-start(f32[256,512]{1,0:T(8,128)S(1)} %get-tuple-element.55), channel_id=1, source_target_pairs={{0,6},{2,0},{4,2},{6,4},{8,14},{10,8},{12,10},{14,12},{16,22},{18,... | collective-permute-start | bytes 1572872 | tf_op jit(solution)/shard_map/ppermute | solution.py:332
  36.8 5.1 %collective-permute-start.5 = (f32[4,32,128]{2,1,0:T(8,128)S(1)}, f32[4,32,128]{2,1,0:T(8,128)S(1)}, u32[]{:S(2)}, u32[]{:S(2)}) collective-permute-start(f32[4,32,128]{2,1,0:T(8,128)S(1)} %get-tuple-element.66), channel_id=1, source_target_pairs={{0,8},{2,10},{4,12},{6,14},{8,16},{10,18},{12,20},{14,22},{16,24},... | collective-permute-start | bytes 196616 | tf_op jit(solution)/shard_map/ppermute | solution.py:341
  37.1 2.5 %copy-start.4 = (f32[1024]{0:T(1024)S(1)}, f32[1024]{0:T(1024)}, u32[]{:S(2)}) copy-start(f32[1024]{0:T(1024)} %param.8) | copy-start | bytes 12292
  37.1 4.7 %collective-permute-start.6 = (f32[4,32,128]{2,1,0:T(8,128)S(1)}, f32[4,32,128]{2,1,0:T(8,128)S(1)}, u32[]{:S(2)}, u32[]{:S(2)}) collective-permute-start(f32[4,32,128]{2,1,0:T(8,128)S(1)} %get-tuple-element.67), channel_id=1, source_target_pairs={{0,16},{2,18},{4,20},{6,22},{8,24},{10,26},{12,28},{14,30},{16,0},... | collective-permute-start | bytes 196616 | tf_op jit(solution)/shard_map/ppermute | solution.py:341
  38.4 4.1 %collective-permute-start.7 = (f32[4,32,128]{2,1,0:T(8,128)S(1)}, f32[4,32,128]{2,1,0:T(8,128)S(1)}, u32[]{:S(2)}, u32[]{:S(2)}) collective-permute-start(f32[4,32,128]{2,1,0:T(8,128)S(1)} %get-tuple-element.68), channel_id=1, source_target_pairs={{0,24},{2,26},{4,28},{6,30},{8,0},{10,2},{12,4},{14,6},{16,8},{18,... | collective-permute-start | bytes 196616 | tf_op jit(solution)/shard_map/ppermute | solution.py:341
  43.2 4.4 %collective-permute-start.8 = (f32[4,32,128]{2,1,0:T(8,128)S(1)}, f32[4,32,128]{2,1,0:T(8,128)S(1)}, u32[]{:S(2)}, u32[]{:S(2)}) collective-permute-start(f32[4,32,128]{2,1,0:T(8,128)S(1)} %get-tuple-element.70), channel_id=1, source_target_pairs={{0,8},{2,10},{4,12},{6,14},{8,16},{10,18},{12,20},{14,22},{16,24},... | collective-permute-start | bytes 196616 | tf_op jit(solution)/shard_map/ppermute | solution.py:341
  44.0 5.0 %collective-permute-start.9 = (f32[4,32,128]{2,1,0:T(8,128)S(1)}, f32[4,32,128]{2,1,0:T(8,128)S(1)}, u32[]{:S(2)}, u32[]{:S(2)}) collective-permute-start(f32[4,32,128]{2,1,0:T(8,128)S(1)} %get-tuple-element.71), channel_id=1, source_target_pairs={{0,16},{2,18},{4,20},{6,22},{8,24},{10,26},{12,28},{14,30},{16,0},... | collective-permute-start | bytes 196616 | tf_op jit(solution)/shard_map/ppermute | solution.py:341
  46.7 3.1 %collective-permute-start.10 = (f32[4,32,128]{2,1,0:T(8,128)S(1)}, f32[4,32,128]{2,1,0:T(8,128)S(1)}, u32[]{:S(2)}, u32[]{:S(2)}) collective-permute-start(f32[4,32,128]{2,1,0:T(8,128)S(1)} %get-tuple-element.72), channel_id=1, source_target_pairs={{0,24},{2,26},{4,28},{6,30},{8,0},{10,2},{12,4},{14,6},{16,8},{18,... | collective-permute-start | bytes 196616 | tf_op jit(solution)/shard_map/ppermute | solution.py:341
  50.5 11.2 %all-to-all-start.2 = ((f32[8,32,128]{2,1,0:T(8,128)}), f32[8,32,128]{2,1,0:T(8,128)S(1)}, u32[]{:S(2)}, u32[]{:S(2)}) async-start(f32[8,32,128]{2,1,0:T(8,128)} %get-tuple-element.83), calls=%async_computation.2 | async-start | bytes 262144 | tf_op jit(solution)/shard_map/all_to_all | solution.py:390
  53.9 12.3 %collective-permute-start.11 = (f32[128,128]{1,0:T(8,128)S(1)}, f32[128,128]{1,0:T(8,128)S(1)}, u32[]{:S(2)}, u32[]{:S(2)}) collective-permute-start(f32[128,128]{1,0:T(8,128)S(1)} %get-tuple-element.75), channel_id=1, source_target_pairs={{0,2},{2,4},{4,6},{6,0},{8,10},{10,12},{12,14},{14,8},{16,18},{18,... | collective-permute-start | bytes 196616 | tf_op jit(solution)/shard_map/ppermute | solution.py:332
  54.0 12.2 %collective-permute-start.12 = (f32[128,128]{1,0:T(8,128)S(1)}, f32[128,128]{1,0:T(8,128)S(1)}, u32[]{:S(2)}, u32[]{:S(2)}) collective-permute-start(f32[128,128]{1,0:T(8,128)S(1)} %get-tuple-element.76), channel_id=1, source_target_pairs={{0,4},{2,6},{4,0},{6,2},{8,12},{10,14},{12,8},{14,10},{16,20},{18,... | collective-permute-start | bytes 196616 | tf_op jit(solution)/shard_map/ppermute | solution.py:332
  55.8 10.4 %collective-permute-start.13 = (f32[128,128]{1,0:T(8,128)S(1)}, f32[128,128]{1,0:T(8,128)S(1)}, u32[]{:S(2)}, u32[]{:S(2)}) collective-permute-start(f32[128,128]{1,0:T(8,128)S(1)} %get-tuple-element.77), channel_id=1, source_target_pairs={{0,6},{2,0},{4,2},{6,4},{8,14},{10,8},{12,10},{14,12},{16,22},{18,... | collective-permute-start | bytes 196616 | tf_op jit(solution)/shard_map/ppermute | solution.py:332
  62.4 17.8 %all-to-all-start.3 = ((f32[16,32,128]{2,1,0:T(8,128)}), f32[16,32,128]{2,1,0:T(8,128)S(1)}, u32[]{:S(2)}, u32[]{:S(2)}) async-start(f32[16,32,128]{2,1,0:T(8,128)} %shard_map.94), calls=%async_computation.3 | async-start | bytes 524288 | tf_op jit(solution)/shard_map/all_to_all | solution.py:402
  70.9 11.9 %collective-permute-start.14 = (f32[128,1024]{1,0:T(8,128)}, f32[128,1024]{1,0:T(8,128)S(1)}, u32[]{:S(2)}, u32[]{:S(2)}) collective-permute-start(f32[128,1024]{1,0:T(8,128)} %get-tuple-element.79), channel_id=1, source_target_pairs={{0,1},{1,0},{2,3},{3,2},{4,5},{5,4},{6,7},{7,6},{8,9},{9,8},{10,11... | collective-permute-start | bytes 1572872 | tf_op jit(solution)/shard_map/ppermute | solution.py:313
  80.6 3.6 %collective-permute-start.15 = (f32[128,1024]{1,0:T(8,128)S(1)}, f32[128,1024]{1,0:T(8,128)S(1)}, u32[]{:S(2)}, u32[]{:S(2)}) collective-permute-start(f32[128,1024]{1,0:T(8,128)S(1)} %shard_map.97), channel_id=1, source_target_pairs={{0,1},{1,0},{2,3},{3,2},{4,5},{5,4},{6,7},{7,6},{8,9},{9,8},{10,11... | collective-permute-start | bytes 1572872 | tf_op jit(solution)/shard_map/ppermute | solution.py:313

commit v6 on v5

--- a/solution.py
+++ b/solution.py
@@ -243,7 +243,7 @@
 
 def query_body(
     q2_ref, k2_ref, v2_ref, dy2_ref, gain_ref, b0, b1, b2, b3,
-    send_ref, own_ref, delta_ref, before_ref, all_ref,
+    send_ref, own_ref, delta_ref, weights_ref, scores_ref, before_ref, all_ref,
 ):
     mine, _ = halves()
     own, far = rows()
@@ -262,27 +262,25 @@
             if b == 0:
                 before = before + dot(k, v, TN)
             weights = jnp.where(mask, dot(q, k, NT), 0.0).astype(BF16)
+            weights_ref[h, b] = weights
             out = dot(weights, v, NN) + dot(q, before_b, NN)
             normed, delta = deltas(out, dy2_ref[at, head(h)].astype(F32) * gain)
             delta_ref[at, head(h)] = delta
             all_ref[at, head(h)] = normed * gain
             scores = jnp.where(mask, dot(delta, v, NT), 0.0).astype(BF16)
+            scores_ref[h, b] = scores
             all_ref[at, query] = dot(scores, k, NN) + dot(delta, before_b, NT)
     own_ref[...] = all_ref[own, :].astype(BF16)
     send_ref[...] = all_ref[far, :].astype(BF16).astype(F32)
 
 
-def keys_body(q2_ref, k2_ref, v2_ref, delta_ref, gk_ref, gv_ref, second_ref):
-    mask = causal()
+def keys_body(q2_ref, delta_ref, weights_ref, scores_ref, gk_ref, gv_ref, second_ref):
     for h in range(HALF):
         for b in range(2):
             at = block(b)
-            q, k, v = q2_ref[at, head(h)], k2_ref[at, head(h)], v2_ref[at, head(h)]
-            delta = delta_ref[at, head(h)]
-            weights = jnp.where(mask, dot(q, k, NT), 0.0).astype(BF16)
-            scores = jnp.where(mask, dot(delta, v, NT), 0.0).astype(BF16)
-            gk_ref[at, head(h)] = dot(scores, q, TN)
-            gv_ref[at, head(h)] = dot(weights, delta, TN)
+            q, delta = q2_ref[at, head(h)], delta_ref[at, head(h)]
+            gk_ref[at, head(h)] = dot(scores_ref[h, b], q, TN)
+            gv_ref[at, head(h)] = dot(weights_ref[h, b], delta, TN)
         second_ref[h] = dot(q, delta, TN)
 
 
@@ -390,13 +388,13 @@
     totals = lax.all_to_all(total, "z", 0, 0, tiled=True)
     b_got = shift_line(b_sends)
     (later,) = call(later_body, [slices], cost=10**11)(pairs, totals)
-    send, own, delta = call(
+    send, own, delta, weights, scores = call(
         query_body,
-        [(own_shape, F32), (own_shape, BF16), (pair, BF16)],
+        [(own_shape, F32), (own_shape, BF16), (pair, BF16)] + [((HALF, 2, TOK, TOK), BF16)] * 2,
         [pltpu.VMEM(*states), pltpu.VMEM((PAIR, 2 * WIDE), F32)],
         cost=10**11,
     )(q2, k2, v2, dy2, gain, b_own, *b_got)
-    gk, gv, second = call(keys_body, [(pair, F32), (pair, F32), states])(q2, k2, v2, delta)
+    gk, gv, second = call(keys_body, [(pair, F32), (pair, F32), states])(q2, delta, weights, scores)
     merge = call(merge_body, [(own_shape, BF16), (own_shape, BF16)])
     attended, grad_query = merge(own, swap(send))
     after = lax.all_to_all(later, ("y", "x"), 0, 0, tiled=True)

time: 85.5 us -> 85.5 us (level)
  Pallas kernels: 15.1 us -> 13.8 us
  starting transfers between devices: 40.4 us -> 41.5 us
    pallas_call x2, Pallas kernels: 6.62 us -> 5.11 us  [the longest x1 4.74 us: per_device(): call(query_body, [(own_shape, F32), (own_shape, BF16), (pair, BF16)] + [(...]
    ppermute x4, starting transfers between devices: 13.8 us -> 14.9 us  [swap(): return lax.ppermute(x, 'core', [(0, 1), (1, 0)])]
  transfers between devices with their start and end apart: 19 -> 19, of which waited for: 9 -> 9; matrix products, arithmetic and copies ran while one was open for 0% -> 0% of each run, Pallas kernels for 15% -> 13%
where the time goes in v6:
time: 85.5 us; the launch traced here: 85 us
  starting transfers between devices  41.5 us (49%)
  blocking collectives  15.9 us (19%)
  Pallas kernels  13.8 us (16%)
  waiting for transfers between devices  11.9 us (14%)
  local copies, waits for them, and re-layouts  1.02 us (1%)
    all_to_all x1, blocking collectives, per_device(): earlier = lax.all_to_all(total, 'z', 0, 0, tiled=True)  15.9 us
    ppermute x4, starting transfers between devices, swap(): return lax.ppermute(x, 'core', [(0, 1), (1, 0)])  14.9 us
    ppermute x6, starting transfers between devices, shift_line(): lax.ppermute(a, AXES, [(device(z, c, i, j), device(z, c, i, (j + s) % SID...  7.76 us
    ppermute x6, starting transfers between devices, shift_cross(): lax.ppermute(a, AXES, [(device(z, c, i, j), device(z, c, (i + s) % SIDE,...  6.7 us
    all_to_all x1, waiting for transfers between devices, per_device(): totals = lax.all_to_all(total, 'z', 0, 0, tiled=True)  5.08 us
    all_to_all x1, starting transfers between devices, per_device(): parts = lax.all_to_all(pieces, ('y', 'x'), 0, 0, tiled=True)  5.02 us
    pallas_call x1, Pallas kernels, per_device(): call(query_body, [(own_shape, F32), (own_shape, BF16), (pair, BF16)] + [(...  4.74 us
    ppermute x6, waiting for transfers between devices, shift_cross(): lax.ppermute(a, AXES, [(device(z, c, i, j), device(z, c, (i + s) % SIDE,...  3.85 us
  transfers between devices with their start and end apart: 19, of which 9 were waited for; matrix products, arithmetic and copies ran while one was open for 0% of the time, Pallas kernels for 13%

profile of v6, /device:TPU:1, one launch (start us, length us, event | category | flops | bytes accessed | tf_op | source)
XLA Modules:
  0.0 85.0 jit_solution(17152539266392275003)
XLA Ops:
  0.6 1.0 %constant_dynamic-slice_fusion = (bf16[128,512]{1,0:T(8,128)(2,1)S(1)}, bf16[128,512]{1,0:T(8,128)(2,1)S(1)}) fusion(bf16[128,1024]{1,0:T(8,128)(2,1)} %v_ref.1, s32[]{:T(128)S(6)} %select_n.4, bf16[128,1024]{1,0:T(8,128)(2,1)} %k_ref.1), kind=kLoop, calls=%fused_computation.1 | loop fusion | bytes 524292 | tf_op jit(solution)/shard_map/dynamic_slice | solution.py:357
  1.6 0.0 copy-start
  1.6 0.0 copy-start.1
  1.7 0.0 copy-start.2
  1.7 0.0 copy-start.3
  1.7 3.3 %collective-permute-start.1 = (f32[128,1024]{1,0:T(8,128)S(1)}, f32[128,1024]{1,0:T(8,128)S(1)}, u32[]{:S(2)}, u32[]{:S(2)}) collective-permute-start(f32[128,1024]{1,0:T(8,128)S(1)} %maximum_convert_fusion), channel_id=1, source_target_pairs={{0,1},{1,0},{2,3},{3,2},{4,5},{5,4},{6,7},{7,6},{8,9},{9,8},{10,11... | collective-permute-start | bytes 1572872 | tf_op jit(solution)/shard_map/ppermute | solution.py:311
  5.1 0.0 copy-done
  5.1 0.0 copy-done.1
  5.1 0.9 %collective-permute-start = (f32[128,1024]{1,0:T(8,128)S(1)}, f32[128,1024]{1,0:T(8,128)S(1)}, u32[]{:S(2)}, u32[]{:S(2)}) collective-permute-start(f32[128,1024]{1,0:T(8,128)S(1)} %get-tuple-element.49), channel_id=1, source_target_pairs={{0,1},{1,0},{2,3},{3,2},{4,5},{5,4},{6,7},{7,6},{8,9},{9,8},{10,11... | collective-permute-start | bytes 1572872 | tf_op jit(solution)/shard_map/ppermute | solution.py:311
  6.0 0.6 collective-permute-done.1.got_ref
  6.6 0.0 copy-done.2
  6.6 0.0 copy-done.3
  6.6 1.0 %shard_map.85 = (bf16[256,512]{1,0:T(8,128)(2,1)S(1)}, bf16[256,512]{1,0:T(8,128)(2,1)S(1)}, f32[16,32,128]{2,1,0:T(8,128)}) custom-call(bf16[128,1024]{1,0:T(8,128)(2,1)S(1)} %copy-done.2, bf16[128,1024]{1,0:T(8,128)(2,1)S(1)} %copy-done.3, f32[128,1024]{1,0:T(8,128)S(1)} %collective-permute-done.1.got_ref, f32[8,128]{1,0:T(8,128)S(1)} %get-tuple-element.50._), custom_call_target="tpu_custom_call" | custom-call | tf_op jit(solution)/shard_map/pallas_call | solution.py:362
  7.6 5.0 %all-to-all-start = ((f32[16,32,128]{2,1,0:T(8,128)}), f32[16,32,128]{2,1,0:T(8,128)S(1)}, u32[]{:S(2)}, u32[]{:S(2)}) async-start(f32[16,32,128]{2,1,0:T(8,128)} %get-tuple-element.63), calls=%async_computation | async-start | bytes 524288 | tf_op jit(solution)/shard_map/all_to_all | solution.py:365
  12.7 0.0 collective-permute-done.got_ref
  12.7 1.1 %shard_map.86 = (bf16[256,512]{1,0:T(8,128)(2,1)S(1)}, bf16[256,512]{1,0:T(8,128)(2,1)S(1)}, f32[8,128]{1,0:T(8,128)S(1)}, f32[256,512]{1,0:T(8,128)}, f32[256,512]{1,0:T(8,128)}, /*index=5*/f32[256,512]{1,0:T(8,128)S(1)}) custom-call(bf16[128,1024]{1,0:T(8,128)(2,1)S(1)} %copy-done, bf16[128,1024]{1,0:T(8,128)(2,1)S(1)} %copy-done.1, ...), custom_call_target="tpu_custom_call" | custom-call | tf_op jit(solution)/shard_map/pallas_call | solution.py:366
  13.8 1.4 %collective-permute-start.2 = (f32[256,512]{1,0:T(8,128)}, f32[256,512]{1,0:T(8,128)S(1)}, u32[]{:S(2)}, u32[]{:S(2)}) collective-permute-start(f32[256,512]{1,0:T(8,128)} %get-tuple-element.55), channel_id=1, source_target_pairs={{0,2},{2,4},{4,6},{6,0},{8,10},{10,12},{12,14},{14,8},{16,18},{18,... | collective-permute-start | bytes 1572872 | tf_op jit(solution)/shard_map/ppermute | solution.py:330
  15.2 2.4 %collective-permute-start.3 = (f32[256,512]{1,0:T(8,128)}, f32[256,512]{1,0:T(8,128)S(1)}, u32[]{:S(2)}, u32[]{:S(2)}) collective-permute-start(f32[256,512]{1,0:T(8,128)} %get-tuple-element.56), channel_id=1, source_target_pairs={{0,4},{2,6},{4,0},{6,2},{8,12},{10,14},{12,8},{14,10},{16,20},{18,... | collective-permute-start | bytes 1572872 | tf_op jit(solution)/shard_map/ppermute | solution.py:330
  17.6 1.2 %collective-permute-start.4 = (f32[256,512]{1,0:T(8,128)S(1)}, f32[256,512]{1,0:T(8,128)}, u32[]{:S(2)}, u32[]{:S(2)}) collective-permute-start(f32[256,512]{1,0:T(8,128)S(1)} %get-tuple-element.57), channel_id=1, source_target_pairs={{0,6},{2,0},{4,2},{6,4},{8,14},{10,8},{12,10},{14,12},{16,22},{18,... | collective-permute-start | bytes 1572872 | tf_op jit(solution)/shard_map/ppermute | solution.py:330
  18.8 1.9 %all-to-all-done.parts_ref = f32[16,32,128]{2,1,0:T(8,128)S(1)} async-done(((f32[16,32,128]{2,1,0:T(8,128)}), f32[16,32,128]{2,1,0:T(8,128)S(1)}, u32[]{:S(2)}, u32[]{:S(2)}) %all-to-all-start) | async-done | bytes 262176 | tf_op jit(solution)/shard_map/all_to_all | solution.py:365
  20.8 15.9 %all_to_all.20.got_ref = f32[8,32,128]{2,1,0:T(8,128)S(1)} all-to-all(f32[8,32,128]{2,1,0:T(8,128)S(1)} %get-tuple-element.66), channel_id=1, replica_groups=mesh['z'=8,'y'=4,'x'=4,'core'=2] {'z'}, dimensions={0} | all-to-all | bytes 262144 | tf_op jit(solution)/shard_map/all_to_all | solution.py:380
  36.8 0.4 collective-permute-start.5
  37.1 0.0 copy-start.4
  37.1 1.5 %collective-permute-start.6 = (f32[4,32,128]{2,1,0:T(8,128)S(1)}, f32[4,32,128]{2,1,0:T(8,128)S(1)}, u32[]{:S(2)}, u32[]{:S(2)}) collective-permute-start(f32[4,32,128]{2,1,0:T(8,128)S(1)} %get-tuple-element.69), channel_id=1, source_target_pairs={{0,16},{2,18},{4,20},{6,22},{8,24},{10,26},{12,28},{14,30},{16,0},... | collective-permute-start | bytes 196616 | tf_op jit(solution)/shard_map/ppermute | solution.py:339
  38.6 0.0 collective-permute-done.2.got1_ref
  38.6 1.1 %collective-permute-start.7 = (f32[4,32,128]{2,1,0:T(8,128)S(1)}, f32[4,32,128]{2,1,0:T(8,128)S(1)}, u32[]{:S(2)}, u32[]{:S(2)}) collective-permute-start(f32[4,32,128]{2,1,0:T(8,128)S(1)} %get-tuple-element.70), channel_id=1, source_target_pairs={{0,24},{2,26},{4,28},{6,30},{8,0},{10,2},{12,4},{14,6},{16,8},{18,... | collective-permute-start | bytes 196616 | tf_op jit(solution)/shard_map/ppermute | solution.py:339
  39.7 0.0 collective-permute-done.3.got2_ref
  39.7 0.0 collective-permute-done.4.got3_ref
  39.7 0.0 copy-done.4
  39.7 2.0 %shard_map.87 = (bf16[1024,128]{1,0:T(8,128)(2,1)S(1)}, bf16[1024,128]{1,0:T(8,128)(2,1)S(1)}, f32[8,128]{1,0:T(8,128)S(1)}, f32[1024,128]{1,0:T(8,128)S(1)}, f32[4,128,128]{2,1,0:T(8,128)S(1)}) custom-call(bf16[256,512]{1,0:T(8,128)(2,1)S(1)} %get-tuple-element.51.k2_ref, bf16[256,512]{1,0:T(8,128)(2,1)S(1)} %get-tuple-element.52.v2_ref, ...), custom_call_target="tpu_custom_call" | custom-call | flops 99999997952 | tf_op jit(solution)/shard_map/pallas_call | solution.py:373
  41.7 0.2 collective-permute-done.5.w1
  41.9 0.0 collective-permute-done.6.w2
  41.9 0.6 collective-permute-done.7.w3
  42.4 0.7 shard_map.90
  43.2 0.8 collective-permute-start.8
  44.0 3.0 %collective-permute-start.9 = (f32[4,32,128]{2,1,0:T(8,128)S(1)}, f32[4,32,128]{2,1,0:T(8,128)S(1)}, u32[]{:S(2)}, u32[]{:S(2)}) collective-permute-start(f32[4,32,128]{2,1,0:T(8,128)S(1)} %get-tuple-element.73), channel_id=1, source_target_pairs={{0,16},{2,18},{4,20},{6,22},{8,24},{10,26},{12,28},{14,30},{16,0},... | collective-permute-start | bytes 196616 | tf_op jit(solution)/shard_map/ppermute | solution.py:339
  47.0 0.0 collective-permute-start.10
  47.0 0.6 collective-permute-done.8.p1
  47.6 1.8 %collective-permute-done.9.p2 = f32[4,32,128]{2,1,0:T(8,128)S(1)} collective-permute-done((f32[4,32,128]{2,1,0:T(8,128)S(1)}, f32[4,32,128]{2,1,0:T(8,128)S(1)}, u32[]{:S(2)}, u32[]{:S(2)}) %collective-permute-start.9) | collective-permute-done | bytes 65568 | tf_op jit(solution)/shard_map/ppermute | solution.py:339
  49.3 0.8 collective-permute-done.10.p3
  50.1 0.7 shard_map.91
  50.8 3.4 %all-to-all-start.2 = ((f32[8,32,128]{2,1,0:T(8,128)}), f32[8,32,128]{2,1,0:T(8,128)S(1)}, u32[]{:S(2)}, u32[]{:S(2)}) async-start(f32[8,32,128]{2,1,0:T(8,128)} %get-tuple-element.85), calls=%async_computation.2 | async-start | bytes 262144 | tf_op jit(solution)/shard_map/all_to_all | solution.py:388
  54.2 0.1 collective-permute-start.11
  54.3 1.5 %collective-permute-start.12 = (f32[128,128]{1,0:T(8,128)S(1)}, f32[128,128]{1,0:T(8,128)S(1)}, u32[]{:S(2)}, u32[]{:S(2)}) collective-permute-start(f32[128,128]{1,0:T(8,128)S(1)} %get-tuple-element.78), channel_id=1, source_target_pairs={{0,4},{2,6},{4,0},{6,2},{8,12},{10,14},{12,8},{14,10},{16,20},{18,... | collective-permute-start | bytes 196616 | tf_op jit(solution)/shard_map/ppermute | solution.py:330
  55.8 1.2 %collective-permute-start.13 = (f32[128,128]{1,0:T(8,128)S(1)}, f32[128,128]{1,0:T(8,128)S(1)}, u32[]{:S(2)}, u32[]{:S(2)}) collective-permute-start(f32[128,128]{1,0:T(8,128)S(1)} %get-tuple-element.79), channel_id=1, source_target_pairs={{0,6},{2,0},{4,2},{6,4},{8,14},{10,8},{12,10},{14,12},{16,22},{18,... | collective-permute-start | bytes 196616 | tf_op jit(solution)/shard_map/ppermute | solution.py:330
  57.0 5.1 %all-to-all-done.2.got_ref = f32[8,32,128]{2,1,0:T(8,128)S(1)} async-done(((f32[8,32,128]{2,1,0:T(8,128)}), f32[8,32,128]{2,1,0:T(8,128)S(1)}, u32[]{:S(2)}, u32[]{:S(2)}) %all-to-all-start.2) | async-done | bytes 131104 | tf_op jit(solution)/shard_map/all_to_all | solution.py:388
  62.0 0.7 shard_map.94
  62.8 3.7 %all-to-all-start.3 = ((f32[16,32,128]{2,1,0:T(8,128)}), f32[16,32,128]{2,1,0:T(8,128)S(1)}, u32[]{:S(2)}, u32[]{:S(2)}) async-start(f32[16,32,128]{2,1,0:T(8,128)} %shard_map.94), calls=%async_computation.3 | async-start | bytes 524288 | tf_op jit(solution)/shard_map/all_to_all | solution.py:400
  66.5 0.0 collective-permute-done.11.b1
  66.5 0.0 collective-permute-done.12.b2
  66.5 0.0 collective-permute-done.13.b3
  66.5 4.7 %shard_map.92 = (f32[128,1024]{1,0:T(8,128)}, bf16[128,1024]{1,0:T(8,128)(2,1)S(1)}, bf16[256,512]{1,0:T(8,128)(2,1)S(1)}, bf16[4,2,128,128]{3,2,1,0:T(8,128)(2,1)S(1)}, bf16[4,2,128,128]{3,2,1,0:T(8,128)(2,1)S(1)}) custom-call(bf16[256,512]{1,0:T(8,128)(2,1)S(1)} %get-tuple-element.53.q2_ref, bf16[256,512]{1,0:T(8,128)(2,1)S(1)} %get-tuple-element.51.k2_ref, ...), custom_call_target="tpu_custom_call" | custom-call | flops 99999997952 | tf_op jit(solution)/shard_map/pallas_call | solution.py:391
  71.3 7.1 %collective-permute-start.14 = (f32[128,1024]{1,0:T(8,128)}, f32[128,1024]{1,0:T(8,128)S(1)}, u32[]{:S(2)}, u32[]{:S(2)}) collective-permute-start(f32[128,1024]{1,0:T(8,128)} %get-tuple-element.81), channel_id=1, source_target_pairs={{0,1},{1,0},{2,3},{3,2},{4,5},{5,4},{6,7},{7,6},{8,9},{9,8},{10,11... | collective-permute-start | bytes 1572872 | tf_op jit(solution)/shard_map/ppermute | solution.py:311
  78.4 0.4 shard_map.95
  78.8 0.0 all-to-all-done.3.later_ref
  78.8 0.3 shard_map.97
  79.0 3.6 %collective-permute-start.15 = (f32[128,1024]{1,0:T(8,128)S(1)}, f32[128,1024]{1,0:T(8,128)S(1)}, u32[]{:S(2)}, u32[]{:S(2)}) collective-permute-start(f32[128,1024]{1,0:T(8,128)S(1)} %shard_map.97), channel_id=1, source_target_pairs={{0,1},{1,0},{2,3},{3,2},{4,5},{5,4},{6,7},{7,6},{8,9},{9,8},{10,11... | collective-permute-start | bytes 1572872 | tf_op jit(solution)/shard_map/ppermute | solution.py:311
  82.6 0.2 shard_map.96.own_ref
  82.9 0.0 collective-permute-done.14.got_ref
  82.9 0.8 shard_map.93
  83.7 0.4 collective-permute-done.15.got_ref
  84.2 0.8 shard_map.98
  (4 shorter events, 0.1 us)
Async XLA Ops:
  1.6 3.4 %copy-start = (bf16[128,1024]{1,0:T(8,128)(2,1)S(1)}, bf16[128,1024]{1,0:T(8,128)(2,1)}, u32[]{:S(2)}) copy-start(bf16[128,1024]{1,0:T(8,128)(2,1)} %q_ref.1) | copy-start | bytes 786436
  1.6 3.4 %copy-start.1 = (bf16[128,1024]{1,0:T(8,128)(2,1)S(1)}, bf16[128,1024]{1,0:T(8,128)(2,1)}, u32[]{:S(2)}) copy-start(bf16[128,1024]{1,0:T(8,128)(2,1)} %dy_ref.1) | copy-start | bytes 786436
  1.7 4.9 %copy-start.2 = (bf16[128,1024]{1,0:T(8,128)(2,1)S(1)}, bf16[128,1024]{1,0:T(8,128)(2,1)}, u32[]{:S(2)}) copy-start(bf16[128,1024]{1,0:T(8,128)(2,1)} %k_ref.1) | copy-start | bytes 786436
  1.7 4.9 %copy-start.3 = (bf16[128,1024]{1,0:T(8,128)(2,1)S(1)}, bf16[128,1024]{1,0:T(8,128)(2,1)}, u32[]{:S(2)}) copy-start(bf16[128,1024]{1,0:T(8,128)(2,1)} %v_ref.1) | copy-start | bytes 786436
  1.7 4.9 %collective-permute-start.1 = (f32[128,1024]{1,0:T(8,128)S(1)}, f32[128,1024]{1,0:T(8,128)S(1)}, u32[]{:S(2)}, u32[]{:S(2)}) collective-permute-start(f32[128,1024]{1,0:T(8,128)S(1)} %maximum_convert_fusion), channel_id=1, source_target_pairs={{0,1},{1,0},{2,3},{3,2},{4,5},{5,4},{6,7},{7,6},{8,9},{9,8},{10,11... | collective-permute-start | bytes 1572872 | tf_op jit(solution)/shard_map/ppermute | solution.py:311
  5.1 7.5 %collective-permute-start = (f32[128,1024]{1,0:T(8,128)S(1)}, f32[128,1024]{1,0:T(8,128)S(1)}, u32[]{:S(2)}, u32[]{:S(2)}) collective-permute-start(f32[128,1024]{1,0:T(8,128)S(1)} %get-tuple-element.49), channel_id=1, source_target_pairs={{0,1},{1,0},{2,3},{3,2},{4,5},{5,4},{6,7},{7,6},{8,9},{9,8},{10,11... | collective-permute-start | bytes 1572872 | tf_op jit(solution)/shard_map/ppermute | solution.py:311
  7.6 13.1 %all-to-all-start = ((f32[16,32,128]{2,1,0:T(8,128)}), f32[16,32,128]{2,1,0:T(8,128)S(1)}, u32[]{:S(2)}, u32[]{:S(2)}) async-start(f32[16,32,128]{2,1,0:T(8,128)} %get-tuple-element.63), calls=%async_computation | async-start | bytes 524288 | tf_op jit(solution)/shard_map/all_to_all | solution.py:365
  13.8 24.8 %collective-permute-start.2 = (f32[256,512]{1,0:T(8,128)}, f32[256,512]{1,0:T(8,128)S(1)}, u32[]{:S(2)}, u32[]{:S(2)}) collective-permute-start(f32[256,512]{1,0:T(8,128)} %get-tuple-element.55), channel_id=1, source_target_pairs={{0,2},{2,4},{4,6},{6,0},{8,10},{10,12},{12,14},{14,8},{16,18},{18,... | collective-permute-start | bytes 1572872 | tf_op jit(solution)/shard_map/ppermute | solution.py:330
  15.2 24.4 %collective-permute-start.3 = (f32[256,512]{1,0:T(8,128)}, f32[256,512]{1,0:T(8,128)S(1)}, u32[]{:S(2)}, u32[]{:S(2)}) collective-permute-start(f32[256,512]{1,0:T(8,128)} %get-tuple-element.56), channel_id=1, source_target_pairs={{0,4},{2,6},{4,0},{6,2},{8,12},{10,14},{12,8},{14,10},{16,20},{18,... | collective-permute-start | bytes 1572872 | tf_op jit(solution)/shard_map/ppermute | solution.py:330
  17.6 22.0 %collective-permute-start.4 = (f32[256,512]{1,0:T(8,128)S(1)}, f32[256,512]{1,0:T(8,128)}, u32[]{:S(2)}, u32[]{:S(2)}) collective-permute-start(f32[256,512]{1,0:T(8,128)S(1)} %get-tuple-element.57), channel_id=1, source_target_pairs={{0,6},{2,0},{4,2},{6,4},{8,14},{10,8},{12,10},{14,12},{16,22},{18,... | collective-permute-start | bytes 1572872 | tf_op jit(solution)/shard_map/ppermute | solution.py:330
  36.8 5.1 %collective-permute-start.5 = (f32[4,32,128]{2,1,0:T(8,128)S(1)}, f32[4,32,128]{2,1,0:T(8,128)S(1)}, u32[]{:S(2)}, u32[]{:S(2)}) collective-permute-start(f32[4,32,128]{2,1,0:T(8,128)S(1)} %get-tuple-element.68), channel_id=1, source_target_pairs={{0,8},{2,10},{4,12},{6,14},{8,16},{10,18},{12,20},{14,22},{16,24},... | collective-permute-start | bytes 196616 | tf_op jit(solution)/shard_map/ppermute | solution.py:339
  37.1 2.6 %copy-start.4 = (f32[1024]{0:T(1024)S(1)}, f32[1024]{0:T(1024)}, u32[]{:S(2)}) copy-start(f32[1024]{0:T(1024)} %param.8) | copy-start | bytes 12292
  37.1 4.7 %collective-permute-start.6 = (f32[4,32,128]{2,1,0:T(8,128)S(1)}, f32[4,32,128]{2,1,0:T(8,128)S(1)}, u32[]{:S(2)}, u32[]{:S(2)}) collective-permute-start(f32[4,32,128]{2,1,0:T(8,128)S(1)} %get-tuple-element.69), channel_id=1, source_target_pairs={{0,16},{2,18},{4,20},{6,22},{8,24},{10,26},{12,28},{14,30},{16,0},... | collective-permute-start | bytes 196616 | tf_op jit(solution)/shard_map/ppermute | solution.py:339
  38.6 3.9 %collective-permute-start.7 = (f32[4,32,128]{2,1,0:T(8,128)S(1)}, f32[4,32,128]{2,1,0:T(8,128)S(1)}, u32[]{:S(2)}, u32[]{:S(2)}) collective-permute-start(f32[4,32,128]{2,1,0:T(8,128)S(1)} %get-tuple-element.70), channel_id=1, source_target_pairs={{0,24},{2,26},{4,28},{6,30},{8,0},{10,2},{12,4},{14,6},{16,8},{18,... | collective-permute-start | bytes 196616 | tf_op jit(solution)/shard_map/ppermute | solution.py:339
  43.2 4.4 %collective-permute-start.8 = (f32[4,32,128]{2,1,0:T(8,128)S(1)}, f32[4,32,128]{2,1,0:T(8,128)S(1)}, u32[]{:S(2)}, u32[]{:S(2)}) collective-permute-start(f32[4,32,128]{2,1,0:T(8,128)S(1)} %get-tuple-element.72), channel_id=1, source_target_pairs={{0,8},{2,10},{4,12},{6,14},{8,16},{10,18},{12,20},{14,22},{16,24},... | collective-permute-start | bytes 196616 | tf_op jit(solution)/shard_map/ppermute | solution.py:339
  44.0 5.3 %collective-permute-start.9 = (f32[4,32,128]{2,1,0:T(8,128)S(1)}, f32[4,32,128]{2,1,0:T(8,128)S(1)}, u32[]{:S(2)}, u32[]{:S(2)}) collective-permute-start(f32[4,32,128]{2,1,0:T(8,128)S(1)} %get-tuple-element.73), channel_id=1, source_target_pairs={{0,16},{2,18},{4,20},{6,22},{8,24},{10,26},{12,28},{14,30},{16,0},... | collective-permute-start | bytes 196616 | tf_op jit(solution)/shard_map/ppermute | solution.py:339
  47.0 3.1 %collective-permute-start.10 = (f32[4,32,128]{2,1,0:T(8,128)S(1)}, f32[4,32,128]{2,1,0:T(8,128)S(1)}, u32[]{:S(2)}, u32[]{:S(2)}) collective-permute-start(f32[4,32,128]{2,1,0:T(8,128)S(1)} %get-tuple-element.74), channel_id=1, source_target_pairs={{0,24},{2,26},{4,28},{6,30},{8,0},{10,2},{12,4},{14,6},{16,8},{18,... | collective-permute-start | bytes 196616 | tf_op jit(solution)/shard_map/ppermute | solution.py:339
  50.8 11.2 %all-to-all-start.2 = ((f32[8,32,128]{2,1,0:T(8,128)}), f32[8,32,128]{2,1,0:T(8,128)S(1)}, u32[]{:S(2)}, u32[]{:S(2)}) async-start(f32[8,32,128]{2,1,0:T(8,128)} %get-tuple-element.85), calls=%async_computation.2 | async-start | bytes 262144 | tf_op jit(solution)/shard_map/all_to_all | solution.py:388
  54.2 12.3 %collective-permute-start.11 = (f32[128,128]{1,0:T(8,128)S(1)}, f32[128,128]{1,0:T(8,128)S(1)}, u32[]{:S(2)}, u32[]{:S(2)}) collective-permute-start(f32[128,128]{1,0:T(8,128)S(1)} %get-tuple-element.77), channel_id=1, source_target_pairs={{0,2},{2,4},{4,6},{6,0},{8,10},{10,12},{12,14},{14,8},{16,18},{18,... | collective-permute-start | bytes 196616 | tf_op jit(solution)/shard_map/ppermute | solution.py:330
  54.3 12.2 %collective-permute-start.12 = (f32[128,128]{1,0:T(8,128)S(1)}, f32[128,128]{1,0:T(8,128)S(1)}, u32[]{:S(2)}, u32[]{:S(2)}) collective-permute-start(f32[128,128]{1,0:T(8,128)S(1)} %get-tuple-element.78), channel_id=1, source_target_pairs={{0,4},{2,6},{4,0},{6,2},{8,12},{10,14},{12,8},{14,10},{16,20},{18,... | collective-permute-start | bytes 196616 | tf_op jit(solution)/shard_map/ppermute | solution.py:330
  55.8 10.7 %collective-permute-start.13 = (f32[128,128]{1,0:T(8,128)S(1)}, f32[128,128]{1,0:T(8,128)S(1)}, u32[]{:S(2)}, u32[]{:S(2)}) collective-permute-start(f32[128,128]{1,0:T(8,128)S(1)} %get-tuple-element.79), channel_id=1, source_target_pairs={{0,6},{2,0},{4,2},{6,4},{8,14},{10,8},{12,10},{14,12},{16,22},{18,... | collective-permute-start | bytes 196616 | tf_op jit(solution)/shard_map/ppermute | solution.py:330
  62.8 16.0 %all-to-all-start.3 = ((f32[16,32,128]{2,1,0:T(8,128)}), f32[16,32,128]{2,1,0:T(8,128)S(1)}, u32[]{:S(2)}, u32[]{:S(2)}) async-start(f32[16,32,128]{2,1,0:T(8,128)} %shard_map.94), calls=%async_computation.3 | async-start | bytes 524288 | tf_op jit(solution)/shard_map/all_to_all | solution.py:400
  71.3 11.6 %collective-permute-start.14 = (f32[128,1024]{1,0:T(8,128)}, f32[128,1024]{1,0:T(8,128)S(1)}, u32[]{:S(2)}, u32[]{:S(2)}) collective-permute-start(f32[128,1024]{1,0:T(8,128)} %get-tuple-element.81), channel_id=1, source_target_pairs={{0,1},{1,0},{2,3},{3,2},{4,5},{5,4},{6,7},{7,6},{8,9},{9,8},{10,11... | collective-permute-start | bytes 1572872 | tf_op jit(solution)/shard_map/ppermute | solution.py:311
  79.0 5.1 %collective-permute-start.15 = (f32[128,1024]{1,0:T(8,128)S(1)}, f32[128,1024]{1,0:T(8,128)S(1)}, u32[]{:S(2)}, u32[]{:S(2)}) collective-permute-start(f32[128,1024]{1,0:T(8,128)S(1)} %shard_map.97), channel_id=1, source_target_pairs={{0,1},{1,0},{2,3},{3,2},{4,5},{5,4},{6,7},{7,6},{8,9},{9,8},{10,11... | collective-permute-start | bytes 1572872 | tf_op jit(solution)/shard_map/ppermute | solution.py:311
